TPU v7x, 256 devices: a whole 4x4x8 slice. The times are simulated.
256 devices in a mesh: replica: 16 (over z, core), tensor: 16 (over x, y).
Axes of the slice: x: 4, y: 4, z: 8, core: 2. Of those that a mesh axis runs over, the one named last changes fastest.
Arguments:
- hidden_in: bfloat16 [8192, 5120], P('replica'), may hold values from -6 to 6
- norm_gain: float32 [5120], replicated, may hold values from 0.1 to 1.9
- w_query: bfloat16 [5120, 4096], P(None, 'tensor'), may hold values from -0.078125 to 0.078125
- w_keyval: bfloat16 [5120, 4096], P(None, 'tensor'), as said below
- query_gain: float32 [128], replicated, may hold values from 0.1 to 1.9
- key_gain: float32 [128], replicated, may hold values from 0.1 to 1.9
- w_output: bfloat16 [4096, 5120], P('tensor'), may hold values from -0.09375 to 0.09375
- kv_pool: bfloat16 [128, 128, 4096], P('replica', None, 'tensor'), as said below
- prefix_len: int32 [16], replicated, may hold values from 3072 to 6144, as said below
- hit_holder: int32 [16, 48], replicated, may hold values from 0 to 15, as said below
- hit_slot: int32 [16, 48], replicated, may hold values from 0 to 7
- dest_holder: int32 [16, 4], replicated, may hold values from 0 to 15, as said below
- dest_slot: int32 [16, 4], replicated, may hold values from 0 to 7
Outputs:
- attended: bfloat16 [8192, 5120], P('replica', 'tensor')
- pool_after: bfloat16 [128, 128, 4096], P('replica', None, 'tensor')
Inputs may be any that keep to these rules, and one draw needn't show every extreme that they name: `prefix_len`: one request has exactly 6144 cached tokens, every request at least half of that. `hit_holder`: among the first ceil(prefix_len / 128) entries of a row, no holder appears more than 3 times; the longest request reaches 3 on every holder. The pairs (dest_holder, dest_slot) are all different. `w_keyval`: copies 2 h and 2 h + 1 of every key-value head are equal. `kv_pool`: copies 2 h and 2 h + 1 of every key-value head are equal.
All inputs are finite; a program needn't handle non-finite values.
Results may differ from a plain program's by a relative error of at most 0.02.
The roundings to bfloat16 on the way count: a program that leaves them out, or rounds other values in their place, can miss the bound.
Values may be sent and summed in bfloat16 or wider, within the bound.
No kernel may reach another device: no remote copies, remote signals or barrier semaphores. Data moves between devices by JAX's collectives and lax.ppermute only.
A program may use at most 256 MiB of HBM per device.

v0:
```python
import jax
import jax.numpy as jnp
from jax import lax
from jax.sharding import PartitionSpec as P

EPS = 1e-06
THETA = 1000000.0


def rms_scale(values, gain):
    mean_sq = jnp.mean(values * values, axis=-1, keepdims=True)
    return values * lax.rsqrt(mean_sq + EPS) * gain


def rotate(values, position):
    half = values.shape[-1] // 2
    freqs = THETA ** (-2.0 * jnp.arange(half, dtype=jnp.float32) / values.shape[-1])
    angle = position[..., None] * freqs
    cosine = jnp.cos(angle)
    sine = jnp.sin(angle)
    first = values[..., :half]
    second = values[..., half:]
    return jnp.concatenate(
        [first * cosine - second * sine, second * cosine + first * sine], axis=-1
    )


def arrange(incoming, own_holders, capacity):
    entries = own_holders.shape[0]
    same = own_holders[None, :] == own_holders[:, None]
    earlier = jnp.arange(entries)[None, :] < jnp.arange(entries)[:, None]
    rank = jnp.sum(same & earlier, axis=1)
    index = own_holders * capacity + jnp.minimum(rank, capacity - 1)
    flat = incoming.reshape((-1,) + incoming.shape[2:])
    return flat[index]


def local(
    hidden_in,
    norm_gain,
    w_query,
    w_keyval,
    query_gain,
    key_gain,
    w_output,
    kv_pool,
    prefix_len,
    hit_holder,
    hit_slot,
    dest_holder,
    dest_slot,
):
    requests = lax.axis_size("replica")
    own_req = lax.axis_index("replica")
    span = hidden_in.shape[0]
    pool_rows, block, pair_width = kv_pool.shape
    head_dim = pair_width // 2
    per_req = hit_holder.shape[1]
    capacity = per_req // requests
    new_blocks = span // block
    cached_len = per_req * block
    normed = rms_scale(hidden_in.astype(jnp.float32), norm_gain).astype(jnp.bfloat16)
    query = jnp.dot(normed, w_query, preferred_element_type=jnp.float32).reshape(span, -1, head_dim)
    length = prefix_len[own_req]
    position = (length + jnp.arange(span, dtype=jnp.int32)).astype(jnp.float32)
    query = rotate(rms_scale(query, query_gain), position[:, None]).astype(jnp.bfloat16)
    projected = jnp.dot(normed, w_keyval, preferred_element_type=jnp.float32)
    new_keys = rotate(rms_scale(projected[:, :head_dim], key_gain), position).astype(jnp.bfloat16)
    new_vals = projected[:, head_dim:].astype(jnp.bfloat16)
    own_new = jnp.concatenate([new_keys, new_vals], axis=1)
    gathered = lax.all_gather(
        own_new.reshape(new_blocks, block, pair_width), "replica", axis=0, tiled=True
    )
    flat_holder = dest_holder.reshape(-1)
    flat_slot = dest_slot.reshape(-1)
    match = (flat_holder[None, :] == own_req) & (
        flat_slot[None, :] == jnp.arange(pool_rows)[:, None]
    )
    placed = jnp.dot(
        match.astype(jnp.bfloat16),
        gathered.reshape(-1, block * pair_width),
        preferred_element_type=jnp.float32,
    )
    placed = placed.astype(jnp.bfloat16).reshape(pool_rows, block, pair_width)
    pool_after = jnp.where(jnp.any(match, axis=1)[:, None, None], placed, kv_pool)
    counts = (prefix_len + block - 1) // block
    live = jnp.arange(per_req)[None, :] < counts[:, None]
    held = (hit_holder == own_req) & live
    rank = jnp.cumsum(held.astype(jnp.int32), axis=1) - 1
    picks = held[:, None, :] & (rank[:, None, :] == jnp.arange(capacity)[None, :, None])
    wanted = jnp.sum(jnp.where(picks, hit_slot[:, None, :], 0), axis=2)
    present = jnp.any(picks, axis=2)
    own_holders = hit_holder[own_req]
    outgoing = jnp.where(present[:, :, None, None], kv_pool[wanted], jnp.zeros((), jnp.bfloat16))
    incoming = lax.all_to_all(outgoing, "replica", split_axis=0, concat_axis=0, tiled=True)
    fetched = arrange(incoming, own_holders, capacity)
    fetched = fetched.reshape(cached_len, pair_width)
    keys_all = jnp.concatenate([fetched[:, :head_dim], new_keys], axis=0)
    vals_all = jnp.concatenate([fetched[:, head_dim:], new_vals], axis=0)
    scores = jnp.einsum(
        "chd,sd->hcs", query, keys_all, preferred_element_type=jnp.float32
    ) * head_dim ** (-0.5)
    key_pos = jnp.arange(cached_len + span, dtype=jnp.int32)
    query_pos = jnp.arange(span, dtype=jnp.int32)
    cached_ok = key_pos[None, :] < length
    fresh_ok = key_pos[None, :] - cached_len <= query_pos[:, None]
    visible = jnp.where(key_pos[None, :] < cached_len, cached_ok, fresh_ok)
    scores = jnp.where(visible, scores, -jnp.inf)
    top = jnp.max(scores, axis=-1, keepdims=True)
    weights = jnp.exp(scores - top)
    weights = (weights / jnp.sum(weights, axis=-1, keepdims=True)).astype(jnp.bfloat16)
    mixed = jnp.einsum("hcs,sd->chd", weights, vals_all, preferred_element_type=jnp.float32)
    mixed = mixed.astype(jnp.bfloat16).reshape(span, -1)
    partial_out = jnp.dot(mixed, w_output, preferred_element_type=jnp.float32)
    summed = lax.psum_scatter(
        partial_out.astype(jnp.bfloat16), "tensor", scatter_dimension=1, tiled=True
    )
    return (summed, pool_after)


def solution(mesh):
    return jax.shard_map(
        local,
        mesh=mesh,
        in_specs=(
            P("replica", None),
            P(),
            P(None, "tensor"),
            P(None, "tensor"),
            P(),
            P(),
            P("tensor", None),
            P("replica", None, "tensor"),
            P(),
            P(),
            P(),
            P(),
            P(),
        ),
        out_specs=(P("replica", "tensor"), P("replica", None, "tensor")),
        check_vma=False,
    )
```

profile of v0, /device:TPU:6, one launch (start us, length us, event | category | flops | bytes accessed | tf_op | source)
XLA Modules:
  0.0 340.9 jit_solution(15052725066877418889)
XLA Ops:
  8.0 0.8 and_select_fusion
  8.8 0.8 fusion.33
  10.0 0.8 select_reduce_fusion
  11.1 3.6 %gather_fusion = bf16[48,128,256]{2,1,0:T(8,128)(2,1)} fusion(bf16[8,128,256]{2,1,0:T(8,128)(2,1)} %param.20, s32[1024]{0:T(1024)S(1)} %pad_clamp_fusion.1), kind=kCustom, calls=%fused_computation | custom fusion | bytes 6291648 | tf_op jit(solution)/shard_map/gather | solution.py:94
  14.7 3.9 %broadcast_select_fusion = bf16[16,3,128,256]{3,2,1,0:T(8,128)(2,1)} fusion(bf16[16,3,128,256]{3,2,1,0:T(8,128)(2,1)} %bitcast.53, pred[16,3]{1,0:T(8,128)(4,1)S(1)} %copy.50), kind=kLoop, calls=%fused_computation.17 | loop fusion | flops 1572864 | bytes 6291504 | tf_op jit(solution)/shard_map/jit(_where)/select_n | solution.py:94
  18.6 8.7 %all-to-all-start = ((bf16[16,3,128,256]{3,2,1,0:T(8,128)(2,1)}), bf16[16,3,128,256]{3,2,1,0:T(8,128)(2,1)}, u32[]{:S(2)}, u32[]{:S(2)}) async-start(bf16[16,3,128,256]{3,2,1,0:T(8,128)(2,1)} %broadcast_select_fusion), calls=%async_computation | async-start | bytes 6291456 | tf_op jit(solution)/shard_map/all_to_all | solution.py:95
  28.1 3.7 %fusion.4 = f32[512]{0:T(512)S(1)} fusion(bf16[512,5120]{1,0:T(8,128)(2,1)} %param.13), kind=kLoop, calls=%fused_computation.13 | loop fusion | flops 7863808 | bytes 5244928 | tf_op jit(solution)/shard_map/reduce_sum | solution.py:11
  31.8 4.5 %fusion.14 = f32[512,256]{0,1:T(8,128)S(1)} fusion(bf16[5120,256]{1,0:T(8,128)(2,1)S(1)} %copy-done.8, bf16[512,5120]{1,0:T(8,128)(2,1)} %param.13, f32[5120]{0:T(1024)S(1)} %copy-done.9, f32[512]{0:T(512)S(1)} %add_rsqrt_fusion.2), kind=kOutput, calls=%fused_computation.26 | convolution fusion | flops 1352663040 | bytes 8411136 | tf_op jit(solution)/shard_map/dot_general | solution.py:67
  37.2 1.2 multiply_cosine_fusion
  38.4 0.8 copy.66
  39.3 0.7 copy.52
  40.3 1.7 copy.56
  42.1 6.0 %multiply_reduce_fusion = (f32[512,2]{0,1:T(2,128)S(1)}, f32[512,256]{0,1:T(8,128)}) fusion(bf16[5120,256]{1,0:T(8,128)(2,1)} %param.15, bf16[512,5120]{1,0:T(8,128)(2,1)} %param.13, f32[5120]{0:T(1024)} %param.14, f32[512]{0:T(512)S(1)} %add_rsqrt_fusion.2), kind=kOutput, calls=%fused_computation.32 | convolution fusion | flops 1352924160 | bytes 8415232 | tf_op jit(solution)/shard_map/dot_general | solution.py:63
  48.1 1.2 copy.54
  49.3 0.7 fusion.30
  50.2 0.7 fusion.29
  50.9 0.7 iota_compare_fusion.1
  51.8 1.2 subtract_convert_fusion
  53.0 7.3 %fusion.2 = pred[512,6656]{0,1:T(8,128)(4,1)} fusion(s32[6656]{0:T(1024)S(1)} %iota_add_fusion, pred[6656]{0:T(1024)(128)(4,1)S(1)} %get-tuple-element.18, pred[6656]{0:T(1024)(128)(4,1)S(1)} %get-tuple-element.19), kind=kLoop, calls=%fused_computation.9 | loop fusion | flops 6815744 | bytes 3447808 | tf_op jit(solution)/shard_map/jit(_where)/select_n | solution.py:107
  60.3 56.3 %all-to-all-done = bf16[16,3,128,256]{3,2,1,0:T(8,128)(2,1)} async-done(((bf16[16,3,128,256]{3,2,1,0:T(8,128)(2,1)}), bf16[16,3,128,256]{3,2,1,0:T(8,128)(2,1)}, u32[]{:S(2)}, u32[]{:S(2)}) %all-to-all-start) | async-done | bytes 3145760 | tf_op jit(solution)/shard_map/all_to_all | solution.py:95
  116.6 4.5 %gather_fusion.1 = bf16[48,128,256]{2,1,0:T(8,128)(2,1)} fusion(bf16[48,128,256]{2,1,0:T(8,128)(2,1)} %bitcast.2, s32[1024]{0:T(1024)S(1)} %pad_clamp_fusion), kind=kCustom, calls=%fused_computation.1 | custom fusion | bytes 6291648 | tf_op jit(solution)/shard_map/gather | solution.py:35
  121.1 3.2 fusion.35
  124.3 12.8 %fusion.9 = f32[6656,512,2]{1,0,2:T(8,128)} fusion(bf16[512,128]{1,0:T(8,128)(2,1)S(1)} %copy.53, bf16[6144,128]{1,0:T(8,128)(2,1)S(1)} %get-tuple-element.5, bf16[512,2,64]{2,0,1:T(8,128)(2,1)S(1)} %get-tuple-element.7, bf16[512,2,64]{2,0,1:T(8,128)(2,1)S(1)} %get-tuple-element.6), kind=kOutput, calls=%fused_computation.22 | convolution fusion | flops 1748762624 | bytes 29229056 | tf_op jit(solution)/shard_map/chd,sd->hcs/dot_general | solution.py:100
  137.1 6.5 %broadcast_in_dim.60 = pred[2,512,6656]{1,2,0:T(8,128)(4,1)} broadcast(pred[512,6656]{0,1:T(8,128)(4,1)} %fusion.2), dimensions={1,2} | broadcast | bytes 10223616 | tf_op jit(solution)/shard_map/jit(_where)/broadcast_in_dim | solution.py:108
  143.6 12.5 %mul.185 = f32[6656,512,2]{1,0,2:T(8,128)} broadcast(f32[]{:T(128)} %constant.74.clone.1), dimensions={} | broadcast | bytes 27262980 | tf_op jit(solution)/shard_map/mul | solution.py:100
  156.1 12.5 %broadcast_in_dim.61 = f32[2,512,6656]{1,2,0:T(8,128)} broadcast(f32[]{:T(128)} %constant.75.clone.1), dimensions={} | broadcast | bytes 27262980 | tf_op jit(solution)/shard_map/jit(_where)/broadcast_in_dim | solution.py:108
  168.6 65.1 %fusion.36 = (f32[2,512]{1,0:T(2,128)S(1)}, f32[2,512,6656]{1,2,0:T(8,128)}) fusion(pred[2,512,6656]{1,2,0:T(8,128)(4,1)} %broadcast_in_dim.60, f32[2,512,6656]{1,2,0:T(8,128)} %broadcast_in_dim.61, f32[6656,512,2]{1,0,2:T(8,128)} %fusion.9, f32[6656,512,2]{1,0,2:T(8,128)} %mul.185), kind=kOutput, calls=%fused_computation.85 | output fusion | flops 40901120 | bytes 115871744 | tf_op jit(solution)/shard_map/sub | solution.py:110
  233.8 11.1 %fusion.16 = bf16[128,2,512]{2,0,1:T(8,128)(2,1)S(1)} fusion(f32[2,512,6656]{1,2,0:T(8,128)} %get-tuple-element.17, f32[2,512]{1,0:T(2,128)S(1)} %get-tuple-element.16, bf16[512,128]{1,0:T(8,128)(2,1)S(1)} %copy-done.3, bf16[6144,128]{1,0:T(8,128)(2,1)S(1)} %copy-done.2), kind=kOutput, calls=%fused_computation.27 | convolution fusion | flops 1762000896 | bytes 29233152 | tf_op jit(solution)/shard_map/hcs,sd->chd/dot_general | solution.py:112
  244.9 3.9 %convolution_convert_fusion.1 = bf16[512,5120]{0,1:T(8,128)(2,1)} fusion(bf16[512,256]{0,1:T(8,128)(2,1)S(1)} %bitcast.58, bf16[256,5120]{1,0:T(8,128)(2,1)S(1)} %copy-done), kind=kOutput, calls=%fused_computation.16 | convolution fusion | flops 1344798720 | bytes 8126464 | tf_op jit(solution)/shard_map/dot_general | solution.py:114
  250.0 4.7 %copy.67 = bf16[8,8,128,256]{3,1,2,0:T(8,128)(2,1)S(1)} copy(bf16[8,8,128,256]{3,2,1,0:T(8,128)(2,1)} %bitcast.54) | data formatting | bytes 8388608
  255.8 0.9 copy_select_fusion
  256.7 76.7 %reduce-scatter.2.cloned.1.call-done = bf16[512,320]{0,1:T(8,128)(2,1)} async-done(((bf16[512,5120]{0,1:T(8,128)(2,1)}), bf16[512,320]{0,1:T(8,128)(2,1)}) %reduce-scatter.2.cloned.1.call-update) | async-done | bytes 327696 | tf_op jit(solution)/shard_map/reduce_scatter | solution.py:115
  (59 shorter events, 5.2 us)
Async XLA Ops:
  8.0 236.9 %copy-start = (bf16[256,5120]{1,0:T(8,128)(2,1)S(1)}, bf16[256,5120]{1,0:T(8,128)(2,1)}, u32[]{:S(2)}) copy-start(bf16[256,5120]{1,0:T(8,128)(2,1)} %param.19) | copy-start | bytes 7864324
  18.6 8.8 %copy-start.10 = (s32[16]{0:T(128)S(1)}, s32[16]{0:T(128)}, u32[]{:S(2)}) copy-start(s32[16]{0:T(128)} %param.21) | copy-start | bytes 196
  18.6 98.0 %all-to-all-start = ((bf16[16,3,128,256]{3,2,1,0:T(8,128)(2,1)}), bf16[16,3,128,256]{3,2,1,0:T(8,128)(2,1)}, u32[]{:S(2)}, u32[]{:S(2)}) async-start(bf16[16,3,128,256]{3,2,1,0:T(8,128)(2,1)} %broadcast_select_fusion), calls=%async_computation | async-start | bytes 6291456 | tf_op jit(solution)/shard_map/all_to_all | solution.py:95
  27.3 4.5 %copy-start.9 = (f32[5120]{0:T(1024)S(1)}, f32[5120]{0:T(1024)}, u32[]{:S(2)}) copy-start(f32[5120]{0:T(1024)} %param.14) | copy-start | bytes 61444
  27.3 222.7 %all-gather.2.cloned.1.call-start = ((), (), s32[]{:S(2)}) async-start(), calls=%async_computation.3 | async-start | bytes 4456448 | tf_op jit(solution)/shard_map/all_gather | solution.py:71
  27.4 4.4 %copy-start.8 = (bf16[5120,256]{1,0:T(8,128)(2,1)S(1)}, bf16[5120,256]{1,0:T(8,128)(2,1)}, u32[]{:S(2)}) copy-start(bf16[5120,256]{1,0:T(8,128)(2,1)} %param.16) | copy-start | bytes 7864324
  31.8 5.3 %copy-start.6 = (f32[128]{0:T(128)S(1)}, f32[128]{0:T(128)}, u32[]{:S(2)}) copy-start(f32[128]{0:T(128)} %param.18) | copy-start | bytes 1540
  39.3 294.2 %reduce-scatter.2.cloned.1.call-start = ((), (), s32[]{:S(2)}) async-start(), calls=%async_computation.2 | async-start | bytes 5570560 | tf_op jit(solution)/shard_map/reduce_scatter | solution.py:115
  42.1 9.6 %copy-start.7 = (f32[128]{0:T(128)S(1)}, f32[128]{0:T(128)}, u32[]{:S(2)}) copy-start(f32[128]{0:T(128)} %param.17) | copy-start | bytes 1540
  168.6 65.1 %copy-start.2 = (bf16[6144,128]{1,0:T(8,128)(2,1)S(1)}, bf16[6144,128]{1,0:T(8,128)(2,1)}, u32[]{:S(2)}) copy-start(bf16[6144,128]{1,0:T(8,128)(2,1)} %get-tuple-element.4) | copy-start | bytes 4718596
  168.6 65.1 %copy-start.3 = (bf16[512,128]{1,0:T(8,128)(2,1)S(1)}, bf16[512,128]{1,0:T(8,128)(2,1)}, u32[]{:S(2)}) copy-start(bf16[512,128]{1,0:T(8,128)(2,1)} %copy.52) | copy-start | bytes 393220
  248.8 0.7 copy-start.5
  248.8 0.9 copy-start.4
  254.8 1.0 copy-start.1
Sparse Core Ops, SparseCore 0:
  39.4 80.8 all-gather.1
Sparse Core Ops, SparseCore 1:
  248.9 84.5 reduce-scatter.1
where the time goes:
time: 342 us; the launch traced here: 341 us
  waiting for transfers between devices  133 us (39%)
  other arithmetic  88.9 us (26%)
  local copies, waits for them, and re-layouts  55.5 us (16%)
  matrix products  38.9 us (11%)
  between operations  15.8 us (5%)
  starting transfers between devices  8.83 us (3%)
    reduce_scatter x1, waiting for transfers between devices, local(): lax.psum_scatter(partial_out.astype(jnp.bfloat16), 'tensor', scatter_dime...  76.7 us
    sub x1, other arithmetic, local(): weights = jnp.exp(scores - top)  65.1 us
    all_to_all x1, waiting for transfers between devices, local(): lax.all_to_all(outgoing, 'replica', split_axis=0, concat_axis=0, tiled=True)  56.3 us
    broadcast_in_dim x2, local copies, waits for them, and re-layouts, local(): scores = jnp.where(visible, scores, -jnp.inf)  19.1 us
    dot_general x1, matrix products, local(): jnp.einsum('chd,sd->hcs', query, keys_all, preferred_element_type=jnp.flo...  12.8 us
    mul x1, local copies, waits for them, and re-layouts, local(): jnp.einsum('chd,sd->hcs', query, keys_all, preferred_element_type=jnp.flo...  12.5 us
    dot_general x1, matrix products, local(): jnp.einsum('hcs,sd->chd', weights, vals_all, preferred_element_type=jnp.f...  11.1 us
    all_to_all x1, starting transfers between devices, local(): lax.all_to_all(outgoing, 'replica', split_axis=0, concat_axis=0, tiled=True)  8.75 us
  transfers between devices with their start and end apart: 3, of which 2 were waited for; matrix products, arithmetic and copies ran while one was open for 50% of the time, Pallas kernels for 0%

commit v1 on v0

v1 whole, which is shorter than its diff:
```python
import functools
import math

import jax
import jax.numpy as jnp
from jax import lax
from jax.experimental import pallas as pl
from jax.experimental.pallas import tpu as pltpu
from jax.sharding import PartitionSpec as P

EPS = 1e-06
THETA = 1000000.0
SIDE = 4
NEG = -1e30
VMEM = 58 * 2**20


def rms_scale(values, gain):
    mean_sq = jnp.mean(values * values, axis=-1, keepdims=True)
    return values * lax.rsqrt(mean_sq + EPS) * gain


def rotate(values, position):
    half = values.shape[-1] // 2
    freqs = THETA ** (-2.0 * jnp.arange(half, dtype=jnp.float32) / values.shape[-1])
    angle = position[..., None] * freqs
    cosine = jnp.cos(angle)
    sine = jnp.sin(angle)
    first = values[..., :half]
    second = values[..., half:]
    return jnp.concatenate(
        [first * cosine - second * sine, second * cosine + first * sine], axis=-1
    )


def flash(q, chunks, scale):
    rows, head = q.shape
    top = total = acc = None
    for load, mask in chunks:
        keys, vals = load()
        width = keys.shape[0]
        s = lax.dot_general(
            q, keys, (((1,), (1,)), ((), ())), preferred_element_type=jnp.float32
        )
        s = mask(s)
        part = s[:, :128]
        for k in range(1, width // 128):
            part = jnp.maximum(part, s[:, k * 128:(k + 1) * 128])
        now = jnp.max(part, axis=1, keepdims=True)
        if top is None:
            total = jnp.zeros((rows, 128), jnp.float32)
            acc = jnp.zeros((rows, head), jnp.float32)
        else:
            now = jnp.maximum(top, now)
            shrink = jnp.exp2((top - now) * scale)
            total = total * shrink
            acc = acc * shrink
        p = jnp.exp2((s - now) * scale)
        for k in range(width // 128):
            total = total + p[:, k * 128:(k + 1) * 128]
        acc = acc + jnp.dot(p.astype(jnp.bfloat16), vals, preferred_element_type=jnp.float32)
        top = now
    return top, jnp.sum(total, axis=1, keepdims=True), acc


def picked(rows_ref, info_ref, pool_ref, kv, sems, chunk):
    half = pool_ref.shape[1]
    keys = kv.shape[0]
    head = kv.shape[1] // 2
    copies = [
        pltpu.make_async_copy(pool_ref.at[rows_ref[j]], kv.at[pl.ds(j * half, half)], sems.at[j])
        for j in range(keys // half)
    ]
    for copy in copies:
        copy.start()

    def wait(part, parts):
        for copy in copies[len(copies) * part // parts:len(copies) * (part + 1) // parts]:
            copy.wait()

    def load(c):
        span = slice(c * chunk, (c + 1) * chunk)
        return kv[span, :head], kv[span, head:]

    def mask(c, s):
        if (c + 1) * chunk <= keys // 2:
            return s
        index = lax.broadcasted_iota(jnp.int32, (8, chunk), 1) + c * chunk
        pos = index // half * (2 * half) + index % half + info_ref[1] * half
        return s + jnp.where(pos < info_ref[0], 0.0, NEG)[:1]

    chunks = [
        (functools.partial(load, c), functools.partial(mask, c)) for c in range(keys // chunk)
    ]
    return wait, chunks


def heads(q_ref):
    head = q_ref.shape[1] // 2
    return jnp.concatenate([q_ref[:, :head], q_ref[:, head:]], axis=0)


def log_sums(top, total, scale):
    return top * scale + jnp.log(total) * math.log2(math.e)


def lanes_of(columns, span):
    lane = lax.broadcasted_iota(jnp.int32, (span, 128), 1)
    out = jnp.zeros((span, 128), jnp.float32)
    for k, column in enumerate(columns):
        out = jnp.where(lane == k, column, out)
    return out.T


def after_wait(wait, chunk):
    load, mask = chunk

    def waited():
        wait()
        return load()

    return waited, mask


def other_kernel(
    rows_ref, info_ref, q_hbm, pool_ref, out_ref, kv, q_ref, sems, q_sem, *, chunk
):
    span, width = q_ref.shape
    head = width // 2
    scale = head ** (-0.5) * math.log2(math.e)
    copy = pltpu.make_async_copy(q_hbm, q_ref, q_sem)
    copy.start()
    wait, chunks = picked(rows_ref, info_ref, pool_ref, kv, sems, chunk)
    copy.wait()
    q = heads(q_ref)
    for part, first in enumerate((0, len(chunks) // 2)):
        chunks[first] = after_wait(functools.partial(wait, part, 2), chunks[first])
    top, total, acc = flash(q, chunks, scale)
    out = (acc / total).astype(jnp.bfloat16)
    sums = log_sums(top, total, scale)
    columns = []
    for h in range(2):
        out_ref[:span, h * head:(h + 1) * head] = out[h * span:(h + 1) * span]
        rest = sums[h * span:(h + 1) * span]
        for _ in range(3):
            piece = rest.astype(jnp.bfloat16).astype(jnp.float32)
            columns.append(piece)
            rest = rest - piece
    stats = lanes_of(columns, span)[:16].astype(jnp.bfloat16)
    out_ref[span:span + 16] = stats[:, :width]
    out_ref[span + 16:] = stats[:, width:]


def own_kernel(
    rows_ref, info_ref, q_hbm, fresh_hbm, pool_ref, later_ref, out_ref, sum_ref,
    kv, q_ref, fresh_ref, sems, q_sem, fresh_sem, *, chunk,
):
    del later_ref
    span, width = q_ref.shape
    head = width // 2
    scale = head ** (-0.5) * math.log2(math.e)
    first = pltpu.make_async_copy(q_hbm, q_ref, q_sem)
    first.start()
    second = pltpu.make_async_copy(fresh_hbm, fresh_ref, fresh_sem)
    second.start()
    wait, chunks = picked(rows_ref, info_ref, pool_ref, kv, sems, chunk)
    first.wait()
    second.wait()

    def causal(s):
        pos = lax.broadcasted_iota(jnp.int32, s.shape, 1)
        token = lax.broadcasted_iota(jnp.int32, s.shape, 0)
        token = jnp.where(token < span, token, token - span)
        return jnp.where(pos <= token, s, NEG)

    new = (lambda: (fresh_ref[:, :head], fresh_ref[:, head:]), causal)
    chunks[0] = after_wait(functools.partial(wait, 0, 1), chunks[0])
    top, total, acc = flash(heads(q_ref), [new] + chunks, scale)
    out = acc / total
    sums = log_sums(top, total, scale)
    for h in range(2):
        out_ref[:, h * head:(h + 1) * head] = out[h * span:(h + 1) * span]
    sum_ref[...] = lanes_of([sums[:span], sums[span:]], span)[:8]


def merge_kernel(own_ref, sum_ref, other_ref, first_ref, second_ref):
    span, width = own_ref.shape
    head = width // 2
    half = span // 2
    stats = jnp.concatenate([other_ref[span:span + 16], other_ref[span + 16:]], axis=1)
    stats = stats.astype(jnp.float32)
    shares = []
    for h in range(2):
        theirs = stats[3 * h:3 * h + 1] + stats[3 * h + 1:3 * h + 2] + stats[3 * h + 2:3 * h + 3]
        gap = theirs - sum_ref[h:h + 1]
        shares += [1.0 / (1.0 + jnp.exp2(gap)), 1.0 / (1.0 + jnp.exp2(-gap))]
    row = lax.broadcasted_iota(jnp.int32, (128, span), 0)
    table = jnp.zeros((128, span), jnp.float32)
    for k, share in enumerate(shares):
        table = jnp.where(row == k, share, table)
    table = table.T
    for h in range(2):
        lanes = slice(h * head, (h + 1) * head)
        out = own_ref[:, lanes] * table[:, 2 * h:2 * h + 1]
        out = out + other_ref[:span, lanes].astype(jnp.float32) * table[:, 2 * h + 1:2 * h + 2]
        out = out.astype(jnp.bfloat16)
        first_ref[:, lanes] = out[:half]
        second_ref[:, lanes] = out[half:]


def attend(rows, info, query, query_other, fresh, pool_half, pairs):
    span, width = query.shape
    head = width // 2
    entries = rows.shape[0]
    keys = entries * pool_half.shape[1]
    vmem = pl.BlockSpec(memory_space=pltpu.VMEM)
    smem = pl.BlockSpec(memory_space=pltpu.SMEM)
    hbm = pl.BlockSpec(memory_space=pltpu.HBM)
    params = pltpu.CompilerParams(vmem_limit_bytes=VMEM)
    kv = pltpu.VMEM((keys, width), jnp.bfloat16)
    tokens = pltpu.VMEM((span, width), jnp.bfloat16)
    sems, sem = pltpu.SemaphoreType.DMA((entries,)), pltpu.SemaphoreType.DMA

    def cost(number):
        return pl.CostEstimate(
            flops=8 * span * number * head,
            bytes_accessed=2 * number * width,
            transcendentals=2 * span * number,
        )

    other = pl.pallas_call(
        functools.partial(other_kernel, chunk=512),
        out_shape=jax.ShapeDtypeStruct((span + 32, width), jnp.bfloat16),
        in_specs=[smem, smem, hbm, hbm],
        out_specs=vmem,
        scratch_shapes=[kv, tokens, sems, sem],
        compiler_params=params,
        cost_estimate=cost(keys),
        name="other",
    )(rows, info, query_other, pool_half)
    arrived = lax.ppermute(other, "tensor", pairs)
    own, sums = pl.pallas_call(
        functools.partial(own_kernel, chunk=512),
        out_shape=[
            jax.ShapeDtypeStruct((span, width), jnp.float32),
            jax.ShapeDtypeStruct((8, span), jnp.float32),
        ],
        in_specs=[smem, smem, hbm, hbm, hbm, hbm],
        out_specs=[vmem, vmem],
        scratch_shapes=[kv, tokens, tokens, sems, sem, sem],
        compiler_params=params,
        cost_estimate=cost(keys + span),
        name="own",
    )(rows, info, query, fresh, pool_half, other)
    return pl.pallas_call(
        merge_kernel,
        out_shape=[jax.ShapeDtypeStruct((span // 2, width), jnp.bfloat16)] * 2,
        in_specs=[vmem] * 3,
        out_specs=[vmem] * 2,
        compiler_params=params,
        name="merge",
    )(own, sums, arrived)


def after_kernel(*refs):
    del refs


def after(fresh, others):
    hbm = pl.BlockSpec(memory_space=pl.ANY)
    return pl.pallas_call(
        after_kernel,
        out_shape=jax.ShapeDtypeStruct(fresh.shape, fresh.dtype),
        in_specs=[hbm] * (1 + len(others)),
        out_specs=hbm,
        input_output_aliases={0: 0},
        name="after",
    )(fresh, *others)


def arrange_kernel(place_ref, w_ref, *refs):
    (stay, ahead, back), turned, sem = refs[:-2], refs[-2], refs[-1]
    columns = turned.shape[1]
    for pair in range(SIDE * SIDE // 2):
        both = w_ref[:, 2 * pair * columns:2 * (pair + 1) * columns].T
        turned[2 * pair] = both[:columns]
        turned[2 * pair + 1] = both[columns:]
    x, y = place_ref[0], place_ref[1]
    targets = [(0, j, stay, j) for j in range(SIDE)]
    targets += [(1, j, ahead, j) for j in range(SIDE)] + [(3, j, back, j) for j in range(SIDE)]
    targets += [(2, j, ahead, SIDE + j) for j in range(2)] + [(2, j, back, 2 + j) for j in range(2, SIDE)]
    copies = []
    for n, (i, j, out, slot) in enumerate(targets):
        source = turned.at[lax.rem(x + i, SIDE) * SIDE + lax.rem(y + j, SIDE)]
        copies.append(pltpu.make_async_copy(source, out.at[slot], sem.at[n]))
        copies[-1].start()
    for copy in copies:
        copy.wait()


def arrange(place, w_output):
    width, columns = w_output.shape
    columns //= SIDE * SIDE
    blocks = (SIDE, SIDE + 2, SIDE + 2)
    return pl.pallas_call(
        arrange_kernel,
        out_shape=[
            jax.ShapeDtypeStruct((n, columns, width), w_output.dtype) for n in blocks
        ],
        in_specs=[
            pl.BlockSpec(memory_space=pltpu.SMEM), pl.BlockSpec(memory_space=pltpu.VMEM)
        ],
        out_specs=[pl.BlockSpec(memory_space=pl.ANY)] * len(blocks),
        scratch_shapes=[
            pltpu.VMEM((SIDE * SIDE, columns, width), w_output.dtype),
            pltpu.SemaphoreType.DMA((SIDE * SIDE,)),
        ],
        compiler_params=pltpu.CompilerParams(vmem_limit_bytes=VMEM),
        name="arrange",
    )(place, w_output)


def project_kernel(*refs):
    mixed, (stay, ahead, back, low, high), outs = refs[:SIDE], refs[SIDE:-10], refs[-10:-6]
    m_all, w_all, sent, kept, in_sems, out_sems = refs[-6:]

    def weight(i, j):
        if i == 2:
            return low.at[j] if j < 2 else high.at[j - 2]
        return {0: stay, 1: ahead, 3: back}[i].at[j]

    arrivals = [
        pltpu.make_async_copy(mixed[i], m_all.at[i], in_sems.at[i]) for i in range(SIDE)
    ]
    order = [2, 1, 3, 0]
    for j in order:
        for i in range(SIDE):
            n = j * SIDE + i
            arrivals.append(
                pltpu.make_async_copy(weight(i, j), w_all.at[n], in_sems.at[SIDE + n])
            )
    for copy in arrivals:
        copy.start()
    for copy in arrivals[:SIDE]:
        copy.wait()
    results = []
    for step, j in enumerate(order):
        for copy in arrivals[SIDE * (step + 1):SIDE * (step + 2)]:
            copy.wait()
        total = None
        for i in range(SIDE):
            part = lax.dot_general(
                w_all[j * SIDE + i], m_all[i], (((1,), (1,)), ((), ())),
                preferred_element_type=jnp.float32,
            )
            part = part.astype(jnp.bfloat16).astype(jnp.float32)
            total = part if total is None else total + part
        result = sent.at[j - 1] if j else kept
        result[...] = total.astype(result.dtype)
        results.append(pltpu.make_async_copy(result, outs[j - 1], out_sems.at[j]))
        results[-1].start()
    for copy in results:
        copy.wait()


def project(mixed, weights):
    span, width = mixed[0].shape
    columns = weights[0].shape[1]
    hbm = pl.BlockSpec(memory_space=pltpu.HBM)
    sent = jax.ShapeDtypeStruct((columns, span), jnp.bfloat16)
    return pl.pallas_call(
        project_kernel,
        out_shape=[sent] * (SIDE - 1) + [jax.ShapeDtypeStruct((columns, span), jnp.float32)],
        in_specs=[hbm] * (SIDE + len(weights)),
        out_specs=[hbm] * SIDE,
        scratch_shapes=[
            pltpu.VMEM((SIDE, span, width), jnp.bfloat16),
            pltpu.VMEM((SIDE * SIDE, columns, width), jnp.bfloat16),
            pltpu.VMEM((SIDE - 1, columns, span), jnp.bfloat16),
            pltpu.VMEM((columns, span), jnp.float32),
            pltpu.SemaphoreType.DMA((SIDE + SIDE * SIDE,)),
            pltpu.SemaphoreType.DMA((SIDE,)),
        ],
        compiler_params=pltpu.CompilerParams(vmem_limit_bytes=VMEM),
        cost_estimate=pl.CostEstimate(
            flops=2 * span * width * columns * SIDE * SIDE,
            bytes_accessed=2 * columns * width * SIDE * SIDE,
            transcendentals=0,
        ),
        name="project",
    )(*mixed, *weights)


def store_kernel(pick_ref, have_ref, fresh_ref, pool_ref, out_ref, sems):
    rows = pool_ref.shape[0]

    def copy(s, source):
        return pltpu.make_async_copy(source, out_ref.at[s], sems.at[s])

    for s in range(rows):
        here = have_ref[s] > 0

        @pl.when(here)
        def _():
            copy(s, fresh_ref.at[pick_ref[s]]).start()

        @pl.when(jnp.logical_not(here))
        def _():
            copy(s, pool_ref.at[s]).start()

    for s in range(rows):
        copy(s, pool_ref.at[s]).wait()


def store(pick, have, gathered, kv_pool):
    smem = pl.BlockSpec(memory_space=pltpu.SMEM)
    hbm = pl.BlockSpec(memory_space=pl.ANY)
    return pl.pallas_call(
        store_kernel,
        out_shape=jax.ShapeDtypeStruct(kv_pool.shape, kv_pool.dtype),
        in_specs=[smem, smem, hbm, hbm],
        out_specs=pl.BlockSpec(memory_space=pltpu.VMEM),
        scratch_shapes=[pltpu.SemaphoreType.DMA((kv_pool.shape[0],))],
        name="store",
    )(pick, have, gathered, kv_pool)


def along_y(step):
    return [
        (x * SIDE + y, x * SIDE + (y + step) % SIDE) for x in range(SIDE) for y in range(SIDE)
    ]


def along_x(step):
    return [
        (x * SIDE + y, (x + step) % SIDE * SIDE + y) for x in range(SIDE) for y in range(SIDE)
    ]


def spread(value, along):
    return [value] + [lax.ppermute(value, "tensor", along(k)) for k in range(1, SIDE)]


def settle(subtotals, along):
    total = subtotals[-1]
    for k in range(1, SIDE):
        total = total + lax.ppermute(subtotals[k - 1], "tensor", along(k)).astype(jnp.float32)
    return total.astype(jnp.bfloat16)


def local(
    hidden_in,
    norm_gain,
    w_query,
    w_keyval,
    query_gain,
    key_gain,
    w_output,
    kv_pool,
    prefix_len,
    hit_holder,
    hit_slot,
    dest_holder,
    dest_slot,
):
    own_req = lax.axis_index("replica")
    own_group = lax.axis_index("tensor")
    x, y = own_group // SIDE, own_group % SIDE
    span = hidden_in.shape[0]
    pool_rows, block, pair_width = kv_pool.shape
    head_dim = pair_width // 2
    new_blocks = span // block

    part = own_group % 2
    pairs = [(k, k ^ 1) for k in range(SIDE * SIDE)]
    sent_half = lax.dynamic_slice_in_dim(kv_pool, part * (block // 2), block // 2, axis=1)
    pool_half = lax.all_gather(sent_half, "replica", axis=0, tiled=True)

    place = after(jnp.stack([x, y]), [sent_half])
    pieces = arrange(place, w_output)
    ahead = lax.ppermute(pieces[1], "tensor", along_x(1))
    back = lax.ppermute(pieces[2], "tensor", along_x(3))

    normed = rms_scale(hidden_in.astype(jnp.float32), norm_gain).astype(jnp.bfloat16)
    query = jnp.dot(normed, w_query, preferred_element_type=jnp.float32).reshape(span, -1, head_dim)
    length = prefix_len[own_req]
    position = (length + jnp.arange(span, dtype=jnp.int32)).astype(jnp.float32)
    query = rotate(rms_scale(query, query_gain), position[:, None]).astype(jnp.bfloat16)
    query = query.reshape(span, -1)
    projected = jnp.dot(normed, w_keyval, preferred_element_type=jnp.float32)
    new_keys = rotate(rms_scale(projected[:, :head_dim], key_gain), position).astype(jnp.bfloat16)
    new_vals = projected[:, head_dim:].astype(jnp.bfloat16)
    own_new = jnp.concatenate([new_keys, new_vals], axis=1)

    rows = hit_holder[own_req] * pool_rows + hit_slot[own_req]
    flat_holder = dest_holder.reshape(-1)
    flat_slot = dest_slot.reshape(-1)
    match = (flat_holder[None, :] == own_req) & (
        flat_slot[None, :] == jnp.arange(pool_rows)[:, None]
    )
    pick = jnp.sum(jnp.where(match, jnp.arange(flat_holder.shape[0])[None, :], 0), axis=1)
    have = jnp.any(match, axis=1).astype(jnp.int32)
    pick = pick.astype(jnp.int32)
    info = jnp.stack([length, part.astype(jnp.int32)])
    query = after(query, [ahead, back])
    far_low = lax.ppermute(ahead[SIDE:], "tensor", along_x(1))
    far_high = lax.ppermute(back[SIDE:], "tensor", along_x(3))
    query_other = lax.ppermute(query, "tensor", pairs)
    own_new = after(
        own_new, [pool_half, query, query_other, rows, info, pick, have, far_low, far_high]
    )
    gathered = lax.all_gather(
        own_new.reshape(new_blocks, block, pair_width), "replica", axis=0, tiled=True
    )
    mixed = attend(rows, info, query, query_other, own_new, pool_half, pairs)
    w_out = [pieces[0], ahead, back, far_low, far_high]
    halves = [project(spread(half, along_x), w_out) for half in mixed]
    pool_after = store(pick, have, gathered, kv_pool)
    kept = after(halves[1][-1], [pool_after])
    first = settle(halves[0], along_y)
    second = settle([*halves[1][:-1], kept], along_y)
    attended = jnp.concatenate([first, second], axis=1).T
    return (attended, pool_after)


def solution(mesh):
    return jax.shard_map(
        local,
        mesh=mesh,
        in_specs=(
            P("replica", None),
            P(),
            P(None, "tensor"),
            P(None, "tensor"),
            P(),
            P(),
            P("tensor", None),
            P("replica", None, "tensor"),
            P(),
            P(),
            P(),
            P(),
            P(),
        ),
        out_specs=(P("replica", "tensor"), P("replica", None, "tensor")),
        check_vma=False,
    )
```

time: 342 us -> 125 us (0.37)
  waiting for transfers between devices: 133 us -> 18.9 us
  other arithmetic: 88.9 us -> 14.1 us
  local copies, waits for them, and re-layouts: 55.5 us -> 10.6 us
  Pallas kernels: 0 us -> 34.3 us
  matrix products: 38.9 us -> 7.77 us
  starting transfers between devices: 8.83 us -> 24.3 us
    reduce_scatter x1 -> x0, waiting for transfers between devices: 76.7 us -> none  [local(): lax.psum_scatter(partial_out.astype(jnp.bfloat16), 'tensor', scatter_dime...]
    sub x3 -> x0, other arithmetic: 65.1 us -> none  [the longest x1 65.1 us: local(): weights = jnp.exp(scores - top)]
    all_to_all x1 -> x0, waiting for transfers between devices: 56.3 us -> none  [local(): lax.all_to_all(outgoing, 'replica', split_axis=0, concat_axis=0, tiled=True)]
    pallas_call x0 -> x11, Pallas kernels: none -> 34.3 us  [the longest x1 9.45 us: attend(): pl.pallas_call(functools.partial(own_kernel, chunk=512), out_shape=[jax.S...]
    dot_general x4 -> x0, matrix products: 28.4 us -> none  [the longest x1 12.8 us: local(): jnp.einsum('chd,sd->hcs', query, keys_all, preferred_element_type=jnp.flo...]
    ppermute x0 -> x18, starting transfers between devices: none -> 24.2 us  [the longest x6 8.15 us: spread(): lax.ppermute(value, 'tensor', along(k))]
    broadcast_in_dim x2 -> x0, local copies, waits for them, and re-layouts: 19.1 us -> none  [local(): scores = jnp.where(visible, scores, -jnp.inf)]
    ppermute x0 -> x18, waiting for transfers between devices: none -> 16.5 us  [the longest x6 5.22 us: spread(): lax.ppermute(value, 'tensor', along(k))]
  transfers between devices with their start and end apart: 3 -> 20, of which waited for: 2 -> 9; matrix products, arithmetic and copies ran while one was open for 50% -> 21% of each run, Pallas kernels for 0% -> 28%
where the time goes in v1:
time: 125 us; the launch traced here: 124 us
  Pallas kernels  34.3 us (27%)
  starting transfers between devices  24.3 us (19%)
  waiting for transfers between devices  18.9 us (15%)
  between operations  14.4 us (12%)
  other arithmetic  14.1 us (11%)
  local copies, waits for them, and re-layouts  10.6 us (8%)
  matrix products  7.77 us (6%)
    pallas_call x1, Pallas kernels, attend(): pl.pallas_call(functools.partial(own_kernel, chunk=512), out_shape=[jax.S...  9.45 us
    pallas_call x1, Pallas kernels, attend(): pl.pallas_call(functools.partial(other_kernel, chunk=512), out_shape=jax....  8.27 us
    ppermute x6, starting transfers between devices, spread(): lax.ppermute(value, 'tensor', along(k))  8.15 us
    ppermute x6, starting transfers between devices, settle(): lax.ppermute(subtotals[k - 1], 'tensor', along(k)).astype(jnp.float32)  7.96 us
    pallas_call x2, Pallas kernels, project(): pl.pallas_call(project_kernel, out_shape=[sent] * (SIDE - 1) + [jax.Shape...  7.54 us
    ppermute x6, waiting for transfers between devices, spread(): lax.ppermute(value, 'tensor', along(k))  5.22 us
    dot_general x1, matrix products, local(): jnp.dot(normed, w_query, preferred_element_type=jnp.float32)  4.4 us
    pallas_call x1, Pallas kernels, arrange(): pl.pallas_call(arrange_kernel, out_shape=[jax.ShapeDtypeStruct((n, column...  4.11 us
  transfers between devices with their start and end apart: 20, of which 9 were waited for; matrix products, arithmetic and copies ran while one was open for 21% of the time, Pallas kernels for 28%

profile of v1, /device:TPU:6, one launch (start us, length us, event | category | flops | bytes accessed | tf_op | source)
XLA Modules:
  0.0 124.3 jit_solution(16831472347353125048)
XLA Ops:
  7.3 1.8 %constant_dynamic-slice_fusion.refs_1_ = bf16[8,64,256]{2,1,0:T(8,128)(2,1)} fusion(bf16[8,128,256]{2,1,0:T(8,128)(2,1)} %pool_ref.1, s32[]{:T(128)S(6)} %select_n.31), kind=kLoop, calls=%fused_computation.32 | loop fusion | bytes 524292 | tf_op jit(solution)/shard_map/dynamic_slice | solution.py:476
  9.8 4.1 %arrange.1 = (bf16[4,320,256]{2,1,0:T(8,128)(2,1)}, bf16[6,320,256]{2,1,0:T(8,128)(2,1)}, bf16[6,320,256]{2,1,0:T(8,128)(2,1)}) custom-call(s32[2]{0:T(128)} %after.4.place_ref, bf16[256,5120]{1,0:T(8,128)(2,1)} %w_ref.1), custom_call_target="tpu_custom_call" | custom-call | tf_op jit(solution)/shard_map/arrange/pallas_call | solution.py:305
  13.9 2.3 %collective-permute-start = (bf16[6,320,256]{2,1,0:T(8,128)(2,1)}, bf16[6,320,256]{2,1,0:T(8,128)(2,1)}, u32[]{:S(2)}, u32[]{:S(2)}) collective-permute-start(bf16[6,320,256]{2,1,0:T(8,128)(2,1)} %get-tuple-element.17), channel_id=1, source_target_pairs={{0,4},{1,5},{2,6},{3,7},{4,8},{5,9},{6,10},{7,11},{8,12},{9,13},{1... | collective-permute-start | bytes 2949128 | tf_op jit(solution)/shard_map/ppermute | solution.py:481
  16.2 1.4 %dynamic_slice.14 = s32[1]{0:T(128)} dynamic-slice(s32[16]{0:T(128)} %param.21, s32[]{:T(128)S(6)} %select_n.27), dynamic_slice_sizes={1} | dynamic-slice | bytes 12 | tf_op jit(solution)/shard_map/dynamic_slice | solution.py:486
  18.3 3.6 %fusion = f32[512]{0:T(512)S(1)} fusion(bf16[512,5120]{1,0:T(8,128)(2,1)} %param.13), kind=kLoop, calls=%fused_computation.2 | loop fusion | flops 7863808 | bytes 5244928 | tf_op jit(solution)/shard_map/reduce_sum | solution.py:19
  21.9 3.4 %fusion.3 = f32[512,256]{1,0:T(8,128)S(1)} fusion(bf16[5120,256]{1,0:T(8,128)(2,1)} %param.16, bf16[512,5120]{1,0:T(8,128)(2,1)S(1)} %copy-done.1, f32[5120]{0:T(1024)S(1)} %copy-done.17, f32[512]{0:T(512)S(1)} %add_rsqrt_fusion.2), kind=kOutput, calls=%fused_computation.5 | convolution fusion | flops 1352663040 | bytes 8411136 | tf_op jit(solution)/shard_map/dot_general | solution.py:490
  25.6 1.2 subtract_convert_fusion
  27.2 4.4 %multiply_reduce_fusion = (f32[512,2]{0,1:T(2,128)S(1)}, f32[512,256]{0,1:T(8,128)S(1)}) fusion(bf16[5120,256]{1,0:T(8,128)(2,1)S(1)} %copy-done, bf16[512,5120]{1,0:T(8,128)(2,1)} %param.13, f32[5120]{0:T(1024)} %param.14, f32[512]{0:T(512)S(1)} %add_rsqrt_fusion.2), kind=kOutput, calls=%fused_computation.8 | convolution fusion | flops 1352924160 | bytes 8415232 | tf_op jit(solution)/shard_map/dot_general | solution.py:485
  34.3 3.5 %collective-permute-done.refs_1_.refs_5_ = bf16[6,320,256]{2,1,0:T(8,128)(2,1)} collective-permute-done((bf16[6,320,256]{2,1,0:T(8,128)(2,1)}, bf16[6,320,256]{2,1,0:T(8,128)(2,1)}, u32[]{:S(2)}, u32[]{:S(2)}) %collective-permute-start) | collective-permute-done | bytes 983072 | tf_op jit(solution)/shard_map/ppermute | solution.py:481
  37.8 1.3 %collective-permute-done.1.refs_2_.refs_6_ = bf16[6,320,256]{2,1,0:T(8,128)(2,1)} collective-permute-done((bf16[6,320,256]{2,1,0:T(8,128)(2,1)}, bf16[6,320,256]{2,1,0:T(8,128)(2,1)}, u32[]{:S(2)}, u32[]{:S(2)}) %collective-permute-start.1) | collective-permute-done | bytes 983072 | tf_op jit(solution)/shard_map/ppermute | solution.py:482
  39.1 1.7 %collective-permute-start.2 = (bf16[512,256]{1,0:T(8,128)(2,1)}, bf16[512,256]{1,0:T(8,128)(2,1)S(1)}, u32[]{:S(2)}, u32[]{:S(2)}) collective-permute-start(bf16[512,256]{1,0:T(8,128)(2,1)} %after.5.refs_2_.q_hbm), channel_id=1, source_target_pairs={{0,1},{1,0},{2,3},{3,2},{4,5},{5,4},{6,7},{7,6},{8,9},{9,8},{10,11... | collective-permute-start | bytes 786440 | tf_op jit(solution)/shard_map/ppermute | solution.py:508
  43.2 2.0 %collective-permute-start.4 = (bf16[2,320,256]{2,1,0:T(8,128)(2,1)S(1)}, bf16[2,320,256]{2,1,0:T(8,128)(2,1)S(1)}, u32[]{:S(2)}, u32[]{:S(2)}) collective-permute-start(bf16[2,320,256]{2,1,0:T(8,128)(2,1)S(1)} %slice.40), channel_id=1, source_target_pairs={{0,12},{1,13},{2,14},{3,15},{4,0},{5,1},{6,2},{7,3},{8,4},{9,5},{1... | collective-permute-start | bytes 983048 | tf_op jit(solution)/shard_map/ppermute | solution.py:507
  45.1 1.3 %fusion.11.refs_4_.rows_ref = s32[48]{0:T(128)} fusion(s32[16,48]{1,0:T(8,128)} %param.23, s32[]{:T(128)S(6)} %select_n.27, s32[16,48]{1,0:T(8,128)} %param.22), kind=kLoop, calls=%fused_computation.40 | loop fusion | flops 96 | bytes 580 | tf_op jit(solution)/shard_map/add | solution.py:495
  50.1 2.5 %collective-permute-done.4.refs_9_.refs_8_ = bf16[2,320,256]{2,1,0:T(8,128)(2,1)S(1)} collective-permute-done((bf16[2,320,256]{2,1,0:T(8,128)(2,1)S(1)}, bf16[2,320,256]{2,1,0:T(8,128)(2,1)S(1)}, u32[]{:S(2)}, u32[]{:S(2)}) %collective-permute-start.4) | collective-permute-done | bytes 327712 | tf_op jit(solution)/shard_map/ppermute | solution.py:507
  52.6 2.4 %all-gather.3.cloned.1.call-done.refs_1_.pool_ref = bf16[128,64,256]{2,1,0:T(8,128)(2,1)} async-done(((bf16[8,64,256]{2,1,0:T(8,128)(2,1)}), bf16[128,64,256]{2,1,0:T(8,128)(2,1)}) %all-gather.3.cloned.1.call-update) | async-done | bytes 4194320 | tf_op jit(solution)/shard_map/all_gather | solution.py:477
  55.0 8.3 %other.1.later_ref = bf16[544,256]{1,0:T(8,128)(2,1)} custom-call(s32[48]{0:T(128)} %fusion.11.refs_4_.rows_ref, s32[2]{0:T(128)} %pad_add_fusion.refs_5_.info_ref, bf16[512,256]{1,0:T(8,128)(2,1)} %copy-done.6, bf16[128,64,256]{2,1,0:T(8,128)(2,1)} %all-gather.3.cloned.1.call-done.refs_1_.pool_ref), custom_call_target="tpu_custom_call" | custom-call | flops 1610612736 | bytes 1572864 | tf_op jit(solution)/shard_map/other/pallas_call | solution.py:231
  63.3 1.8 %collective-permute-start.5 = (bf16[544,256]{1,0:T(8,128)(2,1)}, bf16[544,256]{1,0:T(8,128)(2,1)S(1)}, u32[]{:S(2)}, u32[]{:S(2)}) collective-permute-start(bf16[544,256]{1,0:T(8,128)(2,1)} %other.1.later_ref), channel_id=1, source_target_pairs={{0,1},{1,0},{2,3},{3,2},{4,5},{5,4},{6,7},{7,6},{8,9},{9,8},{10,11... | collective-permute-start | bytes 835592 | tf_op jit(solution)/shard_map/ppermute | solution.py:241
  65.0 9.4 %own.1 = (f32[512,256]{1,0:T(8,128)}, f32[8,512]{1,0:T(8,128)}) custom-call(s32[48]{0:T(128)} %fusion.11.refs_4_.rows_ref, s32[2]{0:T(128)} %pad_add_fusion.refs_5_.info_ref, bf16[512,256]{1,0:T(8,128)(2,1)} %after.5.refs_2_.q_hbm, bf16[512,256]{1,0:T(8,128)(2,1)} %after.6.fresh_hbm, bf16[128,64,256]{2,1,0:T(8,128)(2,1)} %all-gather.3.cloned.1.call-done.refs_1_.pool_ref, ...), custom_call_target="tpu_custom_call" | custom-call | flops 1879048192 | bytes 1835008 | tf_op jit(solution)/shard_map/own/pallas_call | solution.py:242
  75.2 2.3 %merge.1 = (bf16[256,256]{1,0:T(8,128)(2,1)}, bf16[256,256]{1,0:T(8,128)(2,1)}) custom-call(f32[512,256]{1,0:T(8,128)} %get-tuple-element.19.own_ref, f32[8,512]{1,0:T(8,128)} %get-tuple-element.20.sum_ref, bf16[544,256]{1,0:T(8,128)(2,1)} %copy-done.5), custom_call_target="tpu_custom_call" | custom-call | tf_op jit(solution)/shard_map/merge/pallas_call | solution.py:255
  78.1 2.3 %collective-permute-start.7 = (bf16[256,256]{1,0:T(8,128)(2,1)}, bf16[256,256]{1,0:T(8,128)(2,1)S(1)}, u32[]{:S(2)}, u32[]{:S(2)}) collective-permute-start(bf16[256,256]{1,0:T(8,128)(2,1)} %get-tuple-element.21.refs_0_), channel_id=1, source_target_pairs={{0,8},{1,9},{2,10},{3,11},{4,12},{5,13},{6,14},{7,15},{8,0},{9,1},... | collective-permute-start | bytes 393224 | tf_op jit(solution)/shard_map/ppermute | solution.py:441
  80.4 3.2 %collective-permute-start.12 = (bf16[256,256]{1,0:T(8,128)(2,1)}, bf16[256,256]{1,0:T(8,128)(2,1)S(1)}, u32[]{:S(2)}, u32[]{:S(2)}) collective-permute-start(bf16[256,256]{1,0:T(8,128)(2,1)} %get-tuple-element.27.refs_0_), channel_id=1, source_target_pairs={{0,4},{1,5},{2,6},{3,7},{4,8},{5,9},{6,10},{7,11},{8,12},{9,13},{1... | collective-permute-start | bytes 393224 | tf_op jit(solution)/shard_map/ppermute | solution.py:441
  84.1 2.0 %collective-permute-start.14 = (bf16[256,256]{1,0:T(8,128)(2,1)}, bf16[256,256]{1,0:T(8,128)(2,1)S(1)}, u32[]{:S(2)}, u32[]{:S(2)}) collective-permute-start(bf16[256,256]{1,0:T(8,128)(2,1)} %get-tuple-element.27.refs_0_), channel_id=1, source_target_pairs={{0,12},{1,13},{2,14},{3,15},{4,0},{5,1},{6,2},{7,3},{8,4},{9,5},{1... | collective-permute-start | bytes 393224 | tf_op jit(solution)/shard_map/ppermute | solution.py:441
  86.1 4.8 %collective-permute-done.8.refs_3_ = bf16[256,256]{1,0:T(8,128)(2,1)S(1)} collective-permute-done((bf16[256,256]{1,0:T(8,128)(2,1)}, bf16[256,256]{1,0:T(8,128)(2,1)S(1)}, u32[]{:S(2)}, u32[]{:S(2)}) %collective-permute-start.8) | collective-permute-done | bytes 131104 | tf_op jit(solution)/shard_map/ppermute | solution.py:441
  91.6 3.8 %project.2 = (bf16[320,256]{1,0:T(8,128)(2,1)}, bf16[320,256]{1,0:T(8,128)(2,1)}, bf16[320,256]{1,0:T(8,128)(2,1)}, f32[320,256]{1,0:T(8,128)}) custom-call(bf16[256,256]{1,0:T(8,128)(2,1)} %get-tuple-element.21.refs_0_, bf16[256,256]{1,0:T(8,128)(2,1)} %copy-done.10, bf16[256,256]{1,0:T(8,128)(2,1)} %copy-done.11, bf16[256,256]{1,0:T(8,128)(2,1)} %copy-done.12, ...), custom_call_target="tpu_custom_call" | custom-call | flops 671088640 | bytes 2621440 | tf_op jit(solution)/shard_map/project/pallas_call | solution.py:371
  95.4 2.1 %collective-permute-start.11 = (bf16[320,256]{1,0:T(8,128)(2,1)}, bf16[320,256]{1,0:T(8,128)(2,1)S(1)}, u32[]{:S(2)}, u32[]{:S(2)}) collective-permute-start(bf16[320,256]{1,0:T(8,128)(2,1)} %get-tuple-element.26), channel_id=1, source_target_pairs={{0,3},{1,0},{2,1},{3,2},{4,7},{5,4},{6,5},{7,6},{8,11},{9,8},{10,9... | collective-permute-start | bytes 491528 | tf_op jit(solution)/shard_map/ppermute | solution.py:447
  98.5 1.3 %collective-permute-start.9 = (bf16[320,256]{1,0:T(8,128)(2,1)}, bf16[320,256]{1,0:T(8,128)(2,1)S(1)}, u32[]{:S(2)}, u32[]{:S(2)}) collective-permute-start(bf16[320,256]{1,0:T(8,128)(2,1)} %get-tuple-element.24), channel_id=1, source_target_pairs={{0,1},{1,2},{2,3},{3,0},{4,5},{5,6},{6,7},{7,4},{8,9},{9,10},{10,1... | collective-permute-start | bytes 491528 | tf_op jit(solution)/shard_map/ppermute | solution.py:447
  101.1 3.8 %project.3 = (bf16[320,256]{1,0:T(8,128)(2,1)}, bf16[320,256]{1,0:T(8,128)(2,1)}, bf16[320,256]{1,0:T(8,128)(2,1)}, f32[320,256]{1,0:T(8,128)}) custom-call(bf16[256,256]{1,0:T(8,128)(2,1)} %get-tuple-element.27.refs_0_, bf16[256,256]{1,0:T(8,128)(2,1)} %copy-done.7, bf16[256,256]{1,0:T(8,128)(2,1)} %copy-done.8, bf16[256,256]{1,0:T(8,128)(2,1)} %copy-done.9, ...), custom_call_target="tpu_custom_call" | custom-call | flops 671088640 | bytes 2621440 | tf_op jit(solution)/shard_map/project/pallas_call | solution.py:371
  104.9 2.0 %collective-permute-start.17 = (bf16[320,256]{1,0:T(8,128)(2,1)}, bf16[320,256]{1,0:T(8,128)(2,1)S(1)}, u32[]{:S(2)}, u32[]{:S(2)}) collective-permute-start(bf16[320,256]{1,0:T(8,128)(2,1)} %get-tuple-element.31), channel_id=1, source_target_pairs={{0,3},{1,0},{2,1},{3,2},{4,7},{5,4},{6,5},{7,6},{8,11},{9,8},{10,9... | collective-permute-start | bytes 491528 | tf_op jit(solution)/shard_map/ppermute | solution.py:447
  106.9 1.3 %collective-permute-start.16 = (bf16[320,256]{1,0:T(8,128)(2,1)}, bf16[320,256]{1,0:T(8,128)(2,1)S(1)}, u32[]{:S(2)}, u32[]{:S(2)}) collective-permute-start(bf16[320,256]{1,0:T(8,128)(2,1)} %get-tuple-element.30), channel_id=1, source_target_pairs={{0,2},{1,3},{2,0},{3,1},{4,6},{5,7},{6,4},{7,5},{8,10},{9,11},{10,... | collective-permute-start | bytes 491528 | tf_op jit(solution)/shard_map/ppermute | solution.py:447
  109.5 2.6 %store.1.refs_1_ = bf16[8,128,256]{2,1,0:T(8,128)(2,1)} custom-call(s32[8]{0:T(128)} %select_reduce_fusion.refs_6_.pick_ref, s32[8]{0:T(128)} %convert_element_type.55.refs_7_.have_ref, bf16[64,128,256]{2,1,0:T(8,128)(2,1)} %all-gather.5.cloned.1.call-done.fresh_ref, bf16[8,128,256]{2,1,0:T(8,128)(2,1)} %pool_ref.1), custom_call_target="tpu_custom_call" | custom-call | tf_op jit(solution)/shard_map/store/pallas_call | solution.py:418
  112.1 1.9 %collective-permute-done.16 = bf16[320,256]{1,0:T(8,128)(2,1)S(1)} collective-permute-done((bf16[320,256]{1,0:T(8,128)(2,1)}, bf16[320,256]{1,0:T(8,128)(2,1)S(1)}, u32[]{:S(2)}, u32[]{:S(2)}) %collective-permute-start.16) | collective-permute-done | bytes 163872 | tf_op jit(solution)/shard_map/ppermute | solution.py:447
  114.0 1.7 %collective-permute-done.15 = bf16[320,256]{1,0:T(8,128)(2,1)S(1)} collective-permute-done((bf16[320,256]{1,0:T(8,128)(2,1)}, bf16[320,256]{1,0:T(8,128)(2,1)S(1)}, u32[]{:S(2)}, u32[]{:S(2)}) %collective-permute-start.15) | collective-permute-done | bytes 163872 | tf_op jit(solution)/shard_map/ppermute | solution.py:447
  (94 shorter events, 18.7 us)
Async XLA Ops:
  7.2 20.0 %copy-start = (bf16[5120,256]{1,0:T(8,128)(2,1)S(1)}, bf16[5120,256]{1,0:T(8,128)(2,1)}, u32[]{:S(2)}) copy-start(bf16[5120,256]{1,0:T(8,128)(2,1)} %param.15) | copy-start | bytes 7864324
  7.2 14.7 %copy-start.17 = (f32[5120]{0:T(1024)S(1)}, f32[5120]{0:T(1024)}, u32[]{:S(2)}) copy-start(f32[5120]{0:T(1024)} %param.14) | copy-start | bytes 61444
  7.2 47.8 %all-gather.3.cloned.1.call-start = ((), (), s32[]{:S(2)}) async-start(), calls=%async_computation | async-start | bytes 4456448 | tf_op jit(solution)/shard_map/all_gather | solution.py:477
  9.1 100.4 %all-gather.5.cloned.1.call-start = ((), (), s32[]{:S(2)}) async-start(), calls=%async_computation.1 | async-start | bytes 4456448 | tf_op jit(solution)/shard_map/all_gather | solution.py:512
  13.9 23.9 %collective-permute-start = (bf16[6,320,256]{2,1,0:T(8,128)(2,1)}, bf16[6,320,256]{2,1,0:T(8,128)(2,1)}, u32[]{:S(2)}, u32[]{:S(2)}) collective-permute-start(bf16[6,320,256]{2,1,0:T(8,128)(2,1)} %get-tuple-element.17), channel_id=1, source_target_pairs={{0,4},{1,5},{2,6},{3,7},{4,8},{5,9},{6,10},{7,11},{8,12},{9,13},{1... | collective-permute-start | bytes 2949128 | tf_op jit(solution)/shard_map/ppermute | solution.py:481
  16.2 22.9 %collective-permute-start.1 = (bf16[6,320,256]{2,1,0:T(8,128)(2,1)}, bf16[6,320,256]{2,1,0:T(8,128)(2,1)}, u32[]{:S(2)}, u32[]{:S(2)}) collective-permute-start(bf16[6,320,256]{2,1,0:T(8,128)(2,1)} %get-tuple-element.18), channel_id=1, source_target_pairs={{0,12},{1,13},{2,14},{3,15},{4,0},{5,1},{6,2},{7,3},{8,4},{9,5},{1... | collective-permute-start | bytes 2949128 | tf_op jit(solution)/shard_map/ppermute | solution.py:482
  16.2 5.7 %copy-start.1 = (bf16[512,5120]{1,0:T(8,128)(2,1)S(1)}, bf16[512,5120]{1,0:T(8,128)(2,1)}, u32[]{:S(2)}) copy-start(bf16[512,5120]{1,0:T(8,128)(2,1)} %param.13) | copy-start | bytes 15728644
  21.9 3.6 %copy-start.15 = (f32[128]{0:T(128)S(1)}, f32[128]{0:T(128)}, u32[]{:S(2)}) copy-start(f32[128]{0:T(128)} %param.18) | copy-start | bytes 1540
  25.3 1.6 %copy-start.4 = (f32[512,256]{1,0:T(8,128)}, f32[512,256]{1,0:T(8,128)S(1)}, u32[]{:S(2)}) copy-start(f32[512,256]{1,0:T(8,128)S(1)} %fusion.3) | copy-start | bytes 1572868
  27.1 4.5 %copy-start.16 = (f32[128]{0:T(128)S(1)}, f32[128]{0:T(128)}, u32[]{:S(2)}) copy-start(f32[128]{0:T(128)} %param.17) | copy-start | bytes 1540
  27.1 5.5 %copy-start.13 = (s32[16,4]{0,1:T(4,128)S(1)}, s32[16,4]{0,1:T(4,128)}, u32[]{:S(2)}) copy-start(s32[16,4]{0,1:T(4,128)} %param.25) | copy-start | bytes 772
  27.2 5.7 %copy-start.14 = (s32[16,4]{0,1:T(4,128)S(1)}, s32[16,4]{0,1:T(4,128)}, u32[]{:S(2)}) copy-start(s32[16,4]{0,1:T(4,128)} %param.24) | copy-start | bytes 772
  39.1 10.3 %collective-permute-start.2 = (bf16[512,256]{1,0:T(8,128)(2,1)}, bf16[512,256]{1,0:T(8,128)(2,1)S(1)}, u32[]{:S(2)}, u32[]{:S(2)}) collective-permute-start(bf16[512,256]{1,0:T(8,128)(2,1)} %after.5.refs_2_.q_hbm), channel_id=1, source_target_pairs={{0,1},{1,0},{2,3},{3,2},{4,5},{5,4},{6,7},{7,6},{8,9},{9,8},{10,11... | collective-permute-start | bytes 786440 | tf_op jit(solution)/shard_map/ppermute | solution.py:508
  41.8 8.1 %collective-permute-start.3 = (bf16[2,320,256]{2,1,0:T(8,128)(2,1)S(1)}, bf16[2,320,256]{2,1,0:T(8,128)(2,1)S(1)}, u32[]{:S(2)}, u32[]{:S(2)}) collective-permute-start(bf16[2,320,256]{2,1,0:T(8,128)(2,1)S(1)} %slice.39), channel_id=1, source_target_pairs={{0,4},{1,5},{2,6},{3,7},{4,8},{5,9},{6,10},{7,11},{8,12},{9,13},{1... | collective-permute-start | bytes 983048 | tf_op jit(solution)/shard_map/ppermute | solution.py:506
  43.2 9.5 %collective-permute-start.4 = (bf16[2,320,256]{2,1,0:T(8,128)(2,1)S(1)}, bf16[2,320,256]{2,1,0:T(8,128)(2,1)S(1)}, u32[]{:S(2)}, u32[]{:S(2)}) collective-permute-start(bf16[2,320,256]{2,1,0:T(8,128)(2,1)S(1)} %slice.40), channel_id=1, source_target_pairs={{0,12},{1,13},{2,14},{3,15},{4,0},{5,1},{6,2},{7,3},{8,4},{9,5},{1... | collective-permute-start | bytes 983048 | tf_op jit(solution)/shard_map/ppermute | solution.py:507
  50.1 4.9 %copy-start.2 = (bf16[2,320,256]{2,1,0:T(8,128)(2,1)}, bf16[2,320,256]{2,1,0:T(8,128)(2,1)S(1)}, u32[]{:S(2)}) copy-start(bf16[2,320,256]{2,1,0:T(8,128)(2,1)S(1)} %collective-permute-done.3.refs_8_.refs_7_) | copy-start | bytes 983044
  52.6 2.4 %copy-start.3 = (bf16[2,320,256]{2,1,0:T(8,128)(2,1)}, bf16[2,320,256]{2,1,0:T(8,128)(2,1)S(1)}, u32[]{:S(2)}) copy-start(bf16[2,320,256]{2,1,0:T(8,128)(2,1)S(1)} %collective-permute-done.4.refs_9_.refs_8_) | copy-start | bytes 983044
  63.3 11.2 %collective-permute-start.5 = (bf16[544,256]{1,0:T(8,128)(2,1)}, bf16[544,256]{1,0:T(8,128)(2,1)S(1)}, u32[]{:S(2)}, u32[]{:S(2)}) collective-permute-start(bf16[544,256]{1,0:T(8,128)(2,1)} %other.1.later_ref), channel_id=1, source_target_pairs={{0,1},{1,0},{2,3},{3,2},{4,5},{5,4},{6,7},{7,6},{8,9},{9,8},{10,11... | collective-permute-start | bytes 835592 | tf_op jit(solution)/shard_map/ppermute | solution.py:241
  77.5 6.6 %collective-permute-start.6 = (bf16[256,256]{1,0:T(8,128)(2,1)}, bf16[256,256]{1,0:T(8,128)(2,1)S(1)}, u32[]{:S(2)}, u32[]{:S(2)}) collective-permute-start(bf16[256,256]{1,0:T(8,128)(2,1)} %get-tuple-element.21.refs_0_), channel_id=1, source_target_pairs={{0,4},{1,5},{2,6},{3,7},{4,8},{5,9},{6,10},{7,11},{8,12},{9,13},{1... | collective-permute-start | bytes 393224 | tf_op jit(solution)/shard_map/ppermute | solution.py:441
  78.1 8.0 %collective-permute-start.7 = (bf16[256,256]{1,0:T(8,128)(2,1)}, bf16[256,256]{1,0:T(8,128)(2,1)S(1)}, u32[]{:S(2)}, u32[]{:S(2)}) collective-permute-start(bf16[256,256]{1,0:T(8,128)(2,1)} %get-tuple-element.21.refs_0_), channel_id=1, source_target_pairs={{0,8},{1,9},{2,10},{3,11},{4,12},{5,13},{6,14},{7,15},{8,0},{9,1},... | collective-permute-start | bytes 393224 | tf_op jit(solution)/shard_map/ppermute | solution.py:441
  80.4 10.5 %collective-permute-start.8 = (bf16[256,256]{1,0:T(8,128)(2,1)}, bf16[256,256]{1,0:T(8,128)(2,1)S(1)}, u32[]{:S(2)}, u32[]{:S(2)}) collective-permute-start(bf16[256,256]{1,0:T(8,128)(2,1)} %get-tuple-element.21.refs_0_), channel_id=1, source_target_pairs={{0,12},{1,13},{2,14},{3,15},{4,0},{5,1},{6,2},{7,3},{8,4},{9,5},{1... | collective-permute-start | bytes 393224 | tf_op jit(solution)/shard_map/ppermute | solution.py:441
  80.4 18.1 %collective-permute-start.12 = (bf16[256,256]{1,0:T(8,128)(2,1)}, bf16[256,256]{1,0:T(8,128)(2,1)S(1)}, u32[]{:S(2)}, u32[]{:S(2)}) collective-permute-start(bf16[256,256]{1,0:T(8,128)(2,1)} %get-tuple-element.27.refs_0_), channel_id=1, source_target_pairs={{0,4},{1,5},{2,6},{3,7},{4,8},{5,9},{6,10},{7,11},{8,12},{9,13},{1... | collective-permute-start | bytes 393224 | tf_op jit(solution)/shard_map/ppermute | solution.py:441
  83.6 16.2 %collective-permute-start.13 = (bf16[256,256]{1,0:T(8,128)(2,1)}, bf16[256,256]{1,0:T(8,128)(2,1)S(1)}, u32[]{:S(2)}, u32[]{:S(2)}) collective-permute-start(bf16[256,256]{1,0:T(8,128)(2,1)} %get-tuple-element.27.refs_0_), channel_id=1, source_target_pairs={{0,8},{1,9},{2,10},{3,11},{4,12},{5,13},{6,14},{7,15},{8,0},{9,1},... | collective-permute-start | bytes 393224 | tf_op jit(solution)/shard_map/ppermute | solution.py:441
  84.1 6.8 %copy-start.10 = (bf16[256,256]{1,0:T(8,128)(2,1)}, bf16[256,256]{1,0:T(8,128)(2,1)S(1)}, u32[]{:S(2)}) copy-start(bf16[256,256]{1,0:T(8,128)(2,1)S(1)} %collective-permute-done.6.refs_1_) | copy-start | bytes 393220
  84.1 15.7 %collective-permute-start.14 = (bf16[256,256]{1,0:T(8,128)(2,1)}, bf16[256,256]{1,0:T(8,128)(2,1)S(1)}, u32[]{:S(2)}, u32[]{:S(2)}) collective-permute-start(bf16[256,256]{1,0:T(8,128)(2,1)} %get-tuple-element.27.refs_0_), channel_id=1, source_target_pairs={{0,12},{1,13},{2,14},{3,15},{4,0},{5,1},{6,2},{7,3},{8,4},{9,5},{1... | collective-permute-start | bytes 393224 | tf_op jit(solution)/shard_map/ppermute | solution.py:441
  86.1 4.8 %copy-start.11 = (bf16[256,256]{1,0:T(8,128)(2,1)}, bf16[256,256]{1,0:T(8,128)(2,1)S(1)}, u32[]{:S(2)}) copy-start(bf16[256,256]{1,0:T(8,128)(2,1)S(1)} %collective-permute-done.7.refs_2_) | copy-start | bytes 393220
  95.4 12.8 %collective-permute-start.11 = (bf16[320,256]{1,0:T(8,128)(2,1)}, bf16[320,256]{1,0:T(8,128)(2,1)S(1)}, u32[]{:S(2)}, u32[]{:S(2)}) collective-permute-start(bf16[320,256]{1,0:T(8,128)(2,1)} %get-tuple-element.26), channel_id=1, source_target_pairs={{0,3},{1,0},{2,1},{3,2},{4,7},{5,4},{6,5},{7,6},{8,11},{9,8},{10,9... | collective-permute-start | bytes 491528 | tf_op jit(solution)/shard_map/ppermute | solution.py:447
  97.4 11.0 %collective-permute-start.10 = (bf16[320,256]{1,0:T(8,128)(2,1)}, bf16[320,256]{1,0:T(8,128)(2,1)S(1)}, u32[]{:S(2)}, u32[]{:S(2)}) collective-permute-start(bf16[320,256]{1,0:T(8,128)(2,1)} %get-tuple-element.25), channel_id=1, source_target_pairs={{0,2},{1,3},{2,0},{3,1},{4,6},{5,7},{6,4},{7,5},{8,10},{9,11},{10,... | collective-permute-start | bytes 491528 | tf_op jit(solution)/shard_map/ppermute | solution.py:447
  98.5 9.9 %collective-permute-start.9 = (bf16[320,256]{1,0:T(8,128)(2,1)}, bf16[320,256]{1,0:T(8,128)(2,1)S(1)}, u32[]{:S(2)}, u32[]{:S(2)}) collective-permute-start(bf16[320,256]{1,0:T(8,128)(2,1)} %get-tuple-element.24), channel_id=1, source_target_pairs={{0,1},{1,2},{2,3},{3,0},{4,5},{5,6},{6,7},{7,4},{8,9},{9,10},{10,1... | collective-permute-start | bytes 491528 | tf_op jit(solution)/shard_map/ppermute | solution.py:447
  104.9 7.2 %collective-permute-start.17 = (bf16[320,256]{1,0:T(8,128)(2,1)}, bf16[320,256]{1,0:T(8,128)(2,1)S(1)}, u32[]{:S(2)}, u32[]{:S(2)}) collective-permute-start(bf16[320,256]{1,0:T(8,128)(2,1)} %get-tuple-element.31), channel_id=1, source_target_pairs={{0,3},{1,0},{2,1},{3,2},{4,7},{5,4},{6,5},{7,6},{8,11},{9,8},{10,9... | collective-permute-start | bytes 491528 | tf_op jit(solution)/shard_map/ppermute | solution.py:447
  106.9 7.1 %collective-permute-start.16 = (bf16[320,256]{1,0:T(8,128)(2,1)}, bf16[320,256]{1,0:T(8,128)(2,1)S(1)}, u32[]{:S(2)}, u32[]{:S(2)}) collective-permute-start(bf16[320,256]{1,0:T(8,128)(2,1)} %get-tuple-element.30), channel_id=1, source_target_pairs={{0,2},{1,3},{2,0},{3,1},{4,6},{5,7},{6,4},{7,5},{8,10},{9,11},{10,... | collective-permute-start | bytes 491528 | tf_op jit(solution)/shard_map/ppermute | solution.py:447
  108.2 7.5 %collective-permute-start.15 = (bf16[320,256]{1,0:T(8,128)(2,1)}, bf16[320,256]{1,0:T(8,128)(2,1)S(1)}, u32[]{:S(2)}, u32[]{:S(2)}) collective-permute-start(bf16[320,256]{1,0:T(8,128)(2,1)} %get-tuple-element.29), channel_id=1, source_target_pairs={{0,1},{1,2},{2,3},{3,0},{4,5},{5,6},{6,7},{7,4},{8,9},{9,10},{10,1... | collective-permute-start | bytes 491528 | tf_op jit(solution)/shard_map/ppermute | solution.py:447
  (6 other events, 4.7 us)
Sparse Core Ops, SparseCore 0:
  9.9 45.0 all-gather.2
  56.8 41.1 all-gather.4

commit v2 on v1

--- a/solution.py
+++ b/solution.py
@@ -152,20 +152,13 @@
 
 
 def own_kernel(
-    rows_ref, info_ref, q_hbm, fresh_hbm, pool_ref, later_ref, out_ref, sum_ref,
-    kv, q_ref, fresh_ref, sems, q_sem, fresh_sem, *, chunk,
+    rows_ref, info_ref, q_ref, fresh_ref, pool_ref, later_ref, out_ref, sum_ref, kv, sems, *, chunk
 ):
     del later_ref
     span, width = q_ref.shape
     head = width // 2
     scale = head ** (-0.5) * math.log2(math.e)
-    first = pltpu.make_async_copy(q_hbm, q_ref, q_sem)
-    first.start()
-    second = pltpu.make_async_copy(fresh_hbm, fresh_ref, fresh_sem)
-    second.start()
     wait, chunks = picked(rows_ref, info_ref, pool_ref, kv, sems, chunk)
-    first.wait()
-    second.wait()
 
     def causal(s):
         pos = lax.broadcasted_iota(jnp.int32, s.shape, 1)
@@ -215,7 +208,7 @@
     keys = entries * pool_half.shape[1]
     vmem = pl.BlockSpec(memory_space=pltpu.VMEM)
     smem = pl.BlockSpec(memory_space=pltpu.SMEM)
-    hbm = pl.BlockSpec(memory_space=pltpu.HBM)
+    anywhere = pl.BlockSpec(memory_space=pl.ANY)
     params = pltpu.CompilerParams(vmem_limit_bytes=VMEM)
     kv = pltpu.VMEM((keys, width), jnp.bfloat16)
     tokens = pltpu.VMEM((span, width), jnp.bfloat16)
@@ -231,7 +224,7 @@
     other = pl.pallas_call(
         functools.partial(other_kernel, chunk=512),
         out_shape=jax.ShapeDtypeStruct((span + 32, width), jnp.bfloat16),
-        in_specs=[smem, smem, hbm, hbm],
+        in_specs=[smem, smem, anywhere, anywhere],
         out_specs=vmem,
         scratch_shapes=[kv, tokens, sems, sem],
         compiler_params=params,
@@ -245,9 +238,9 @@
             jax.ShapeDtypeStruct((span, width), jnp.float32),
             jax.ShapeDtypeStruct((8, span), jnp.float32),
         ],
-        in_specs=[smem, smem, hbm, hbm, hbm, hbm],
+        in_specs=[smem, smem, vmem, vmem, anywhere, anywhere],
         out_specs=[vmem, vmem],
-        scratch_shapes=[kv, tokens, tokens, sems, sem, sem],
+        scratch_shapes=[kv, sems],
         compiler_params=params,
         cost_estimate=cost(keys + span),
         name="own",
@@ -366,13 +359,13 @@
 def project(mixed, weights):
     span, width = mixed[0].shape
     columns = weights[0].shape[1]
-    hbm = pl.BlockSpec(memory_space=pltpu.HBM)
+    anywhere = pl.BlockSpec(memory_space=pl.ANY)
     sent = jax.ShapeDtypeStruct((columns, span), jnp.bfloat16)
     return pl.pallas_call(
         project_kernel,
         out_shape=[sent] * (SIDE - 1) + [jax.ShapeDtypeStruct((columns, span), jnp.float32)],
-        in_specs=[hbm] * (SIDE + len(weights)),
-        out_specs=[hbm] * SIDE,
+        in_specs=[anywhere] * (SIDE + len(weights)),
+        out_specs=[anywhere] * SIDE,
         scratch_shapes=[
             pltpu.VMEM((SIDE, span, width), jnp.bfloat16),
             pltpu.VMEM((SIDE * SIDE, columns, width), jnp.bfloat16),
@@ -437,13 +430,13 @@
     ]
 
 
-def spread(value, along):
-    return [value] + [lax.ppermute(value, "tensor", along(k)) for k in range(1, SIDE)]
+def spread(value):
+    return [value] + [lax.ppermute(value, "tensor", along_x(k)) for k in range(1, SIDE)]
 
 
 def settle(subtotals, along):
     total = subtotals[-1]
-    for k in range(1, SIDE):
+    for k in (3, 1, 2):
         total = total + lax.ppermute(subtotals[k - 1], "tensor", along(k)).astype(jnp.float32)
     return total.astype(jnp.bfloat16)
 
@@ -514,7 +507,7 @@
     )
     mixed = attend(rows, info, query, query_other, own_new, pool_half, pairs)
     w_out = [pieces[0], ahead, back, far_low, far_high]
-    halves = [project(spread(half, along_x), w_out) for half in mixed]
+    halves = [project(spread(half), w_out) for half in mixed]
     pool_after = store(pick, have, gathered, kv_pool)
     kept = after(halves[1][-1], [pool_after])
     first = settle(halves[0], along_y)

time: 125 us -> 124 us (level)
  waiting for transfers between devices: 18.9 us -> 17.4 us
    ppermute x6, waiting for transfers between devices: 3.55 us -> 1.56 us  [settle(): lax.ppermute(subtotals[k - 1], 'tensor', along(k)).astype(jnp.float32)]
    ppermute x6, starting transfers between devices: 7.96 us -> 9.49 us  [settle(): lax.ppermute(subtotals[k - 1], 'tensor', along(k)).astype(jnp.float32)]
  transfers between devices with their start and end apart: 20 -> 20, of which waited for: 9 -> 10; matrix products, arithmetic and copies ran while one was open for 21% -> 21% of each run, Pallas kernels for 28% -> 27%
where the time goes in v2:
time: 124 us; the launch traced here: 123 us
  Pallas kernels  33.4 us (27%)
  starting transfers between devices  25.4 us (20%)
  waiting for transfers between devices  17.4 us (14%)
  between operations  14.4 us (12%)
  other arithmetic  14.1 us (11%)
  local copies, waits for them, and re-layouts  10.6 us (9%)
  matrix products  7.77 us (6%)
    ppermute x6, starting transfers between devices, settle(): lax.ppermute(subtotals[k - 1], 'tensor', along(k)).astype(jnp.float32)  9.49 us
    pallas_call x1, Pallas kernels, attend(): pl.pallas_call(functools.partial(own_kernel, chunk=512), out_shape=[jax.S...  8.57 us
    pallas_call x1, Pallas kernels, attend(): pl.pallas_call(functools.partial(other_kernel, chunk=512), out_shape=jax....  8.27 us
    ppermute x6, starting transfers between devices, spread(): lax.ppermute(value, 'tensor', along_x(k))  7.71 us
    pallas_call x2, Pallas kernels, project(): pl.pallas_call(project_kernel, out_shape=[sent] * (SIDE - 1) + [jax.Shape...  7.55 us
    ppermute x6, waiting for transfers between devices, spread(): lax.ppermute(value, 'tensor', along_x(k))  5.73 us
    dot_general x1, matrix products, local(): jnp.dot(normed, w_query, preferred_element_type=jnp.float32)  4.4 us
    pallas_call x1, Pallas kernels, arrange(): pl.pallas_call(arrange_kernel, out_shape=[jax.ShapeDtypeStruct((n, column...  4.11 us
  transfers between devices with their start and end apart: 20, of which 10 were waited for; matrix products, arithmetic and copies ran while one was open for 21% of the time, Pallas kernels for 27%

profile of v2, /device:TPU:6, one launch (start us, length us, event | category | flops | bytes accessed | tf_op | source)
XLA Modules:
  0.0 123.1 jit_solution(16723008574795570091)
XLA Ops:
  7.3 1.8 %constant_dynamic-slice_fusion.refs_1_ = bf16[8,64,256]{2,1,0:T(8,128)(2,1)} fusion(bf16[8,128,256]{2,1,0:T(8,128)(2,1)} %pool_ref.1, s32[]{:T(128)S(6)} %select_n.31), kind=kLoop, calls=%fused_computation.32 | loop fusion | bytes 524292 | tf_op jit(solution)/shard_map/dynamic_slice | solution.py:469
  9.8 4.1 %arrange.1 = (bf16[4,320,256]{2,1,0:T(8,128)(2,1)}, bf16[6,320,256]{2,1,0:T(8,128)(2,1)}, bf16[6,320,256]{2,1,0:T(8,128)(2,1)}) custom-call(s32[2]{0:T(128)} %after.4.place_ref, bf16[256,5120]{1,0:T(8,128)(2,1)} %w_ref.1), custom_call_target="tpu_custom_call" | custom-call | tf_op jit(solution)/shard_map/arrange/pallas_call | solution.py:298
  13.9 2.3 %collective-permute-start = (bf16[6,320,256]{2,1,0:T(8,128)(2,1)}, bf16[6,320,256]{2,1,0:T(8,128)(2,1)}, u32[]{:S(2)}, u32[]{:S(2)}) collective-permute-start(bf16[6,320,256]{2,1,0:T(8,128)(2,1)} %get-tuple-element.17), channel_id=1, source_target_pairs={{0,4},{1,5},{2,6},{3,7},{4,8},{5,9},{6,10},{7,11},{8,12},{9,13},{1... | collective-permute-start | bytes 2949128 | tf_op jit(solution)/shard_map/ppermute | solution.py:474
  16.2 1.4 %dynamic_slice.14 = s32[1]{0:T(128)} dynamic-slice(s32[16]{0:T(128)} %param.21, s32[]{:T(128)S(6)} %select_n.27), dynamic_slice_sizes={1} | dynamic-slice | bytes 12 | tf_op jit(solution)/shard_map/dynamic_slice | solution.py:479
  18.3 3.6 %fusion = f32[512]{0:T(512)S(1)} fusion(bf16[512,5120]{1,0:T(8,128)(2,1)} %param.13), kind=kLoop, calls=%fused_computation.2 | loop fusion | flops 7863808 | bytes 5244928 | tf_op jit(solution)/shard_map/reduce_sum | solution.py:19
  21.9 3.4 %fusion.3 = f32[512,256]{1,0:T(8,128)S(1)} fusion(bf16[5120,256]{1,0:T(8,128)(2,1)} %param.16, bf16[512,5120]{1,0:T(8,128)(2,1)S(1)} %copy-done.1, f32[5120]{0:T(1024)S(1)} %copy-done.17, f32[512]{0:T(512)S(1)} %add_rsqrt_fusion.2), kind=kOutput, calls=%fused_computation.5 | convolution fusion | flops 1352663040 | bytes 8411136 | tf_op jit(solution)/shard_map/dot_general | solution.py:483
  25.6 1.2 subtract_convert_fusion
  27.2 4.4 %multiply_reduce_fusion = (f32[512,2]{0,1:T(2,128)S(1)}, f32[512,256]{0,1:T(8,128)S(1)}) fusion(bf16[5120,256]{1,0:T(8,128)(2,1)S(1)} %copy-done, bf16[512,5120]{1,0:T(8,128)(2,1)} %param.13, f32[5120]{0:T(1024)} %param.14, f32[512]{0:T(512)S(1)} %add_rsqrt_fusion.2), kind=kOutput, calls=%fused_computation.8 | convolution fusion | flops 1352924160 | bytes 8415232 | tf_op jit(solution)/shard_map/dot_general | solution.py:478
  33.1 1.1 pad_add_fusion.refs_5_.info_ref
  34.3 3.5 %collective-permute-done.refs_1_.refs_5_ = bf16[6,320,256]{2,1,0:T(8,128)(2,1)} collective-permute-done((bf16[6,320,256]{2,1,0:T(8,128)(2,1)}, bf16[6,320,256]{2,1,0:T(8,128)(2,1)}, u32[]{:S(2)}, u32[]{:S(2)}) %collective-permute-start) | collective-permute-done | bytes 983072 | tf_op jit(solution)/shard_map/ppermute | solution.py:474
  37.8 1.3 %collective-permute-done.1.refs_2_.refs_6_ = bf16[6,320,256]{2,1,0:T(8,128)(2,1)} collective-permute-done((bf16[6,320,256]{2,1,0:T(8,128)(2,1)}, bf16[6,320,256]{2,1,0:T(8,128)(2,1)}, u32[]{:S(2)}, u32[]{:S(2)}) %collective-permute-start.1) | collective-permute-done | bytes 983072 | tf_op jit(solution)/shard_map/ppermute | solution.py:475
  39.1 1.7 %collective-permute-start.2 = (bf16[512,256]{1,0:T(8,128)(2,1)}, bf16[512,256]{1,0:T(8,128)(2,1)S(1)}, u32[]{:S(2)}, u32[]{:S(2)}) collective-permute-start(bf16[512,256]{1,0:T(8,128)(2,1)} %after.5.refs_2_.q_ref), channel_id=1, source_target_pairs={{0,1},{1,0},{2,3},{3,2},{4,5},{5,4},{6,7},{7,6},{8,9},{9,8},{10,11... | collective-permute-start | bytes 786440 | tf_op jit(solution)/shard_map/ppermute | solution.py:501
  43.2 2.0 %collective-permute-start.4 = (bf16[2,320,256]{2,1,0:T(8,128)(2,1)S(1)}, bf16[2,320,256]{2,1,0:T(8,128)(2,1)S(1)}, u32[]{:S(2)}, u32[]{:S(2)}) collective-permute-start(bf16[2,320,256]{2,1,0:T(8,128)(2,1)S(1)} %slice.40), channel_id=1, source_target_pairs={{0,12},{1,13},{2,14},{3,15},{4,0},{5,1},{6,2},{7,3},{8,4},{9,5},{1... | collective-permute-start | bytes 983048 | tf_op jit(solution)/shard_map/ppermute | solution.py:500
  45.1 1.3 %fusion.11.refs_4_.rows_ref = s32[48]{0:T(128)} fusion(s32[16,48]{1,0:T(8,128)} %param.23, s32[]{:T(128)S(6)} %select_n.27, s32[16,48]{1,0:T(8,128)} %param.22), kind=kLoop, calls=%fused_computation.40 | loop fusion | flops 96 | bytes 580 | tf_op jit(solution)/shard_map/add | solution.py:488
  50.1 2.5 %collective-permute-done.4.refs_9_.refs_8_ = bf16[2,320,256]{2,1,0:T(8,128)(2,1)S(1)} collective-permute-done((bf16[2,320,256]{2,1,0:T(8,128)(2,1)S(1)}, bf16[2,320,256]{2,1,0:T(8,128)(2,1)S(1)}, u32[]{:S(2)}, u32[]{:S(2)}) %collective-permute-start.4) | collective-permute-done | bytes 327712 | tf_op jit(solution)/shard_map/ppermute | solution.py:500
  52.6 2.4 %all-gather.3.cloned.1.call-done.refs_1_.pool_ref = bf16[128,64,256]{2,1,0:T(8,128)(2,1)} async-done(((bf16[8,64,256]{2,1,0:T(8,128)(2,1)}), bf16[128,64,256]{2,1,0:T(8,128)(2,1)}) %all-gather.3.cloned.1.call-update) | async-done | bytes 4194320 | tf_op jit(solution)/shard_map/all_gather | solution.py:470
  55.0 8.3 %other.1.later_ref = bf16[544,256]{1,0:T(8,128)(2,1)} custom-call(s32[48]{0:T(128)} %fusion.11.refs_4_.rows_ref, s32[2]{0:T(128)} %pad_add_fusion.refs_5_.info_ref, bf16[512,256]{1,0:T(8,128)(2,1)} %copy-done.6, bf16[128,64,256]{2,1,0:T(8,128)(2,1)} %all-gather.3.cloned.1.call-done.refs_1_.pool_ref), custom_call_target="tpu_custom_call" | custom-call | flops 1610612736 | bytes 1572864 | tf_op jit(solution)/shard_map/other/pallas_call | solution.py:224
  63.3 1.8 %collective-permute-start.5 = (bf16[544,256]{1,0:T(8,128)(2,1)}, bf16[544,256]{1,0:T(8,128)(2,1)S(1)}, u32[]{:S(2)}, u32[]{:S(2)}) collective-permute-start(bf16[544,256]{1,0:T(8,128)(2,1)} %other.1.later_ref), channel_id=1, source_target_pairs={{0,1},{1,0},{2,3},{3,2},{4,5},{5,4},{6,7},{7,6},{8,9},{9,8},{10,11... | collective-permute-start | bytes 835592 | tf_op jit(solution)/shard_map/ppermute | solution.py:234
  65.0 8.6 %own.1 = (f32[512,256]{1,0:T(8,128)}, f32[8,512]{1,0:T(8,128)}) custom-call(s32[48]{0:T(128)} %fusion.11.refs_4_.rows_ref, s32[2]{0:T(128)} %pad_add_fusion.refs_5_.info_ref, bf16[512,256]{1,0:T(8,128)(2,1)} %after.5.refs_2_.q_ref, bf16[512,256]{1,0:T(8,128)(2,1)} %after.6.fresh_ref, bf16[128,64,256]{2,1,0:T(8,128)(2,1)} %all-gather.3.cloned.1.call-done.refs_1_.pool_ref, ...), custom_call_target="tpu_custom_call" | custom-call | flops 1879048192 | bytes 1835008 | tf_op jit(solution)/shard_map/own/pallas_call | solution.py:235
  74.4 2.3 %merge.1 = (bf16[256,256]{1,0:T(8,128)(2,1)}, bf16[256,256]{1,0:T(8,128)(2,1)}) custom-call(f32[512,256]{1,0:T(8,128)} %get-tuple-element.19.own_ref, f32[8,512]{1,0:T(8,128)} %get-tuple-element.20.sum_ref, bf16[544,256]{1,0:T(8,128)(2,1)} %copy-done.5), custom_call_target="tpu_custom_call" | custom-call | tf_op jit(solution)/shard_map/merge/pallas_call | solution.py:248
  77.0 2.5 %collective-permute-start.7 = (bf16[256,256]{1,0:T(8,128)(2,1)}, bf16[256,256]{1,0:T(8,128)(2,1)S(1)}, u32[]{:S(2)}, u32[]{:S(2)}) collective-permute-start(bf16[256,256]{1,0:T(8,128)(2,1)} %get-tuple-element.21.refs_0_), channel_id=1, source_target_pairs={{0,8},{1,9},{2,10},{3,11},{4,12},{5,13},{6,14},{7,15},{8,0},{9,1},... | collective-permute-start | bytes 393224 | tf_op jit(solution)/shard_map/ppermute | solution.py:434
  79.5 3.2 %collective-permute-start.12 = (bf16[256,256]{1,0:T(8,128)(2,1)}, bf16[256,256]{1,0:T(8,128)(2,1)S(1)}, u32[]{:S(2)}, u32[]{:S(2)}) collective-permute-start(bf16[256,256]{1,0:T(8,128)(2,1)} %get-tuple-element.27.refs_0_), channel_id=1, source_target_pairs={{0,4},{1,5},{2,6},{3,7},{4,8},{5,9},{6,10},{7,11},{8,12},{9,13},{1... | collective-permute-start | bytes 393224 | tf_op jit(solution)/shard_map/ppermute | solution.py:434
  83.3 1.5 %collective-permute-start.14 = (bf16[256,256]{1,0:T(8,128)(2,1)}, bf16[256,256]{1,0:T(8,128)(2,1)S(1)}, u32[]{:S(2)}, u32[]{:S(2)}) collective-permute-start(bf16[256,256]{1,0:T(8,128)(2,1)} %get-tuple-element.27.refs_0_), channel_id=1, source_target_pairs={{0,12},{1,13},{2,14},{3,15},{4,0},{5,1},{6,2},{7,3},{8,4},{9,5},{1... | collective-permute-start | bytes 393224 | tf_op jit(solution)/shard_map/ppermute | solution.py:434
  85.1 5.0 %collective-permute-done.8.refs_3_ = bf16[256,256]{1,0:T(8,128)(2,1)S(1)} collective-permute-done((bf16[256,256]{1,0:T(8,128)(2,1)}, bf16[256,256]{1,0:T(8,128)(2,1)S(1)}, u32[]{:S(2)}, u32[]{:S(2)}) %collective-permute-start.8) | collective-permute-done | bytes 131104 | tf_op jit(solution)/shard_map/ppermute | solution.py:434
  90.8 3.8 %project.2 = (bf16[320,256]{1,0:T(8,128)(2,1)}, bf16[320,256]{1,0:T(8,128)(2,1)}, bf16[320,256]{1,0:T(8,128)(2,1)}, f32[320,256]{1,0:T(8,128)}) custom-call(bf16[256,256]{1,0:T(8,128)(2,1)} %get-tuple-element.21.refs_0_, bf16[256,256]{1,0:T(8,128)(2,1)} %copy-done.10, bf16[256,256]{1,0:T(8,128)(2,1)} %copy-done.11, bf16[256,256]{1,0:T(8,128)(2,1)} %copy-done.12, ...), custom_call_target="tpu_custom_call" | custom-call | flops 671088640 | bytes 2621440 | tf_op jit(solution)/shard_map/project/pallas_call | solution.py:364
  94.6 2.8 %collective-permute-start.11 = (bf16[320,256]{1,0:T(8,128)(2,1)}, bf16[320,256]{1,0:T(8,128)(2,1)S(1)}, u32[]{:S(2)}, u32[]{:S(2)}) collective-permute-start(bf16[320,256]{1,0:T(8,128)(2,1)} %get-tuple-element.26), channel_id=1, source_target_pairs={{0,2},{1,3},{2,0},{3,1},{4,6},{5,7},{6,4},{7,5},{8,10},{9,11},{10,... | collective-permute-start | bytes 491528 | tf_op jit(solution)/shard_map/ppermute | solution.py:440
  97.4 3.2 %collective-permute-start.9 = (bf16[320,256]{1,0:T(8,128)(2,1)}, bf16[320,256]{1,0:T(8,128)(2,1)S(1)}, u32[]{:S(2)}, u32[]{:S(2)}) collective-permute-start(bf16[320,256]{1,0:T(8,128)(2,1)} %get-tuple-element.24), channel_id=1, source_target_pairs={{0,3},{1,0},{2,1},{3,2},{4,7},{5,4},{6,5},{7,6},{8,11},{9,8},{10,9... | collective-permute-start | bytes 491528 | tf_op jit(solution)/shard_map/ppermute | solution.py:440
  102.0 3.8 %project.3 = (bf16[320,256]{1,0:T(8,128)(2,1)}, bf16[320,256]{1,0:T(8,128)(2,1)}, bf16[320,256]{1,0:T(8,128)(2,1)}, f32[320,256]{1,0:T(8,128)}) custom-call(bf16[256,256]{1,0:T(8,128)(2,1)} %get-tuple-element.27.refs_0_, bf16[256,256]{1,0:T(8,128)(2,1)} %copy-done.7, bf16[256,256]{1,0:T(8,128)(2,1)} %copy-done.8, bf16[256,256]{1,0:T(8,128)(2,1)} %copy-done.9, ...), custom_call_target="tpu_custom_call" | custom-call | flops 671088640 | bytes 2621440 | tf_op jit(solution)/shard_map/project/pallas_call | solution.py:364
  106.7 2.4 %collective-permute-start.15 = (bf16[320,256]{1,0:T(8,128)(2,1)}, bf16[320,256]{1,0:T(8,128)(2,1)S(1)}, u32[]{:S(2)}, u32[]{:S(2)}) collective-permute-start(bf16[320,256]{1,0:T(8,128)(2,1)} %get-tuple-element.29), channel_id=1, source_target_pairs={{0,3},{1,0},{2,1},{3,2},{4,7},{5,4},{6,5},{7,6},{8,11},{9,8},{10,9... | collective-permute-start | bytes 491528 | tf_op jit(solution)/shard_map/ppermute | solution.py:440
  109.2 1.0 add_convert_fusion.1
  110.2 2.6 %store.1.refs_1_ = bf16[8,128,256]{2,1,0:T(8,128)(2,1)} custom-call(s32[8]{0:T(128)} %select_reduce_fusion.refs_6_.pick_ref, s32[8]{0:T(128)} %convert_element_type.55.refs_7_.have_ref, bf16[64,128,256]{2,1,0:T(8,128)(2,1)} %all-gather.5.cloned.1.call-done.fresh_ref, bf16[8,128,256]{2,1,0:T(8,128)(2,1)} %pool_ref.1), custom_call_target="tpu_custom_call" | custom-call | tf_op jit(solution)/shard_map/store/pallas_call | solution.py:411
  113.0 1.4 %collective-permute-done.16 = bf16[320,256]{1,0:T(8,128)(2,1)S(1)} collective-permute-done((bf16[320,256]{1,0:T(8,128)(2,1)}, bf16[320,256]{1,0:T(8,128)(2,1)S(1)}, u32[]{:S(2)}, u32[]{:S(2)}) %collective-permute-start.16) | collective-permute-done | bytes 163872 | tf_op jit(solution)/shard_map/ppermute | solution.py:440
  (94 shorter events, 16.5 us)
Async XLA Ops:
  7.2 20.0 %copy-start = (bf16[5120,256]{1,0:T(8,128)(2,1)S(1)}, bf16[5120,256]{1,0:T(8,128)(2,1)}, u32[]{:S(2)}) copy-start(bf16[5120,256]{1,0:T(8,128)(2,1)} %param.15) | copy-start | bytes 7864324
  7.2 14.7 %copy-start.17 = (f32[5120]{0:T(1024)S(1)}, f32[5120]{0:T(1024)}, u32[]{:S(2)}) copy-start(f32[5120]{0:T(1024)} %param.14) | copy-start | bytes 61444
  7.2 47.8 %all-gather.3.cloned.1.call-start = ((), (), s32[]{:S(2)}) async-start(), calls=%async_computation | async-start | bytes 4456448 | tf_op jit(solution)/shard_map/all_gather | solution.py:470
  9.1 101.1 %all-gather.5.cloned.1.call-start = ((), (), s32[]{:S(2)}) async-start(), calls=%async_computation.1 | async-start | bytes 4456448 | tf_op jit(solution)/shard_map/all_gather | solution.py:505
  13.9 23.9 %collective-permute-start = (bf16[6,320,256]{2,1,0:T(8,128)(2,1)}, bf16[6,320,256]{2,1,0:T(8,128)(2,1)}, u32[]{:S(2)}, u32[]{:S(2)}) collective-permute-start(bf16[6,320,256]{2,1,0:T(8,128)(2,1)} %get-tuple-element.17), channel_id=1, source_target_pairs={{0,4},{1,5},{2,6},{3,7},{4,8},{5,9},{6,10},{7,11},{8,12},{9,13},{1... | collective-permute-start | bytes 2949128 | tf_op jit(solution)/shard_map/ppermute | solution.py:474
  16.2 22.9 %collective-permute-start.1 = (bf16[6,320,256]{2,1,0:T(8,128)(2,1)}, bf16[6,320,256]{2,1,0:T(8,128)(2,1)}, u32[]{:S(2)}, u32[]{:S(2)}) collective-permute-start(bf16[6,320,256]{2,1,0:T(8,128)(2,1)} %get-tuple-element.18), channel_id=1, source_target_pairs={{0,12},{1,13},{2,14},{3,15},{4,0},{5,1},{6,2},{7,3},{8,4},{9,5},{1... | collective-permute-start | bytes 2949128 | tf_op jit(solution)/shard_map/ppermute | solution.py:475
  16.2 5.7 %copy-start.1 = (bf16[512,5120]{1,0:T(8,128)(2,1)S(1)}, bf16[512,5120]{1,0:T(8,128)(2,1)}, u32[]{:S(2)}) copy-start(bf16[512,5120]{1,0:T(8,128)(2,1)} %param.13) | copy-start | bytes 15728644
  21.9 3.6 %copy-start.15 = (f32[128]{0:T(128)S(1)}, f32[128]{0:T(128)}, u32[]{:S(2)}) copy-start(f32[128]{0:T(128)} %param.18) | copy-start | bytes 1540
  27.1 4.5 %copy-start.16 = (f32[128]{0:T(128)S(1)}, f32[128]{0:T(128)}, u32[]{:S(2)}) copy-start(f32[128]{0:T(128)} %param.17) | copy-start | bytes 1540
  27.1 5.5 %copy-start.13 = (s32[16,4]{0,1:T(4,128)S(1)}, s32[16,4]{0,1:T(4,128)}, u32[]{:S(2)}) copy-start(s32[16,4]{0,1:T(4,128)} %param.25) | copy-start | bytes 772
  27.2 5.7 %copy-start.14 = (s32[16,4]{0,1:T(4,128)S(1)}, s32[16,4]{0,1:T(4,128)}, u32[]{:S(2)}) copy-start(s32[16,4]{0,1:T(4,128)} %param.24) | copy-start | bytes 772
  39.1 10.3 %collective-permute-start.2 = (bf16[512,256]{1,0:T(8,128)(2,1)}, bf16[512,256]{1,0:T(8,128)(2,1)S(1)}, u32[]{:S(2)}, u32[]{:S(2)}) collective-permute-start(bf16[512,256]{1,0:T(8,128)(2,1)} %after.5.refs_2_.q_ref), channel_id=1, source_target_pairs={{0,1},{1,0},{2,3},{3,2},{4,5},{5,4},{6,7},{7,6},{8,9},{9,8},{10,11... | collective-permute-start | bytes 786440 | tf_op jit(solution)/shard_map/ppermute | solution.py:501
  41.8 8.1 %collective-permute-start.3 = (bf16[2,320,256]{2,1,0:T(8,128)(2,1)S(1)}, bf16[2,320,256]{2,1,0:T(8,128)(2,1)S(1)}, u32[]{:S(2)}, u32[]{:S(2)}) collective-permute-start(bf16[2,320,256]{2,1,0:T(8,128)(2,1)S(1)} %slice.39), channel_id=1, source_target_pairs={{0,4},{1,5},{2,6},{3,7},{4,8},{5,9},{6,10},{7,11},{8,12},{9,13},{1... | collective-permute-start | bytes 983048 | tf_op jit(solution)/shard_map/ppermute | solution.py:499
  43.2 9.5 %collective-permute-start.4 = (bf16[2,320,256]{2,1,0:T(8,128)(2,1)S(1)}, bf16[2,320,256]{2,1,0:T(8,128)(2,1)S(1)}, u32[]{:S(2)}, u32[]{:S(2)}) collective-permute-start(bf16[2,320,256]{2,1,0:T(8,128)(2,1)S(1)} %slice.40), channel_id=1, source_target_pairs={{0,12},{1,13},{2,14},{3,15},{4,0},{5,1},{6,2},{7,3},{8,4},{9,5},{1... | collective-permute-start | bytes 983048 | tf_op jit(solution)/shard_map/ppermute | solution.py:500
  50.1 4.9 %copy-start.2 = (bf16[2,320,256]{2,1,0:T(8,128)(2,1)}, bf16[2,320,256]{2,1,0:T(8,128)(2,1)S(1)}, u32[]{:S(2)}) copy-start(bf16[2,320,256]{2,1,0:T(8,128)(2,1)S(1)} %collective-permute-done.3.refs_8_.refs_7_) | copy-start | bytes 983044
  52.6 2.4 %copy-start.3 = (bf16[2,320,256]{2,1,0:T(8,128)(2,1)}, bf16[2,320,256]{2,1,0:T(8,128)(2,1)S(1)}, u32[]{:S(2)}) copy-start(bf16[2,320,256]{2,1,0:T(8,128)(2,1)S(1)} %collective-permute-done.4.refs_9_.refs_8_) | copy-start | bytes 983044
  63.3 10.3 %collective-permute-start.5 = (bf16[544,256]{1,0:T(8,128)(2,1)}, bf16[544,256]{1,0:T(8,128)(2,1)S(1)}, u32[]{:S(2)}, u32[]{:S(2)}) collective-permute-start(bf16[544,256]{1,0:T(8,128)(2,1)} %other.1.later_ref), channel_id=1, source_target_pairs={{0,1},{1,0},{2,3},{3,2},{4,5},{5,4},{6,7},{7,6},{8,9},{9,8},{10,11... | collective-permute-start | bytes 835592 | tf_op jit(solution)/shard_map/ppermute | solution.py:234
  76.7 6.6 %collective-permute-start.6 = (bf16[256,256]{1,0:T(8,128)(2,1)}, bf16[256,256]{1,0:T(8,128)(2,1)S(1)}, u32[]{:S(2)}, u32[]{:S(2)}) collective-permute-start(bf16[256,256]{1,0:T(8,128)(2,1)} %get-tuple-element.21.refs_0_), channel_id=1, source_target_pairs={{0,4},{1,5},{2,6},{3,7},{4,8},{5,9},{6,10},{7,11},{8,12},{9,13},{1... | collective-permute-start | bytes 393224 | tf_op jit(solution)/shard_map/ppermute | solution.py:434
  77.0 8.1 %collective-permute-start.7 = (bf16[256,256]{1,0:T(8,128)(2,1)}, bf16[256,256]{1,0:T(8,128)(2,1)S(1)}, u32[]{:S(2)}, u32[]{:S(2)}) collective-permute-start(bf16[256,256]{1,0:T(8,128)(2,1)} %get-tuple-element.21.refs_0_), channel_id=1, source_target_pairs={{0,8},{1,9},{2,10},{3,11},{4,12},{5,13},{6,14},{7,15},{8,0},{9,1},... | collective-permute-start | bytes 393224 | tf_op jit(solution)/shard_map/ppermute | solution.py:434
  79.5 10.6 %collective-permute-start.8 = (bf16[256,256]{1,0:T(8,128)(2,1)}, bf16[256,256]{1,0:T(8,128)(2,1)S(1)}, u32[]{:S(2)}, u32[]{:S(2)}) collective-permute-start(bf16[256,256]{1,0:T(8,128)(2,1)} %get-tuple-element.21.refs_0_), channel_id=1, source_target_pairs={{0,12},{1,13},{2,14},{3,15},{4,0},{5,1},{6,2},{7,3},{8,4},{9,5},{1... | collective-permute-start | bytes 393224 | tf_op jit(solution)/shard_map/ppermute | solution.py:434
  79.5 17.9 %collective-permute-start.12 = (bf16[256,256]{1,0:T(8,128)(2,1)}, bf16[256,256]{1,0:T(8,128)(2,1)S(1)}, u32[]{:S(2)}, u32[]{:S(2)}) collective-permute-start(bf16[256,256]{1,0:T(8,128)(2,1)} %get-tuple-element.27.refs_0_), channel_id=1, source_target_pairs={{0,4},{1,5},{2,6},{3,7},{4,8},{5,9},{6,10},{7,11},{8,12},{9,13},{1... | collective-permute-start | bytes 393224 | tf_op jit(solution)/shard_map/ppermute | solution.py:434
  82.8 17.9 %collective-permute-start.13 = (bf16[256,256]{1,0:T(8,128)(2,1)}, bf16[256,256]{1,0:T(8,128)(2,1)S(1)}, u32[]{:S(2)}, u32[]{:S(2)}) collective-permute-start(bf16[256,256]{1,0:T(8,128)(2,1)} %get-tuple-element.27.refs_0_), channel_id=1, source_target_pairs={{0,8},{1,9},{2,10},{3,11},{4,12},{5,13},{6,14},{7,15},{8,0},{9,1},... | collective-permute-start | bytes 393224 | tf_op jit(solution)/shard_map/ppermute | solution.py:434
  83.3 6.8 %copy-start.10 = (bf16[256,256]{1,0:T(8,128)(2,1)}, bf16[256,256]{1,0:T(8,128)(2,1)S(1)}, u32[]{:S(2)}) copy-start(bf16[256,256]{1,0:T(8,128)(2,1)S(1)} %collective-permute-done.6.refs_1_) | copy-start | bytes 393220
  83.3 17.4 %collective-permute-start.14 = (bf16[256,256]{1,0:T(8,128)(2,1)}, bf16[256,256]{1,0:T(8,128)(2,1)S(1)}, u32[]{:S(2)}, u32[]{:S(2)}) collective-permute-start(bf16[256,256]{1,0:T(8,128)(2,1)} %get-tuple-element.27.refs_0_), channel_id=1, source_target_pairs={{0,12},{1,13},{2,14},{3,15},{4,0},{5,1},{6,2},{7,3},{8,4},{9,5},{1... | collective-permute-start | bytes 393224 | tf_op jit(solution)/shard_map/ppermute | solution.py:434
  85.1 5.0 %copy-start.11 = (bf16[256,256]{1,0:T(8,128)(2,1)}, bf16[256,256]{1,0:T(8,128)(2,1)S(1)}, u32[]{:S(2)}) copy-start(bf16[256,256]{1,0:T(8,128)(2,1)S(1)} %collective-permute-done.7.refs_2_) | copy-start | bytes 393220
  94.6 12.2 %collective-permute-start.11 = (bf16[320,256]{1,0:T(8,128)(2,1)}, bf16[320,256]{1,0:T(8,128)(2,1)S(1)}, u32[]{:S(2)}, u32[]{:S(2)}) collective-permute-start(bf16[320,256]{1,0:T(8,128)(2,1)} %get-tuple-element.26), channel_id=1, source_target_pairs={{0,2},{1,3},{2,0},{3,1},{4,6},{5,7},{6,4},{7,5},{8,10},{9,11},{10,... | collective-permute-start | bytes 491528 | tf_op jit(solution)/shard_map/ppermute | solution.py:440
  97.4 11.8 %collective-permute-start.10 = (bf16[320,256]{1,0:T(8,128)(2,1)}, bf16[320,256]{1,0:T(8,128)(2,1)S(1)}, u32[]{:S(2)}, u32[]{:S(2)}) collective-permute-start(bf16[320,256]{1,0:T(8,128)(2,1)} %get-tuple-element.25), channel_id=1, source_target_pairs={{0,1},{1,2},{2,3},{3,0},{4,5},{5,6},{6,7},{7,4},{8,9},{9,10},{10,1... | collective-permute-start | bytes 491528 | tf_op jit(solution)/shard_map/ppermute | solution.py:440
  97.4 3.2 %copy-start.7 = (bf16[256,256]{1,0:T(8,128)(2,1)}, bf16[256,256]{1,0:T(8,128)(2,1)S(1)}, u32[]{:S(2)}) copy-start(bf16[256,256]{1,0:T(8,128)(2,1)S(1)} %collective-permute-done.12.refs_1_) | copy-start | bytes 393220
  97.4 11.8 %collective-permute-start.9 = (bf16[320,256]{1,0:T(8,128)(2,1)}, bf16[320,256]{1,0:T(8,128)(2,1)S(1)}, u32[]{:S(2)}, u32[]{:S(2)}) collective-permute-start(bf16[320,256]{1,0:T(8,128)(2,1)} %get-tuple-element.24), channel_id=1, source_target_pairs={{0,3},{1,0},{2,1},{3,2},{4,7},{5,4},{6,5},{7,6},{8,11},{9,8},{10,9... | collective-permute-start | bytes 491528 | tf_op jit(solution)/shard_map/ppermute | solution.py:440
  105.7 7.2 %collective-permute-start.17 = (bf16[320,256]{1,0:T(8,128)(2,1)}, bf16[320,256]{1,0:T(8,128)(2,1)S(1)}, u32[]{:S(2)}, u32[]{:S(2)}) collective-permute-start(bf16[320,256]{1,0:T(8,128)(2,1)} %get-tuple-element.31), channel_id=1, source_target_pairs={{0,2},{1,3},{2,0},{3,1},{4,6},{5,7},{6,4},{7,5},{8,10},{9,11},{10,... | collective-permute-start | bytes 491528 | tf_op jit(solution)/shard_map/ppermute | solution.py:440
  105.8 8.6 %collective-permute-start.16 = (bf16[320,256]{1,0:T(8,128)(2,1)}, bf16[320,256]{1,0:T(8,128)(2,1)S(1)}, u32[]{:S(2)}, u32[]{:S(2)}) collective-permute-start(bf16[320,256]{1,0:T(8,128)(2,1)} %get-tuple-element.30), channel_id=1, source_target_pairs={{0,1},{1,2},{2,3},{3,0},{4,5},{5,6},{6,7},{7,4},{8,9},{9,10},{10,1... | collective-permute-start | bytes 491528 | tf_op jit(solution)/shard_map/ppermute | solution.py:440
  106.7 7.7 %collective-permute-start.15 = (bf16[320,256]{1,0:T(8,128)(2,1)}, bf16[320,256]{1,0:T(8,128)(2,1)S(1)}, u32[]{:S(2)}, u32[]{:S(2)}) collective-permute-start(bf16[320,256]{1,0:T(8,128)(2,1)} %get-tuple-element.29), channel_id=1, source_target_pairs={{0,3},{1,0},{2,1},{3,2},{4,7},{5,4},{6,5},{7,6},{8,11},{9,8},{10,9... | collective-permute-start | bytes 491528 | tf_op jit(solution)/shard_map/ppermute | solution.py:440
  (6 other events, 5.0 us)
Sparse Core Ops, SparseCore 0:
  9.9 45.0 all-gather.2
  56.8 41.5 all-gather.4

commit v3 on v2

--- a/solution.py
+++ b/solution.py
@@ -231,7 +231,7 @@
         cost_estimate=cost(keys),
         name="other",
     )(rows, info, query_other, pool_half)
-    arrived = lax.ppermute(other, "tensor", pairs)
+    arrived = in_vmem(lax.ppermute(other, "tensor", pairs))
     own, sums = pl.pallas_call(
         functools.partial(own_kernel, chunk=512),
         out_shape=[
@@ -314,36 +314,32 @@
 
 
 def project_kernel(*refs):
-    mixed, (stay, ahead, back, low, high), outs = refs[:SIDE], refs[SIDE:-10], refs[-10:-6]
-    m_all, w_all, sent, kept, in_sems, out_sems = refs[-6:]
+    mixed, (stay, ahead, back, low, high), outs = refs[:SIDE], refs[SIDE:-9], refs[-9:-5]
+    w_all, sent, kept, in_sems, out_sems = refs[-5:]
 
     def weight(i, j):
         if i == 2:
             return low.at[j] if j < 2 else high.at[j - 2]
         return {0: stay, 1: ahead, 3: back}[i].at[j]
 
-    arrivals = [
-        pltpu.make_async_copy(mixed[i], m_all.at[i], in_sems.at[i]) for i in range(SIDE)
-    ]
+    arrivals = []
     order = [2, 1, 3, 0]
     for j in order:
         for i in range(SIDE):
             n = j * SIDE + i
             arrivals.append(
-                pltpu.make_async_copy(weight(i, j), w_all.at[n], in_sems.at[SIDE + n])
+                pltpu.make_async_copy(weight(i, j), w_all.at[n], in_sems.at[n])
             )
     for copy in arrivals:
         copy.start()
-    for copy in arrivals[:SIDE]:
-        copy.wait()
     results = []
     for step, j in enumerate(order):
-        for copy in arrivals[SIDE * (step + 1):SIDE * (step + 2)]:
+        for copy in arrivals[SIDE * step:SIDE * (step + 1)]:
             copy.wait()
         total = None
         for i in range(SIDE):
             part = lax.dot_general(
-                w_all[j * SIDE + i], m_all[i], (((1,), (1,)), ((), ())),
+                w_all[j * SIDE + i], mixed[i][...], (((1,), (1,)), ((), ())),
                 preferred_element_type=jnp.float32,
             )
             part = part.astype(jnp.bfloat16).astype(jnp.float32)
@@ -364,14 +360,13 @@
     return pl.pallas_call(
         project_kernel,
         out_shape=[sent] * (SIDE - 1) + [jax.ShapeDtypeStruct((columns, span), jnp.float32)],
-        in_specs=[anywhere] * (SIDE + len(weights)),
+        in_specs=[pl.BlockSpec(memory_space=pltpu.VMEM)] * SIDE + [anywhere] * len(weights),
         out_specs=[anywhere] * SIDE,
         scratch_shapes=[
-            pltpu.VMEM((SIDE, span, width), jnp.bfloat16),
             pltpu.VMEM((SIDE * SIDE, columns, width), jnp.bfloat16),
             pltpu.VMEM((SIDE - 1, columns, span), jnp.bfloat16),
             pltpu.VMEM((columns, span), jnp.float32),
-            pltpu.SemaphoreType.DMA((SIDE + SIDE * SIDE,)),
+            pltpu.SemaphoreType.DMA((SIDE * SIDE,)),
             pltpu.SemaphoreType.DMA((SIDE,)),
         ],
         compiler_params=pltpu.CompilerParams(vmem_limit_bytes=VMEM),
@@ -431,7 +426,13 @@
 
 
 def spread(value):
-    return [value] + [lax.ppermute(value, "tensor", along_x(k)) for k in range(1, SIDE)]
+    return [value] + [
+        in_vmem(lax.ppermute(value, "tensor", along_x(k))) for k in range(1, SIDE)
+    ]
+
+
+def in_vmem(value):
+    return pltpu.with_memory_space_constraint(value, pltpu.VMEM)
 
 
 def settle(subtotals, along):

time: 124 us -> 123 us (level)
  local copies, waits for them, and re-layouts: 10.6 us -> 7.95 us
  Pallas kernels: 33.4 us -> 34.8 us
    unnamed x37 -> x23, local copies, waits for them, and re-layouts: 3.09 us -> 0.42 us
    pallas_call x2, Pallas kernels: 7.55 us -> 8.93 us  [project(): pl.pallas_call(project_kernel, out_shape=[sent] * (SIDE - 1) + [jax.Shape...]
  transfers between devices with their start and end apart: 20 -> 20, of which waited for: 10 -> 9; matrix products, arithmetic and copies ran while one was open for 21% -> 21% of each run, Pallas kernels for 27% -> 29%
where the time goes in v3:
time: 123 us; the launch traced here: 122 us
  Pallas kernels  34.8 us (28%)
  starting transfers between devices  26.4 us (21%)
  waiting for transfers between devices  16.4 us (13%)
  between operations  14.4 us (12%)
  other arithmetic  14.1 us (11%)
  local copies, waits for them, and re-layouts  7.95 us (6%)
  matrix products  7.8 us (6%)
    ppermute x6, starting transfers between devices, settle(): lax.ppermute(subtotals[k - 1], 'tensor', along(k)).astype(jnp.float32)  10.6 us
    pallas_call x2, Pallas kernels, project(): pl.pallas_call(project_kernel, out_shape=[sent] * (SIDE - 1) + [jax.Shape...  8.93 us
    pallas_call x1, Pallas kernels, attend(): pl.pallas_call(functools.partial(own_kernel, chunk=512), out_shape=[jax.S...  8.56 us
    pallas_call x1, Pallas kernels, attend(): pl.pallas_call(functools.partial(other_kernel, chunk=512), out_shape=jax....  8.26 us
    ppermute x6, starting transfers between devices, spread(): lax.ppermute(value, 'tensor', along_x(k))  7.82 us
    ppermute x6, waiting for transfers between devices, spread(): lax.ppermute(value, 'tensor', along_x(k))  4.67 us
    dot_general x1, matrix products, local(): jnp.dot(normed, w_query, preferred_element_type=jnp.float32)  4.4 us
    pallas_call x1, Pallas kernels, arrange(): pl.pallas_call(arrange_kernel, out_shape=[jax.ShapeDtypeStruct((n, column...  4.13 us
  transfers between devices with their start and end apart: 20, of which 9 were waited for; matrix products, arithmetic and copies ran while one was open for 21% of the time, Pallas kernels for 29%

profile of v3, /device:TPU:6, one launch (start us, length us, event | category | flops | bytes accessed | tf_op | source)
XLA Modules:
  0.0 121.8 jit_solution(3570251375554347706)
XLA Ops:
  7.3 1.8 %constant_dynamic-slice_fusion.refs_1_ = bf16[8,64,256]{2,1,0:T(8,128)(2,1)} fusion(bf16[8,128,256]{2,1,0:T(8,128)(2,1)} %pool_ref.1, s32[]{:T(128)S(6)} %select_n.31), kind=kLoop, calls=%fused_computation.32 | loop fusion | bytes 524292 | tf_op jit(solution)/shard_map/dynamic_slice | solution.py:470
  9.8 4.1 %arrange.1 = (bf16[4,320,256]{2,1,0:T(8,128)(2,1)}, bf16[6,320,256]{2,1,0:T(8,128)(2,1)}, bf16[6,320,256]{2,1,0:T(8,128)(2,1)}) custom-call(s32[2]{0:T(128)} %after.4.place_ref, bf16[256,5120]{1,0:T(8,128)(2,1)} %w_ref.1), custom_call_target="tpu_custom_call" | custom-call | tf_op jit(solution)/shard_map/arrange/pallas_call | solution.py:298
  13.9 2.3 %collective-permute-start = (bf16[6,320,256]{2,1,0:T(8,128)(2,1)}, bf16[6,320,256]{2,1,0:T(8,128)(2,1)}, u32[]{:S(2)}, u32[]{:S(2)}) collective-permute-start(bf16[6,320,256]{2,1,0:T(8,128)(2,1)} %get-tuple-element.17), channel_id=1, source_target_pairs={{0,4},{1,5},{2,6},{3,7},{4,8},{5,9},{6,10},{7,11},{8,12},{9,13},{1... | collective-permute-start | bytes 2949128 | tf_op jit(solution)/shard_map/ppermute | solution.py:475
  16.2 1.4 %dynamic_slice.14 = s32[1]{0:T(128)} dynamic-slice(s32[16]{0:T(128)} %param.21, s32[]{:T(128)S(6)} %select_n.27), dynamic_slice_sizes={1} | dynamic-slice | bytes 12 | tf_op jit(solution)/shard_map/dynamic_slice | solution.py:480
  18.4 3.6 %fusion = f32[512]{0:T(512)S(1)} fusion(bf16[512,5120]{1,0:T(8,128)(2,1)} %param.13), kind=kLoop, calls=%fused_computation.2 | loop fusion | flops 7863808 | bytes 5244928 | tf_op jit(solution)/shard_map/reduce_sum | solution.py:19
  22.0 3.4 %fusion.3 = f32[512,256]{1,0:T(8,128)S(1)} fusion(bf16[5120,256]{1,0:T(8,128)(2,1)} %param.16, bf16[512,5120]{1,0:T(8,128)(2,1)S(1)} %copy-done.1, f32[5120]{0:T(1024)S(1)} %copy-done.10, f32[512]{0:T(512)S(1)} %add_rsqrt_fusion.2), kind=kOutput, calls=%fused_computation.5 | convolution fusion | flops 1352663040 | bytes 8411136 | tf_op jit(solution)/shard_map/dot_general | solution.py:484
  25.7 1.2 %subtract_convert_fusion = (bf16[512,64]{1,0:T(8,128)(2,1)S(1)}, bf16[512,64]{1,0:T(8,128)(2,1)S(1)}, f32[512,64]{1,0:T(8,128)S(1)}, f32[512,64]{1,0:T(8,128)S(1)}) fusion(f32[512,128]{1,0:T(8,128)S(1)} %multiply_multiply_fusion.1, f32[512]{0:T(512)S(1)} %add_convert_fusion.4, f32[64]{0:T(128)S(1)} %multiply_power_fusion), kind=kLoop, calls=%fused_computation.18 | loop fusion | flops 294912 | bytes 657664 | tf_op jit(solution)/shard_map/convert.1
  27.2 4.4 %multiply_reduce_fusion = (f32[512,2]{0,1:T(2,128)S(1)}, f32[512,256]{0,1:T(8,128)S(1)}) fusion(bf16[5120,256]{1,0:T(8,128)(2,1)S(1)} %copy-done, bf16[512,5120]{1,0:T(8,128)(2,1)} %param.13, f32[5120]{0:T(1024)} %param.14, f32[512]{0:T(512)S(1)} %add_rsqrt_fusion.2), kind=kOutput, calls=%fused_computation.8 | convolution fusion | flops 1352924160 | bytes 8415232 | tf_op jit(solution)/shard_map/dot_general | solution.py:479
  33.1 1.2 pad_add_fusion.refs_5_.info_ref
  34.4 3.4 %collective-permute-done.refs_1_.refs_5_ = bf16[6,320,256]{2,1,0:T(8,128)(2,1)} collective-permute-done((bf16[6,320,256]{2,1,0:T(8,128)(2,1)}, bf16[6,320,256]{2,1,0:T(8,128)(2,1)}, u32[]{:S(2)}, u32[]{:S(2)}) %collective-permute-start) | collective-permute-done | bytes 983072 | tf_op jit(solution)/shard_map/ppermute | solution.py:475
  37.8 1.3 %collective-permute-done.1.refs_2_.refs_6_ = bf16[6,320,256]{2,1,0:T(8,128)(2,1)} collective-permute-done((bf16[6,320,256]{2,1,0:T(8,128)(2,1)}, bf16[6,320,256]{2,1,0:T(8,128)(2,1)}, u32[]{:S(2)}, u32[]{:S(2)}) %collective-permute-start.1) | collective-permute-done | bytes 983072 | tf_op jit(solution)/shard_map/ppermute | solution.py:476
  39.1 1.7 %collective-permute-start.2 = (bf16[512,256]{1,0:T(8,128)(2,1)}, bf16[512,256]{1,0:T(8,128)(2,1)S(1)}, u32[]{:S(2)}, u32[]{:S(2)}) collective-permute-start(bf16[512,256]{1,0:T(8,128)(2,1)} %after.5.refs_2_.q_ref), channel_id=1, source_target_pairs={{0,1},{1,0},{2,3},{3,2},{4,5},{5,4},{6,7},{7,6},{8,9},{9,8},{10,11... | collective-permute-start | bytes 786440 | tf_op jit(solution)/shard_map/ppermute | solution.py:502
  43.2 2.0 %collective-permute-start.4 = (bf16[2,320,256]{2,1,0:T(8,128)(2,1)S(1)}, bf16[2,320,256]{2,1,0:T(8,128)(2,1)S(1)}, u32[]{:S(2)}, u32[]{:S(2)}) collective-permute-start(bf16[2,320,256]{2,1,0:T(8,128)(2,1)S(1)} %slice.40), channel_id=1, source_target_pairs={{0,12},{1,13},{2,14},{3,15},{4,0},{5,1},{6,2},{7,3},{8,4},{9,5},{1... | collective-permute-start | bytes 983048 | tf_op jit(solution)/shard_map/ppermute | solution.py:501
  45.2 1.2 fusion.11.refs_4_.rows_ref
  50.1 2.5 %collective-permute-done.4.refs_9_.refs_8_ = bf16[2,320,256]{2,1,0:T(8,128)(2,1)S(1)} collective-permute-done((bf16[2,320,256]{2,1,0:T(8,128)(2,1)S(1)}, bf16[2,320,256]{2,1,0:T(8,128)(2,1)S(1)}, u32[]{:S(2)}, u32[]{:S(2)}) %collective-permute-start.4) | collective-permute-done | bytes 327712 | tf_op jit(solution)/shard_map/ppermute | solution.py:501
  52.7 2.5 %all-gather.3.cloned.1.call-done.refs_1_.pool_ref = bf16[128,64,256]{2,1,0:T(8,128)(2,1)} async-done(((bf16[8,64,256]{2,1,0:T(8,128)(2,1)}), bf16[128,64,256]{2,1,0:T(8,128)(2,1)}) %all-gather.3.cloned.1.call-update) | async-done | bytes 4194320 | tf_op jit(solution)/shard_map/all_gather | solution.py:471
  55.2 8.3 %other.1.later_ref = bf16[544,256]{1,0:T(8,128)(2,1)} custom-call(s32[48]{0:T(128)} %fusion.11.refs_4_.rows_ref, s32[2]{0:T(128)} %pad_add_fusion.refs_5_.info_ref, bf16[512,256]{1,0:T(8,128)(2,1)} %copy-done.5, bf16[128,64,256]{2,1,0:T(8,128)(2,1)} %all-gather.3.cloned.1.call-done.refs_1_.pool_ref), custom_call_target="tpu_custom_call" | custom-call | flops 1610612736 | bytes 1572864 | tf_op jit(solution)/shard_map/other/pallas_call | solution.py:224
  63.5 1.6 %collective-permute-start.5 = (bf16[544,256]{1,0:T(8,128)(2,1)}, bf16[544,256]{1,0:T(8,128)(2,1)S(1)}, u32[]{:S(2)}, u32[]{:S(2)}) collective-permute-start(bf16[544,256]{1,0:T(8,128)(2,1)} %other.1.later_ref), channel_id=1, source_target_pairs={{0,1},{1,0},{2,3},{3,2},{4,5},{5,4},{6,7},{7,6},{8,9},{9,8},{10,11... | collective-permute-start | bytes 835592 | tf_op jit(solution)/shard_map/ppermute | solution.py:234
  65.0 8.6 %own.1 = (f32[512,256]{1,0:T(8,128)}, f32[8,512]{1,0:T(8,128)}) custom-call(s32[48]{0:T(128)} %fusion.11.refs_4_.rows_ref, s32[2]{0:T(128)} %pad_add_fusion.refs_5_.info_ref, bf16[512,256]{1,0:T(8,128)(2,1)} %after.5.refs_2_.q_ref, bf16[512,256]{1,0:T(8,128)(2,1)} %after.6.fresh_ref, bf16[128,64,256]{2,1,0:T(8,128)(2,1)} %all-gather.3.cloned.1.call-done.refs_1_.pool_ref, ...), custom_call_target="tpu_custom_call" | custom-call | flops 1879048192 | bytes 1835008 | tf_op jit(solution)/shard_map/own/pallas_call | solution.py:235
  73.6 2.3 %merge.1 = (bf16[256,256]{1,0:T(8,128)(2,1)}, bf16[256,256]{1,0:T(8,128)(2,1)}) custom-call(f32[512,256]{1,0:T(8,128)} %get-tuple-element.19.own_ref, f32[8,512]{1,0:T(8,128)} %get-tuple-element.20.sum_ref, bf16[544,256]{1,0:T(8,128)(2,1)S(1)} %collective-permute-done.5.other_ref), custom_call_target="tpu_custom_call" | custom-call | tf_op jit(solution)/shard_map/merge/pallas_call | solution.py:248
  75.9 2.9 %collective-permute-start.7 = (bf16[256,256]{1,0:T(8,128)(2,1)}, bf16[256,256]{1,0:T(8,128)(2,1)S(1)}, u32[]{:S(2)}, u32[]{:S(2)}) collective-permute-start(bf16[256,256]{1,0:T(8,128)(2,1)} %get-tuple-element.21.refs_0_), channel_id=1, source_target_pairs={{0,8},{1,9},{2,10},{3,11},{4,12},{5,13},{6,14},{7,15},{8,0},{9,1},... | collective-permute-start | bytes 393224 | tf_op jit(solution)/shard_map/ppermute | solution.py:430
  78.8 3.2 %collective-permute-start.12 = (bf16[256,256]{1,0:T(8,128)(2,1)}, bf16[256,256]{1,0:T(8,128)(2,1)S(1)}, u32[]{:S(2)}, u32[]{:S(2)}) collective-permute-start(bf16[256,256]{1,0:T(8,128)(2,1)} %get-tuple-element.27.refs_0_), channel_id=1, source_target_pairs={{0,4},{1,5},{2,6},{3,7},{4,8},{5,9},{6,10},{7,11},{8,12},{9,13},{1... | collective-permute-start | bytes 393224 | tf_op jit(solution)/shard_map/ppermute | solution.py:430
  82.5 1.7 %collective-permute-start.14 = (bf16[256,256]{1,0:T(8,128)(2,1)}, bf16[256,256]{1,0:T(8,128)(2,1)S(1)}, u32[]{:S(2)}, u32[]{:S(2)}) collective-permute-start(bf16[256,256]{1,0:T(8,128)(2,1)} %get-tuple-element.27.refs_0_), channel_id=1, source_target_pairs={{0,12},{1,13},{2,14},{3,15},{4,0},{5,1},{6,2},{7,3},{8,4},{9,5},{1... | collective-permute-start | bytes 393224 | tf_op jit(solution)/shard_map/ppermute | solution.py:430
  84.1 4.2 %collective-permute-done.8.refs_3_ = bf16[256,256]{1,0:T(8,128)(2,1)S(1)} collective-permute-done((bf16[256,256]{1,0:T(8,128)(2,1)}, bf16[256,256]{1,0:T(8,128)(2,1)S(1)}, u32[]{:S(2)}, u32[]{:S(2)}) %collective-permute-start.8) | collective-permute-done | bytes 131104 | tf_op jit(solution)/shard_map/ppermute | solution.py:430
  88.4 4.5 %project.2 = (bf16[320,256]{1,0:T(8,128)(2,1)}, bf16[320,256]{1,0:T(8,128)(2,1)}, bf16[320,256]{1,0:T(8,128)(2,1)}, f32[320,256]{1,0:T(8,128)}) custom-call(bf16[256,256]{1,0:T(8,128)(2,1)} %get-tuple-element.21.refs_0_, bf16[256,256]{1,0:T(8,128)(2,1)S(1)} %collective-permute-done.6.refs_1_, bf16[256,256]{1,0:T(8,128)(2,1)S(1)} %collective-permute-done.7.refs_2_, ...), custom_call_target="tpu_custom_call" | custom-call | flops 671088640 | bytes 2621440 | tf_op jit(solution)/shard_map/project/pallas_call | solution.py:360
  92.8 4.0 %collective-permute-start.11 = (bf16[320,256]{1,0:T(8,128)(2,1)}, bf16[320,256]{1,0:T(8,128)(2,1)S(1)}, u32[]{:S(2)}, u32[]{:S(2)}) collective-permute-start(bf16[320,256]{1,0:T(8,128)(2,1)} %get-tuple-element.26), channel_id=1, source_target_pairs={{0,2},{1,3},{2,0},{3,1},{4,6},{5,7},{6,4},{7,5},{8,10},{9,11},{10,... | collective-permute-start | bytes 491528 | tf_op jit(solution)/shard_map/ppermute | solution.py:441
  96.8 3.2 %collective-permute-start.9 = (bf16[320,256]{1,0:T(8,128)(2,1)}, bf16[320,256]{1,0:T(8,128)(2,1)S(1)}, u32[]{:S(2)}, u32[]{:S(2)}) collective-permute-start(bf16[320,256]{1,0:T(8,128)(2,1)} %get-tuple-element.24), channel_id=1, source_target_pairs={{0,3},{1,0},{2,1},{3,2},{4,7},{5,4},{6,5},{7,6},{8,11},{9,8},{10,9... | collective-permute-start | bytes 491528 | tf_op jit(solution)/shard_map/ppermute | solution.py:441
  100.1 4.5 %project.3 = (bf16[320,256]{1,0:T(8,128)(2,1)}, bf16[320,256]{1,0:T(8,128)(2,1)}, bf16[320,256]{1,0:T(8,128)(2,1)}, f32[320,256]{1,0:T(8,128)}) custom-call(bf16[256,256]{1,0:T(8,128)(2,1)} %get-tuple-element.27.refs_0_, bf16[256,256]{1,0:T(8,128)(2,1)S(1)} %collective-permute-done.12.refs_1_, bf16[256,256]{1,0:T(8,128)(2,1)S(1)} %collective-permute-done.13.refs_2_, ...), custom_call_target="tpu_custom_call" | custom-call | flops 671088640 | bytes 2621440 | tf_op jit(solution)/shard_map/project/pallas_call | solution.py:360
  105.5 2.5 %collective-permute-start.15 = (bf16[320,256]{1,0:T(8,128)(2,1)}, bf16[320,256]{1,0:T(8,128)(2,1)S(1)}, u32[]{:S(2)}, u32[]{:S(2)}) collective-permute-start(bf16[320,256]{1,0:T(8,128)(2,1)} %get-tuple-element.29), channel_id=1, source_target_pairs={{0,3},{1,0},{2,1},{3,2},{4,7},{5,4},{6,5},{7,6},{8,11},{9,8},{10,9... | collective-permute-start | bytes 491528 | tf_op jit(solution)/shard_map/ppermute | solution.py:441
  108.0 1.0 add_convert_fusion.1
  109.0 2.6 %store.1.refs_1_ = bf16[8,128,256]{2,1,0:T(8,128)(2,1)} custom-call(s32[8]{0:T(128)} %select_reduce_fusion.refs_6_.pick_ref, s32[8]{0:T(128)} %convert_element_type.55.refs_7_.have_ref, bf16[64,128,256]{2,1,0:T(8,128)(2,1)} %all-gather.5.cloned.1.call-done.fresh_ref, bf16[8,128,256]{2,1,0:T(8,128)(2,1)} %pool_ref.1), custom_call_target="tpu_custom_call" | custom-call | tf_op jit(solution)/shard_map/store/pallas_call | solution.py:406
  111.8 1.4 %collective-permute-done.16 = bf16[320,256]{1,0:T(8,128)(2,1)S(1)} collective-permute-done((bf16[320,256]{1,0:T(8,128)(2,1)}, bf16[320,256]{1,0:T(8,128)(2,1)S(1)}, u32[]{:S(2)}, u32[]{:S(2)}) %collective-permute-start.16) | collective-permute-done | bytes 163872 | tf_op jit(solution)/shard_map/ppermute | solution.py:441
  (80 shorter events, 13.1 us)
Async XLA Ops:
  7.2 20.0 %copy-start = (bf16[5120,256]{1,0:T(8,128)(2,1)S(1)}, bf16[5120,256]{1,0:T(8,128)(2,1)}, u32[]{:S(2)}) copy-start(bf16[5120,256]{1,0:T(8,128)(2,1)} %param.15) | copy-start | bytes 7864324
  7.2 14.8 %copy-start.10 = (f32[5120]{0:T(1024)S(1)}, f32[5120]{0:T(1024)}, u32[]{:S(2)}) copy-start(f32[5120]{0:T(1024)} %param.14) | copy-start | bytes 61444
  7.2 48.0 %all-gather.3.cloned.1.call-start = ((), (), s32[]{:S(2)}) async-start(), calls=%async_computation | async-start | bytes 4456448 | tf_op jit(solution)/shard_map/all_gather | solution.py:471
  9.1 99.9 %all-gather.5.cloned.1.call-start = ((), (), s32[]{:S(2)}) async-start(), calls=%async_computation.1 | async-start | bytes 4456448 | tf_op jit(solution)/shard_map/all_gather | solution.py:506
  13.9 23.9 %collective-permute-start = (bf16[6,320,256]{2,1,0:T(8,128)(2,1)}, bf16[6,320,256]{2,1,0:T(8,128)(2,1)}, u32[]{:S(2)}, u32[]{:S(2)}) collective-permute-start(bf16[6,320,256]{2,1,0:T(8,128)(2,1)} %get-tuple-element.17), channel_id=1, source_target_pairs={{0,4},{1,5},{2,6},{3,7},{4,8},{5,9},{6,10},{7,11},{8,12},{9,13},{1... | collective-permute-start | bytes 2949128 | tf_op jit(solution)/shard_map/ppermute | solution.py:475
  16.2 22.9 %collective-permute-start.1 = (bf16[6,320,256]{2,1,0:T(8,128)(2,1)}, bf16[6,320,256]{2,1,0:T(8,128)(2,1)}, u32[]{:S(2)}, u32[]{:S(2)}) collective-permute-start(bf16[6,320,256]{2,1,0:T(8,128)(2,1)} %get-tuple-element.18), channel_id=1, source_target_pairs={{0,12},{1,13},{2,14},{3,15},{4,0},{5,1},{6,2},{7,3},{8,4},{9,5},{1... | collective-permute-start | bytes 2949128 | tf_op jit(solution)/shard_map/ppermute | solution.py:476
  16.2 5.7 %copy-start.1 = (bf16[512,5120]{1,0:T(8,128)(2,1)S(1)}, bf16[512,5120]{1,0:T(8,128)(2,1)}, u32[]{:S(2)}) copy-start(bf16[512,5120]{1,0:T(8,128)(2,1)} %param.13) | copy-start | bytes 15728644
  22.0 3.6 %copy-start.8 = (f32[128]{0:T(128)S(1)}, f32[128]{0:T(128)}, u32[]{:S(2)}) copy-start(f32[128]{0:T(128)} %param.18) | copy-start | bytes 1540
  25.4 1.6 %copy-start.4 = (f32[512,256]{1,0:T(8,128)}, f32[512,256]{1,0:T(8,128)S(1)}, u32[]{:S(2)}) copy-start(f32[512,256]{1,0:T(8,128)S(1)} %fusion.3) | copy-start | bytes 1572868
  27.2 4.5 %copy-start.9 = (f32[128]{0:T(128)S(1)}, f32[128]{0:T(128)}, u32[]{:S(2)}) copy-start(f32[128]{0:T(128)} %param.17) | copy-start | bytes 1540
  27.2 5.5 %copy-start.6 = (s32[16,4]{0,1:T(4,128)S(1)}, s32[16,4]{0,1:T(4,128)}, u32[]{:S(2)}) copy-start(s32[16,4]{0,1:T(4,128)} %param.25) | copy-start | bytes 772
  27.2 5.7 %copy-start.7 = (s32[16,4]{0,1:T(4,128)S(1)}, s32[16,4]{0,1:T(4,128)}, u32[]{:S(2)}) copy-start(s32[16,4]{0,1:T(4,128)} %param.24) | copy-start | bytes 772
  39.1 10.3 %collective-permute-start.2 = (bf16[512,256]{1,0:T(8,128)(2,1)}, bf16[512,256]{1,0:T(8,128)(2,1)S(1)}, u32[]{:S(2)}, u32[]{:S(2)}) collective-permute-start(bf16[512,256]{1,0:T(8,128)(2,1)} %after.5.refs_2_.q_ref), channel_id=1, source_target_pairs={{0,1},{1,0},{2,3},{3,2},{4,5},{5,4},{6,7},{7,6},{8,9},{9,8},{10,11... | collective-permute-start | bytes 786440 | tf_op jit(solution)/shard_map/ppermute | solution.py:502
  41.8 8.1 %collective-permute-start.3 = (bf16[2,320,256]{2,1,0:T(8,128)(2,1)S(1)}, bf16[2,320,256]{2,1,0:T(8,128)(2,1)S(1)}, u32[]{:S(2)}, u32[]{:S(2)}) collective-permute-start(bf16[2,320,256]{2,1,0:T(8,128)(2,1)S(1)} %slice.39), channel_id=1, source_target_pairs={{0,4},{1,5},{2,6},{3,7},{4,8},{5,9},{6,10},{7,11},{8,12},{9,13},{1... | collective-permute-start | bytes 983048 | tf_op jit(solution)/shard_map/ppermute | solution.py:500
  43.2 9.5 %collective-permute-start.4 = (bf16[2,320,256]{2,1,0:T(8,128)(2,1)S(1)}, bf16[2,320,256]{2,1,0:T(8,128)(2,1)S(1)}, u32[]{:S(2)}, u32[]{:S(2)}) collective-permute-start(bf16[2,320,256]{2,1,0:T(8,128)(2,1)S(1)} %slice.40), channel_id=1, source_target_pairs={{0,12},{1,13},{2,14},{3,15},{4,0},{5,1},{6,2},{7,3},{8,4},{9,5},{1... | collective-permute-start | bytes 983048 | tf_op jit(solution)/shard_map/ppermute | solution.py:501
  49.4 0.7 copy-start.5
  50.1 5.0 %copy-start.2 = (bf16[2,320,256]{2,1,0:T(8,128)(2,1)}, bf16[2,320,256]{2,1,0:T(8,128)(2,1)S(1)}, u32[]{:S(2)}) copy-start(bf16[2,320,256]{2,1,0:T(8,128)(2,1)S(1)} %collective-permute-done.3.refs_8_.refs_7_) | copy-start | bytes 983044
  52.7 2.5 %copy-start.3 = (bf16[2,320,256]{2,1,0:T(8,128)(2,1)}, bf16[2,320,256]{2,1,0:T(8,128)(2,1)S(1)}, u32[]{:S(2)}) copy-start(bf16[2,320,256]{2,1,0:T(8,128)(2,1)S(1)} %collective-permute-done.4.refs_9_.refs_8_) | copy-start | bytes 983044
  63.5 10.1 %collective-permute-start.5 = (bf16[544,256]{1,0:T(8,128)(2,1)}, bf16[544,256]{1,0:T(8,128)(2,1)S(1)}, u32[]{:S(2)}, u32[]{:S(2)}) collective-permute-start(bf16[544,256]{1,0:T(8,128)(2,1)} %other.1.later_ref), channel_id=1, source_target_pairs={{0,1},{1,0},{2,3},{3,2},{4,5},{5,4},{6,7},{7,6},{8,9},{9,8},{10,11... | collective-permute-start | bytes 835592 | tf_op jit(solution)/shard_map/ppermute | solution.py:234
  75.9 6.6 %collective-permute-start.6 = (bf16[256,256]{1,0:T(8,128)(2,1)}, bf16[256,256]{1,0:T(8,128)(2,1)S(1)}, u32[]{:S(2)}, u32[]{:S(2)}) collective-permute-start(bf16[256,256]{1,0:T(8,128)(2,1)} %get-tuple-element.21.refs_0_), channel_id=1, source_target_pairs={{0,4},{1,5},{2,6},{3,7},{4,8},{5,9},{6,10},{7,11},{8,12},{9,13},{1... | collective-permute-start | bytes 393224 | tf_op jit(solution)/shard_map/ppermute | solution.py:430
  75.9 8.2 %collective-permute-start.7 = (bf16[256,256]{1,0:T(8,128)(2,1)}, bf16[256,256]{1,0:T(8,128)(2,1)S(1)}, u32[]{:S(2)}, u32[]{:S(2)}) collective-permute-start(bf16[256,256]{1,0:T(8,128)(2,1)} %get-tuple-element.21.refs_0_), channel_id=1, source_target_pairs={{0,8},{1,9},{2,10},{3,11},{4,12},{5,13},{6,14},{7,15},{8,0},{9,1},... | collective-permute-start | bytes 393224 | tf_op jit(solution)/shard_map/ppermute | solution.py:430
  78.8 9.6 %collective-permute-start.8 = (bf16[256,256]{1,0:T(8,128)(2,1)}, bf16[256,256]{1,0:T(8,128)(2,1)S(1)}, u32[]{:S(2)}, u32[]{:S(2)}) collective-permute-start(bf16[256,256]{1,0:T(8,128)(2,1)} %get-tuple-element.21.refs_0_), channel_id=1, source_target_pairs={{0,12},{1,13},{2,14},{3,15},{4,0},{5,1},{6,2},{7,3},{8,4},{9,5},{1... | collective-permute-start | bytes 393224 | tf_op jit(solution)/shard_map/ppermute | solution.py:430
  78.8 18.0 %collective-permute-start.12 = (bf16[256,256]{1,0:T(8,128)(2,1)}, bf16[256,256]{1,0:T(8,128)(2,1)S(1)}, u32[]{:S(2)}, u32[]{:S(2)}) collective-permute-start(bf16[256,256]{1,0:T(8,128)(2,1)} %get-tuple-element.27.refs_0_), channel_id=1, source_target_pairs={{0,4},{1,5},{2,6},{3,7},{4,8},{5,9},{6,10},{7,11},{8,12},{9,13},{1... | collective-permute-start | bytes 393224 | tf_op jit(solution)/shard_map/ppermute | solution.py:430
  82.0 18.0 %collective-permute-start.13 = (bf16[256,256]{1,0:T(8,128)(2,1)}, bf16[256,256]{1,0:T(8,128)(2,1)S(1)}, u32[]{:S(2)}, u32[]{:S(2)}) collective-permute-start(bf16[256,256]{1,0:T(8,128)(2,1)} %get-tuple-element.27.refs_0_), channel_id=1, source_target_pairs={{0,8},{1,9},{2,10},{3,11},{4,12},{5,13},{6,14},{7,15},{8,0},{9,1},... | collective-permute-start | bytes 393224 | tf_op jit(solution)/shard_map/ppermute | solution.py:430
  82.5 17.6 %collective-permute-start.14 = (bf16[256,256]{1,0:T(8,128)(2,1)}, bf16[256,256]{1,0:T(8,128)(2,1)S(1)}, u32[]{:S(2)}, u32[]{:S(2)}) collective-permute-start(bf16[256,256]{1,0:T(8,128)(2,1)} %get-tuple-element.27.refs_0_), channel_id=1, source_target_pairs={{0,12},{1,13},{2,14},{3,15},{4,0},{5,1},{6,2},{7,3},{8,4},{9,5},{1... | collective-permute-start | bytes 393224 | tf_op jit(solution)/shard_map/ppermute | solution.py:430
  92.8 12.7 %collective-permute-start.11 = (bf16[320,256]{1,0:T(8,128)(2,1)}, bf16[320,256]{1,0:T(8,128)(2,1)S(1)}, u32[]{:S(2)}, u32[]{:S(2)}) collective-permute-start(bf16[320,256]{1,0:T(8,128)(2,1)} %get-tuple-element.26), channel_id=1, source_target_pairs={{0,2},{1,3},{2,0},{3,1},{4,6},{5,7},{6,4},{7,5},{8,10},{9,11},{10,... | collective-permute-start | bytes 491528 | tf_op jit(solution)/shard_map/ppermute | solution.py:441
  96.8 11.1 %collective-permute-start.10 = (bf16[320,256]{1,0:T(8,128)(2,1)}, bf16[320,256]{1,0:T(8,128)(2,1)S(1)}, u32[]{:S(2)}, u32[]{:S(2)}) collective-permute-start(bf16[320,256]{1,0:T(8,128)(2,1)} %get-tuple-element.25), channel_id=1, source_target_pairs={{0,1},{1,2},{2,3},{3,0},{4,5},{5,6},{6,7},{7,4},{8,9},{9,10},{10,1... | collective-permute-start | bytes 491528 | tf_op jit(solution)/shard_map/ppermute | solution.py:441
  96.8 11.1 %collective-permute-start.9 = (bf16[320,256]{1,0:T(8,128)(2,1)}, bf16[320,256]{1,0:T(8,128)(2,1)S(1)}, u32[]{:S(2)}, u32[]{:S(2)}) collective-permute-start(bf16[320,256]{1,0:T(8,128)(2,1)} %get-tuple-element.24), channel_id=1, source_target_pairs={{0,3},{1,0},{2,1},{3,2},{4,7},{5,4},{6,5},{7,6},{8,11},{9,8},{10,9... | collective-permute-start | bytes 491528 | tf_op jit(solution)/shard_map/ppermute | solution.py:441
  104.5 7.2 %collective-permute-start.17 = (bf16[320,256]{1,0:T(8,128)(2,1)}, bf16[320,256]{1,0:T(8,128)(2,1)S(1)}, u32[]{:S(2)}, u32[]{:S(2)}) collective-permute-start(bf16[320,256]{1,0:T(8,128)(2,1)} %get-tuple-element.31), channel_id=1, source_target_pairs={{0,2},{1,3},{2,0},{3,1},{4,6},{5,7},{6,4},{7,5},{8,10},{9,11},{10,... | collective-permute-start | bytes 491528 | tf_op jit(solution)/shard_map/ppermute | solution.py:441
  104.6 8.6 %collective-permute-start.16 = (bf16[320,256]{1,0:T(8,128)(2,1)}, bf16[320,256]{1,0:T(8,128)(2,1)S(1)}, u32[]{:S(2)}, u32[]{:S(2)}) collective-permute-start(bf16[320,256]{1,0:T(8,128)(2,1)} %get-tuple-element.30), channel_id=1, source_target_pairs={{0,1},{1,2},{2,3},{3,0},{4,5},{5,6},{6,7},{7,4},{8,9},{9,10},{10,1... | collective-permute-start | bytes 491528 | tf_op jit(solution)/shard_map/ppermute | solution.py:441
  105.5 7.7 %collective-permute-start.15 = (bf16[320,256]{1,0:T(8,128)(2,1)}, bf16[320,256]{1,0:T(8,128)(2,1)S(1)}, u32[]{:S(2)}, u32[]{:S(2)}) collective-permute-start(bf16[320,256]{1,0:T(8,128)(2,1)} %get-tuple-element.29), channel_id=1, source_target_pairs={{0,3},{1,0},{2,1},{3,2},{4,7},{5,4},{6,5},{7,6},{8,11},{9,8},{10,9... | collective-permute-start | bytes 491528 | tf_op jit(solution)/shard_map/ppermute | solution.py:441
Sparse Core Ops, SparseCore 0:
  9.9 45.2 all-gather.2
  57.0 41.3 all-gather.4

commit v4 on v3

--- a/solution.py
+++ b/solution.py
@@ -314,14 +314,17 @@
 
 
 def project_kernel(*refs):
-    mixed, (stay, ahead, back, low, high), outs = refs[:SIDE], refs[SIDE:-9], refs[-9:-5]
-    w_all, sent, kept, in_sems, out_sems = refs[-5:]
+    mixed, (stay, ahead, back, low, high), outs = refs[:SIDE], refs[SIDE:-10], refs[-10:-6]
+    here, w_all, sent, kept, in_sems, out_sems = refs[-6:]
 
     def weight(i, j):
         if i == 2:
             return low.at[j] if j < 2 else high.at[j - 2]
         return {0: stay, 1: ahead, 3: back}[i].at[j]
 
+    own = pltpu.make_async_copy(mixed[0], here, in_sems.at[SIDE * SIDE])
+    own.start()
+    mixed = (here, *mixed[1:])
     arrivals = []
     order = [2, 1, 3, 0]
     for j in order:
@@ -332,6 +335,7 @@
             )
     for copy in arrivals:
         copy.start()
+    own.wait()
     results = []
     for step, j in enumerate(order):
         for copy in arrivals[SIDE * step:SIDE * (step + 1)]:
@@ -356,17 +360,19 @@
     span, width = mixed[0].shape
     columns = weights[0].shape[1]
     anywhere = pl.BlockSpec(memory_space=pl.ANY)
+    vmem = pl.BlockSpec(memory_space=pltpu.VMEM)
     sent = jax.ShapeDtypeStruct((columns, span), jnp.bfloat16)
     return pl.pallas_call(
         project_kernel,
         out_shape=[sent] * (SIDE - 1) + [jax.ShapeDtypeStruct((columns, span), jnp.float32)],
-        in_specs=[pl.BlockSpec(memory_space=pltpu.VMEM)] * SIDE + [anywhere] * len(weights),
+        in_specs=[anywhere] + [vmem] * (SIDE - 1) + [anywhere] * len(weights),
         out_specs=[anywhere] * SIDE,
         scratch_shapes=[
+            pltpu.VMEM((span, width), jnp.bfloat16),
             pltpu.VMEM((SIDE * SIDE, columns, width), jnp.bfloat16),
             pltpu.VMEM((SIDE - 1, columns, span), jnp.bfloat16),
             pltpu.VMEM((columns, span), jnp.float32),
-            pltpu.SemaphoreType.DMA((SIDE * SIDE,)),
+            pltpu.SemaphoreType.DMA((SIDE * SIDE + 1,)),
             pltpu.SemaphoreType.DMA((SIDE,)),
         ],
         compiler_params=pltpu.CompilerParams(vmem_limit_bytes=VMEM),

time: 123 us -> 121 us (0.984)
  Pallas kernels: 34.8 us -> 33.1 us
    pallas_call x2, Pallas kernels: 8.93 us -> 7.28 us  [project(): pl.pallas_call(project_kernel, out_shape=[sent] * (SIDE - 1) + [jax.Shape...]
  transfers between devices with their start and end apart: 20 -> 20, of which waited for: 9 -> 9; matrix products, arithmetic and copies ran while one was open for 21% -> 22% of each run, Pallas kernels for 29% -> 28%
where the time goes in v4:
time: 121 us; the launch traced here: 120 us
  Pallas kernels  33.1 us (27%)
  starting transfers between devices  26.5 us (22%)
  waiting for transfers between devices  16.4 us (14%)
  between operations  14.4 us (12%)
  other arithmetic  14.1 us (12%)
  local copies, waits for them, and re-layouts  7.95 us (7%)
  matrix products  7.8 us (6%)
    ppermute x6, starting transfers between devices, settle(): lax.ppermute(subtotals[k - 1], 'tensor', along(k)).astype(jnp.float32)  10.6 us
    pallas_call x1, Pallas kernels, attend(): pl.pallas_call(functools.partial(own_kernel, chunk=512), out_shape=[jax.S...  8.55 us
    pallas_call x1, Pallas kernels, attend(): pl.pallas_call(functools.partial(other_kernel, chunk=512), out_shape=jax....  8.25 us
    ppermute x6, starting transfers between devices, spread(): lax.ppermute(value, 'tensor', along_x(k))  7.88 us
    pallas_call x2, Pallas kernels, project(): pl.pallas_call(project_kernel, out_shape=[sent] * (SIDE - 1) + [jax.Shape...  7.28 us
    ppermute x6, waiting for transfers between devices, spread(): lax.ppermute(value, 'tensor', along_x(k))  4.64 us
    dot_general x1, matrix products, local(): jnp.dot(normed, w_query, preferred_element_type=jnp.float32)  4.4 us
    pallas_call x1, Pallas kernels, arrange(): pl.pallas_call(arrange_kernel, out_shape=[jax.ShapeDtypeStruct((n, column...  4.13 us
  transfers between devices with their start and end apart: 20, of which 9 were waited for; matrix products, arithmetic and copies ran while one was open for 22% of the time, Pallas kernels for 28%

profile of v4, /device:TPU:6, one launch (start us, length us, event | category | flops | bytes accessed | tf_op | source)
XLA Modules:
  0.0 120.2 jit_solution(6260801483659429815)
XLA Ops:
  7.3 1.8 %constant_dynamic-slice_fusion.refs_1_ = bf16[8,64,256]{2,1,0:T(8,128)(2,1)} fusion(bf16[8,128,256]{2,1,0:T(8,128)(2,1)} %pool_ref.1, s32[]{:T(128)S(6)} %select_n.31), kind=kLoop, calls=%fused_computation.32 | loop fusion | bytes 524292 | tf_op jit(solution)/shard_map/dynamic_slice | solution.py:476
  9.8 4.1 %arrange.1 = (bf16[4,320,256]{2,1,0:T(8,128)(2,1)}, bf16[6,320,256]{2,1,0:T(8,128)(2,1)}, bf16[6,320,256]{2,1,0:T(8,128)(2,1)}) custom-call(s32[2]{0:T(128)} %after.4.place_ref, bf16[256,5120]{1,0:T(8,128)(2,1)} %w_ref.1), custom_call_target="tpu_custom_call" | custom-call | tf_op jit(solution)/shard_map/arrange/pallas_call | solution.py:298
  13.9 2.3 %collective-permute-start = (bf16[6,320,256]{2,1,0:T(8,128)(2,1)}, bf16[6,320,256]{2,1,0:T(8,128)(2,1)}, u32[]{:S(2)}, u32[]{:S(2)}) collective-permute-start(bf16[6,320,256]{2,1,0:T(8,128)(2,1)} %get-tuple-element.17), channel_id=1, source_target_pairs={{0,4},{1,5},{2,6},{3,7},{4,8},{5,9},{6,10},{7,11},{8,12},{9,13},{1... | collective-permute-start | bytes 2949128 | tf_op jit(solution)/shard_map/ppermute | solution.py:481
  16.2 1.4 %dynamic_slice.14 = s32[1]{0:T(128)} dynamic-slice(s32[16]{0:T(128)} %param.21, s32[]{:T(128)S(6)} %select_n.27), dynamic_slice_sizes={1} | dynamic-slice | bytes 12 | tf_op jit(solution)/shard_map/dynamic_slice | solution.py:486
  18.4 3.6 %fusion = f32[512]{0:T(512)S(1)} fusion(bf16[512,5120]{1,0:T(8,128)(2,1)} %param.13), kind=kLoop, calls=%fused_computation.2 | loop fusion | flops 7863808 | bytes 5244928 | tf_op jit(solution)/shard_map/reduce_sum | solution.py:19
  22.0 3.4 %fusion.3 = f32[512,256]{1,0:T(8,128)S(1)} fusion(bf16[5120,256]{1,0:T(8,128)(2,1)} %param.16, bf16[512,5120]{1,0:T(8,128)(2,1)S(1)} %copy-done.1, f32[5120]{0:T(1024)S(1)} %copy-done.10, f32[512]{0:T(512)S(1)} %add_rsqrt_fusion.2), kind=kOutput, calls=%fused_computation.5 | convolution fusion | flops 1352663040 | bytes 8411136 | tf_op jit(solution)/shard_map/dot_general | solution.py:490
  25.7 1.2 %subtract_convert_fusion = (bf16[512,64]{1,0:T(8,128)(2,1)S(1)}, bf16[512,64]{1,0:T(8,128)(2,1)S(1)}, f32[512,64]{1,0:T(8,128)S(1)}, f32[512,64]{1,0:T(8,128)S(1)}) fusion(f32[512,128]{1,0:T(8,128)S(1)} %multiply_multiply_fusion.1, f32[512]{0:T(512)S(1)} %add_convert_fusion.4, f32[64]{0:T(128)S(1)} %multiply_power_fusion), kind=kLoop, calls=%fused_computation.18 | loop fusion | flops 294912 | bytes 657664 | tf_op jit(solution)/shard_map/convert.1
  27.2 4.4 %multiply_reduce_fusion = (f32[512,2]{0,1:T(2,128)S(1)}, f32[512,256]{0,1:T(8,128)S(1)}) fusion(bf16[5120,256]{1,0:T(8,128)(2,1)S(1)} %copy-done, bf16[512,5120]{1,0:T(8,128)(2,1)} %param.13, f32[5120]{0:T(1024)} %param.14, f32[512]{0:T(512)S(1)} %add_rsqrt_fusion.2), kind=kOutput, calls=%fused_computation.8 | convolution fusion | flops 1352924160 | bytes 8415232 | tf_op jit(solution)/shard_map/dot_general | solution.py:485
  33.1 1.2 pad_add_fusion.refs_5_.info_ref
  34.4 3.4 %collective-permute-done.refs_1_.refs_5_ = bf16[6,320,256]{2,1,0:T(8,128)(2,1)} collective-permute-done((bf16[6,320,256]{2,1,0:T(8,128)(2,1)}, bf16[6,320,256]{2,1,0:T(8,128)(2,1)}, u32[]{:S(2)}, u32[]{:S(2)}) %collective-permute-start) | collective-permute-done | bytes 983072 | tf_op jit(solution)/shard_map/ppermute | solution.py:481
  37.8 1.3 %collective-permute-done.1.refs_2_.refs_6_ = bf16[6,320,256]{2,1,0:T(8,128)(2,1)} collective-permute-done((bf16[6,320,256]{2,1,0:T(8,128)(2,1)}, bf16[6,320,256]{2,1,0:T(8,128)(2,1)}, u32[]{:S(2)}, u32[]{:S(2)}) %collective-permute-start.1) | collective-permute-done | bytes 983072 | tf_op jit(solution)/shard_map/ppermute | solution.py:482
  39.1 1.7 %collective-permute-start.2 = (bf16[512,256]{1,0:T(8,128)(2,1)}, bf16[512,256]{1,0:T(8,128)(2,1)S(1)}, u32[]{:S(2)}, u32[]{:S(2)}) collective-permute-start(bf16[512,256]{1,0:T(8,128)(2,1)} %after.5.refs_2_.q_ref), channel_id=1, source_target_pairs={{0,1},{1,0},{2,3},{3,2},{4,5},{5,4},{6,7},{7,6},{8,9},{9,8},{10,11... | collective-permute-start | bytes 786440 | tf_op jit(solution)/shard_map/ppermute | solution.py:508
  43.2 2.0 %collective-permute-start.4 = (bf16[2,320,256]{2,1,0:T(8,128)(2,1)S(1)}, bf16[2,320,256]{2,1,0:T(8,128)(2,1)S(1)}, u32[]{:S(2)}, u32[]{:S(2)}) collective-permute-start(bf16[2,320,256]{2,1,0:T(8,128)(2,1)S(1)} %slice.40), channel_id=1, source_target_pairs={{0,12},{1,13},{2,14},{3,15},{4,0},{5,1},{6,2},{7,3},{8,4},{9,5},{1... | collective-permute-start | bytes 983048 | tf_op jit(solution)/shard_map/ppermute | solution.py:507
  45.2 1.2 fusion.11.refs_4_.rows_ref
  50.1 2.5 %collective-permute-done.4.refs_9_.refs_8_ = bf16[2,320,256]{2,1,0:T(8,128)(2,1)S(1)} collective-permute-done((bf16[2,320,256]{2,1,0:T(8,128)(2,1)S(1)}, bf16[2,320,256]{2,1,0:T(8,128)(2,1)S(1)}, u32[]{:S(2)}, u32[]{:S(2)}) %collective-permute-start.4) | collective-permute-done | bytes 327712 | tf_op jit(solution)/shard_map/ppermute | solution.py:507
  52.7 2.5 %all-gather.3.cloned.1.call-done.refs_1_.pool_ref = bf16[128,64,256]{2,1,0:T(8,128)(2,1)} async-done(((bf16[8,64,256]{2,1,0:T(8,128)(2,1)}), bf16[128,64,256]{2,1,0:T(8,128)(2,1)}) %all-gather.3.cloned.1.call-update) | async-done | bytes 4194320 | tf_op jit(solution)/shard_map/all_gather | solution.py:477
  55.2 8.3 %other.1.later_ref = bf16[544,256]{1,0:T(8,128)(2,1)} custom-call(s32[48]{0:T(128)} %fusion.11.refs_4_.rows_ref, s32[2]{0:T(128)} %pad_add_fusion.refs_5_.info_ref, bf16[512,256]{1,0:T(8,128)(2,1)} %copy-done.5, bf16[128,64,256]{2,1,0:T(8,128)(2,1)} %all-gather.3.cloned.1.call-done.refs_1_.pool_ref), custom_call_target="tpu_custom_call" | custom-call | flops 1610612736 | bytes 1572864 | tf_op jit(solution)/shard_map/other/pallas_call | solution.py:224
  63.5 1.6 %collective-permute-start.5 = (bf16[544,256]{1,0:T(8,128)(2,1)}, bf16[544,256]{1,0:T(8,128)(2,1)S(1)}, u32[]{:S(2)}, u32[]{:S(2)}) collective-permute-start(bf16[544,256]{1,0:T(8,128)(2,1)} %other.1.later_ref), channel_id=1, source_target_pairs={{0,1},{1,0},{2,3},{3,2},{4,5},{5,4},{6,7},{7,6},{8,9},{9,8},{10,11... | collective-permute-start | bytes 835592 | tf_op jit(solution)/shard_map/ppermute | solution.py:234
  65.0 8.5 %own.1 = (f32[512,256]{1,0:T(8,128)}, f32[8,512]{1,0:T(8,128)}) custom-call(s32[48]{0:T(128)} %fusion.11.refs_4_.rows_ref, s32[2]{0:T(128)} %pad_add_fusion.refs_5_.info_ref, bf16[512,256]{1,0:T(8,128)(2,1)} %after.5.refs_2_.q_ref, bf16[512,256]{1,0:T(8,128)(2,1)} %after.6.fresh_ref, bf16[128,64,256]{2,1,0:T(8,128)(2,1)} %all-gather.3.cloned.1.call-done.refs_1_.pool_ref, ...), custom_call_target="tpu_custom_call" | custom-call | flops 1879048192 | bytes 1835008 | tf_op jit(solution)/shard_map/own/pallas_call | solution.py:235
  73.6 2.3 %merge.1 = (bf16[256,256]{1,0:T(8,128)(2,1)}, bf16[256,256]{1,0:T(8,128)(2,1)}) custom-call(f32[512,256]{1,0:T(8,128)} %get-tuple-element.19.own_ref, f32[8,512]{1,0:T(8,128)} %get-tuple-element.20.sum_ref, bf16[544,256]{1,0:T(8,128)(2,1)S(1)} %collective-permute-done.5.other_ref), custom_call_target="tpu_custom_call" | custom-call | tf_op jit(solution)/shard_map/merge/pallas_call | solution.py:248
  75.9 2.9 %collective-permute-start.7 = (bf16[256,256]{1,0:T(8,128)(2,1)}, bf16[256,256]{1,0:T(8,128)(2,1)S(1)}, u32[]{:S(2)}, u32[]{:S(2)}) collective-permute-start(bf16[256,256]{1,0:T(8,128)(2,1)} %get-tuple-element.21.refs_0_), channel_id=1, source_target_pairs={{0,8},{1,9},{2,10},{3,11},{4,12},{5,13},{6,14},{7,15},{8,0},{9,1},... | collective-permute-start | bytes 393224 | tf_op jit(solution)/shard_map/ppermute | solution.py:436
  78.8 3.2 %collective-permute-start.12 = (bf16[256,256]{1,0:T(8,128)(2,1)}, bf16[256,256]{1,0:T(8,128)(2,1)S(1)}, u32[]{:S(2)}, u32[]{:S(2)}) collective-permute-start(bf16[256,256]{1,0:T(8,128)(2,1)} %get-tuple-element.27.refs_0_), channel_id=1, source_target_pairs={{0,4},{1,5},{2,6},{3,7},{4,8},{5,9},{6,10},{7,11},{8,12},{9,13},{1... | collective-permute-start | bytes 393224 | tf_op jit(solution)/shard_map/ppermute | solution.py:436
  82.5 1.7 %collective-permute-start.14 = (bf16[256,256]{1,0:T(8,128)(2,1)}, bf16[256,256]{1,0:T(8,128)(2,1)S(1)}, u32[]{:S(2)}, u32[]{:S(2)}) collective-permute-start(bf16[256,256]{1,0:T(8,128)(2,1)} %get-tuple-element.27.refs_0_), channel_id=1, source_target_pairs={{0,12},{1,13},{2,14},{3,15},{4,0},{5,1},{6,2},{7,3},{8,4},{9,5},{1... | collective-permute-start | bytes 393224 | tf_op jit(solution)/shard_map/ppermute | solution.py:436
  84.2 4.2 %collective-permute-done.8.refs_3_ = bf16[256,256]{1,0:T(8,128)(2,1)S(1)} collective-permute-done((bf16[256,256]{1,0:T(8,128)(2,1)}, bf16[256,256]{1,0:T(8,128)(2,1)S(1)}, u32[]{:S(2)}, u32[]{:S(2)}) %collective-permute-start.8) | collective-permute-done | bytes 131104 | tf_op jit(solution)/shard_map/ppermute | solution.py:436
  88.4 3.6 %project.2 = (bf16[320,256]{1,0:T(8,128)(2,1)}, bf16[320,256]{1,0:T(8,128)(2,1)}, bf16[320,256]{1,0:T(8,128)(2,1)}, f32[320,256]{1,0:T(8,128)}) custom-call(bf16[256,256]{1,0:T(8,128)(2,1)} %get-tuple-element.21.refs_0_, bf16[256,256]{1,0:T(8,128)(2,1)S(1)} %collective-permute-done.6.refs_1_, bf16[256,256]{1,0:T(8,128)(2,1)S(1)} %collective-permute-done.7.refs_2_, ...), custom_call_target="tpu_custom_call" | custom-call | flops 671088640 | bytes 2621440 | tf_op jit(solution)/shard_map/project/pallas_call | solution.py:365
  92.0 3.9 %collective-permute-start.11 = (bf16[320,256]{1,0:T(8,128)(2,1)}, bf16[320,256]{1,0:T(8,128)(2,1)S(1)}, u32[]{:S(2)}, u32[]{:S(2)}) collective-permute-start(bf16[320,256]{1,0:T(8,128)(2,1)} %get-tuple-element.26), channel_id=1, source_target_pairs={{0,2},{1,3},{2,0},{3,1},{4,6},{5,7},{6,4},{7,5},{8,10},{9,11},{10,... | collective-permute-start | bytes 491528 | tf_op jit(solution)/shard_map/ppermute | solution.py:447
  96.0 3.2 %collective-permute-start.9 = (bf16[320,256]{1,0:T(8,128)(2,1)}, bf16[320,256]{1,0:T(8,128)(2,1)S(1)}, u32[]{:S(2)}, u32[]{:S(2)}) collective-permute-start(bf16[320,256]{1,0:T(8,128)(2,1)} %get-tuple-element.24), channel_id=1, source_target_pairs={{0,3},{1,0},{2,1},{3,2},{4,7},{5,4},{6,5},{7,6},{8,11},{9,8},{10,9... | collective-permute-start | bytes 491528 | tf_op jit(solution)/shard_map/ppermute | solution.py:447
  99.2 3.6 %project.3 = (bf16[320,256]{1,0:T(8,128)(2,1)}, bf16[320,256]{1,0:T(8,128)(2,1)}, bf16[320,256]{1,0:T(8,128)(2,1)}, f32[320,256]{1,0:T(8,128)}) custom-call(bf16[256,256]{1,0:T(8,128)(2,1)} %get-tuple-element.27.refs_0_, bf16[256,256]{1,0:T(8,128)(2,1)S(1)} %collective-permute-done.12.refs_1_, bf16[256,256]{1,0:T(8,128)(2,1)S(1)} %collective-permute-done.13.refs_2_, ...), custom_call_target="tpu_custom_call" | custom-call | flops 671088640 | bytes 2621440 | tf_op jit(solution)/shard_map/project/pallas_call | solution.py:365
  103.8 2.5 %collective-permute-start.15 = (bf16[320,256]{1,0:T(8,128)(2,1)}, bf16[320,256]{1,0:T(8,128)(2,1)S(1)}, u32[]{:S(2)}, u32[]{:S(2)}) collective-permute-start(bf16[320,256]{1,0:T(8,128)(2,1)} %get-tuple-element.29), channel_id=1, source_target_pairs={{0,3},{1,0},{2,1},{3,2},{4,7},{5,4},{6,5},{7,6},{8,11},{9,8},{10,9... | collective-permute-start | bytes 491528 | tf_op jit(solution)/shard_map/ppermute | solution.py:447
  106.3 1.0 add_convert_fusion.1
  107.4 2.6 %store.1.refs_1_ = bf16[8,128,256]{2,1,0:T(8,128)(2,1)} custom-call(s32[8]{0:T(128)} %select_reduce_fusion.refs_6_.pick_ref, s32[8]{0:T(128)} %convert_element_type.55.refs_7_.have_ref, bf16[64,128,256]{2,1,0:T(8,128)(2,1)} %all-gather.5.cloned.1.call-done.fresh_ref, bf16[8,128,256]{2,1,0:T(8,128)(2,1)} %pool_ref.1), custom_call_target="tpu_custom_call" | custom-call | tf_op jit(solution)/shard_map/store/pallas_call | solution.py:412
  110.1 1.4 %collective-permute-done.16 = bf16[320,256]{1,0:T(8,128)(2,1)S(1)} collective-permute-done((bf16[320,256]{1,0:T(8,128)(2,1)}, bf16[320,256]{1,0:T(8,128)(2,1)S(1)}, u32[]{:S(2)}, u32[]{:S(2)}) %collective-permute-start.16) | collective-permute-done | bytes 163872 | tf_op jit(solution)/shard_map/ppermute | solution.py:447
  (80 shorter events, 13.1 us)
Async XLA Ops:
  7.2 20.0 %copy-start = (bf16[5120,256]{1,0:T(8,128)(2,1)S(1)}, bf16[5120,256]{1,0:T(8,128)(2,1)}, u32[]{:S(2)}) copy-start(bf16[5120,256]{1,0:T(8,128)(2,1)} %param.15) | copy-start | bytes 7864324
  7.2 14.8 %copy-start.10 = (f32[5120]{0:T(1024)S(1)}, f32[5120]{0:T(1024)}, u32[]{:S(2)}) copy-start(f32[5120]{0:T(1024)} %param.14) | copy-start | bytes 61444
  7.2 48.0 %all-gather.3.cloned.1.call-start = ((), (), s32[]{:S(2)}) async-start(), calls=%async_computation | async-start | bytes 4456448 | tf_op jit(solution)/shard_map/all_gather | solution.py:477
  9.1 98.2 %all-gather.5.cloned.1.call-start = ((), (), s32[]{:S(2)}) async-start(), calls=%async_computation.1 | async-start | bytes 4456448 | tf_op jit(solution)/shard_map/all_gather | solution.py:512
  13.9 23.9 %collective-permute-start = (bf16[6,320,256]{2,1,0:T(8,128)(2,1)}, bf16[6,320,256]{2,1,0:T(8,128)(2,1)}, u32[]{:S(2)}, u32[]{:S(2)}) collective-permute-start(bf16[6,320,256]{2,1,0:T(8,128)(2,1)} %get-tuple-element.17), channel_id=1, source_target_pairs={{0,4},{1,5},{2,6},{3,7},{4,8},{5,9},{6,10},{7,11},{8,12},{9,13},{1... | collective-permute-start | bytes 2949128 | tf_op jit(solution)/shard_map/ppermute | solution.py:481
  16.2 22.9 %collective-permute-start.1 = (bf16[6,320,256]{2,1,0:T(8,128)(2,1)}, bf16[6,320,256]{2,1,0:T(8,128)(2,1)}, u32[]{:S(2)}, u32[]{:S(2)}) collective-permute-start(bf16[6,320,256]{2,1,0:T(8,128)(2,1)} %get-tuple-element.18), channel_id=1, source_target_pairs={{0,12},{1,13},{2,14},{3,15},{4,0},{5,1},{6,2},{7,3},{8,4},{9,5},{1... | collective-permute-start | bytes 2949128 | tf_op jit(solution)/shard_map/ppermute | solution.py:482
  16.2 5.7 %copy-start.1 = (bf16[512,5120]{1,0:T(8,128)(2,1)S(1)}, bf16[512,5120]{1,0:T(8,128)(2,1)}, u32[]{:S(2)}) copy-start(bf16[512,5120]{1,0:T(8,128)(2,1)} %param.13) | copy-start | bytes 15728644
  22.0 3.6 %copy-start.8 = (f32[128]{0:T(128)S(1)}, f32[128]{0:T(128)}, u32[]{:S(2)}) copy-start(f32[128]{0:T(128)} %param.18) | copy-start | bytes 1540
  25.4 1.6 %copy-start.4 = (f32[512,256]{1,0:T(8,128)}, f32[512,256]{1,0:T(8,128)S(1)}, u32[]{:S(2)}) copy-start(f32[512,256]{1,0:T(8,128)S(1)} %fusion.3) | copy-start | bytes 1572868
  27.2 4.5 %copy-start.9 = (f32[128]{0:T(128)S(1)}, f32[128]{0:T(128)}, u32[]{:S(2)}) copy-start(f32[128]{0:T(128)} %param.17) | copy-start | bytes 1540
  27.2 5.5 %copy-start.6 = (s32[16,4]{0,1:T(4,128)S(1)}, s32[16,4]{0,1:T(4,128)}, u32[]{:S(2)}) copy-start(s32[16,4]{0,1:T(4,128)} %param.25) | copy-start | bytes 772
  27.2 5.7 %copy-start.7 = (s32[16,4]{0,1:T(4,128)S(1)}, s32[16,4]{0,1:T(4,128)}, u32[]{:S(2)}) copy-start(s32[16,4]{0,1:T(4,128)} %param.24) | copy-start | bytes 772
  39.1 10.3 %collective-permute-start.2 = (bf16[512,256]{1,0:T(8,128)(2,1)}, bf16[512,256]{1,0:T(8,128)(2,1)S(1)}, u32[]{:S(2)}, u32[]{:S(2)}) collective-permute-start(bf16[512,256]{1,0:T(8,128)(2,1)} %after.5.refs_2_.q_ref), channel_id=1, source_target_pairs={{0,1},{1,0},{2,3},{3,2},{4,5},{5,4},{6,7},{7,6},{8,9},{9,8},{10,11... | collective-permute-start | bytes 786440 | tf_op jit(solution)/shard_map/ppermute | solution.py:508
  41.8 8.1 %collective-permute-start.3 = (bf16[2,320,256]{2,1,0:T(8,128)(2,1)S(1)}, bf16[2,320,256]{2,1,0:T(8,128)(2,1)S(1)}, u32[]{:S(2)}, u32[]{:S(2)}) collective-permute-start(bf16[2,320,256]{2,1,0:T(8,128)(2,1)S(1)} %slice.39), channel_id=1, source_target_pairs={{0,4},{1,5},{2,6},{3,7},{4,8},{5,9},{6,10},{7,11},{8,12},{9,13},{1... | collective-permute-start | bytes 983048 | tf_op jit(solution)/shard_map/ppermute | solution.py:506
  43.2 9.5 %collective-permute-start.4 = (bf16[2,320,256]{2,1,0:T(8,128)(2,1)S(1)}, bf16[2,320,256]{2,1,0:T(8,128)(2,1)S(1)}, u32[]{:S(2)}, u32[]{:S(2)}) collective-permute-start(bf16[2,320,256]{2,1,0:T(8,128)(2,1)S(1)} %slice.40), channel_id=1, source_target_pairs={{0,12},{1,13},{2,14},{3,15},{4,0},{5,1},{6,2},{7,3},{8,4},{9,5},{1... | collective-permute-start | bytes 983048 | tf_op jit(solution)/shard_map/ppermute | solution.py:507
  49.4 0.7 copy-start.5
  50.1 5.0 %copy-start.2 = (bf16[2,320,256]{2,1,0:T(8,128)(2,1)}, bf16[2,320,256]{2,1,0:T(8,128)(2,1)S(1)}, u32[]{:S(2)}) copy-start(bf16[2,320,256]{2,1,0:T(8,128)(2,1)S(1)} %collective-permute-done.3.refs_8_.refs_7_) | copy-start | bytes 983044
  52.7 2.5 %copy-start.3 = (bf16[2,320,256]{2,1,0:T(8,128)(2,1)}, bf16[2,320,256]{2,1,0:T(8,128)(2,1)S(1)}, u32[]{:S(2)}) copy-start(bf16[2,320,256]{2,1,0:T(8,128)(2,1)S(1)} %collective-permute-done.4.refs_9_.refs_8_) | copy-start | bytes 983044
  63.5 10.1 %collective-permute-start.5 = (bf16[544,256]{1,0:T(8,128)(2,1)}, bf16[544,256]{1,0:T(8,128)(2,1)S(1)}, u32[]{:S(2)}, u32[]{:S(2)}) collective-permute-start(bf16[544,256]{1,0:T(8,128)(2,1)} %other.1.later_ref), channel_id=1, source_target_pairs={{0,1},{1,0},{2,3},{3,2},{4,5},{5,4},{6,7},{7,6},{8,9},{9,8},{10,11... | collective-permute-start | bytes 835592 | tf_op jit(solution)/shard_map/ppermute | solution.py:234
  75.9 6.6 %collective-permute-start.6 = (bf16[256,256]{1,0:T(8,128)(2,1)}, bf16[256,256]{1,0:T(8,128)(2,1)S(1)}, u32[]{:S(2)}, u32[]{:S(2)}) collective-permute-start(bf16[256,256]{1,0:T(8,128)(2,1)} %get-tuple-element.21.refs_0_), channel_id=1, source_target_pairs={{0,4},{1,5},{2,6},{3,7},{4,8},{5,9},{6,10},{7,11},{8,12},{9,13},{1... | collective-permute-start | bytes 393224 | tf_op jit(solution)/shard_map/ppermute | solution.py:436
  75.9 8.3 %collective-permute-start.7 = (bf16[256,256]{1,0:T(8,128)(2,1)}, bf16[256,256]{1,0:T(8,128)(2,1)S(1)}, u32[]{:S(2)}, u32[]{:S(2)}) collective-permute-start(bf16[256,256]{1,0:T(8,128)(2,1)} %get-tuple-element.21.refs_0_), channel_id=1, source_target_pairs={{0,8},{1,9},{2,10},{3,11},{4,12},{5,13},{6,14},{7,15},{8,0},{9,1},... | collective-permute-start | bytes 393224 | tf_op jit(solution)/shard_map/ppermute | solution.py:436
  78.8 9.6 %collective-permute-start.8 = (bf16[256,256]{1,0:T(8,128)(2,1)}, bf16[256,256]{1,0:T(8,128)(2,1)S(1)}, u32[]{:S(2)}, u32[]{:S(2)}) collective-permute-start(bf16[256,256]{1,0:T(8,128)(2,1)} %get-tuple-element.21.refs_0_), channel_id=1, source_target_pairs={{0,12},{1,13},{2,14},{3,15},{4,0},{5,1},{6,2},{7,3},{8,4},{9,5},{1... | collective-permute-start | bytes 393224 | tf_op jit(solution)/shard_map/ppermute | solution.py:436
  78.8 17.2 %collective-permute-start.12 = (bf16[256,256]{1,0:T(8,128)(2,1)}, bf16[256,256]{1,0:T(8,128)(2,1)S(1)}, u32[]{:S(2)}, u32[]{:S(2)}) collective-permute-start(bf16[256,256]{1,0:T(8,128)(2,1)} %get-tuple-element.27.refs_0_), channel_id=1, source_target_pairs={{0,4},{1,5},{2,6},{3,7},{4,8},{5,9},{6,10},{7,11},{8,12},{9,13},{1... | collective-permute-start | bytes 393224 | tf_op jit(solution)/shard_map/ppermute | solution.py:436
  82.0 17.2 %collective-permute-start.13 = (bf16[256,256]{1,0:T(8,128)(2,1)}, bf16[256,256]{1,0:T(8,128)(2,1)S(1)}, u32[]{:S(2)}, u32[]{:S(2)}) collective-permute-start(bf16[256,256]{1,0:T(8,128)(2,1)} %get-tuple-element.27.refs_0_), channel_id=1, source_target_pairs={{0,8},{1,9},{2,10},{3,11},{4,12},{5,13},{6,14},{7,15},{8,0},{9,1},... | collective-permute-start | bytes 393224 | tf_op jit(solution)/shard_map/ppermute | solution.py:436
  82.5 16.8 %collective-permute-start.14 = (bf16[256,256]{1,0:T(8,128)(2,1)}, bf16[256,256]{1,0:T(8,128)(2,1)S(1)}, u32[]{:S(2)}, u32[]{:S(2)}) collective-permute-start(bf16[256,256]{1,0:T(8,128)(2,1)} %get-tuple-element.27.refs_0_), channel_id=1, source_target_pairs={{0,12},{1,13},{2,14},{3,15},{4,0},{5,1},{6,2},{7,3},{8,4},{9,5},{1... | collective-permute-start | bytes 393224 | tf_op jit(solution)/shard_map/ppermute | solution.py:436
  92.0 11.8 %collective-permute-start.11 = (bf16[320,256]{1,0:T(8,128)(2,1)}, bf16[320,256]{1,0:T(8,128)(2,1)S(1)}, u32[]{:S(2)}, u32[]{:S(2)}) collective-permute-start(bf16[320,256]{1,0:T(8,128)(2,1)} %get-tuple-element.26), channel_id=1, source_target_pairs={{0,2},{1,3},{2,0},{3,1},{4,6},{5,7},{6,4},{7,5},{8,10},{9,11},{10,... | collective-permute-start | bytes 491528 | tf_op jit(solution)/shard_map/ppermute | solution.py:447
  96.0 10.3 %collective-permute-start.10 = (bf16[320,256]{1,0:T(8,128)(2,1)}, bf16[320,256]{1,0:T(8,128)(2,1)S(1)}, u32[]{:S(2)}, u32[]{:S(2)}) collective-permute-start(bf16[320,256]{1,0:T(8,128)(2,1)} %get-tuple-element.25), channel_id=1, source_target_pairs={{0,1},{1,2},{2,3},{3,0},{4,5},{5,6},{6,7},{7,4},{8,9},{9,10},{10,1... | collective-permute-start | bytes 491528 | tf_op jit(solution)/shard_map/ppermute | solution.py:447
  96.0 10.3 %collective-permute-start.9 = (bf16[320,256]{1,0:T(8,128)(2,1)}, bf16[320,256]{1,0:T(8,128)(2,1)S(1)}, u32[]{:S(2)}, u32[]{:S(2)}) collective-permute-start(bf16[320,256]{1,0:T(8,128)(2,1)} %get-tuple-element.24), channel_id=1, source_target_pairs={{0,3},{1,0},{2,1},{3,2},{4,7},{5,4},{6,5},{7,6},{8,11},{9,8},{10,9... | collective-permute-start | bytes 491528 | tf_op jit(solution)/shard_map/ppermute | solution.py:447
  102.9 7.2 %collective-permute-start.17 = (bf16[320,256]{1,0:T(8,128)(2,1)}, bf16[320,256]{1,0:T(8,128)(2,1)S(1)}, u32[]{:S(2)}, u32[]{:S(2)}) collective-permute-start(bf16[320,256]{1,0:T(8,128)(2,1)} %get-tuple-element.31), channel_id=1, source_target_pairs={{0,2},{1,3},{2,0},{3,1},{4,6},{5,7},{6,4},{7,5},{8,10},{9,11},{10,... | collective-permute-start | bytes 491528 | tf_op jit(solution)/shard_map/ppermute | solution.py:447
  103.0 8.6 %collective-permute-start.16 = (bf16[320,256]{1,0:T(8,128)(2,1)}, bf16[320,256]{1,0:T(8,128)(2,1)S(1)}, u32[]{:S(2)}, u32[]{:S(2)}) collective-permute-start(bf16[320,256]{1,0:T(8,128)(2,1)} %get-tuple-element.30), channel_id=1, source_target_pairs={{0,1},{1,2},{2,3},{3,0},{4,5},{5,6},{6,7},{7,4},{8,9},{9,10},{10,1... | collective-permute-start | bytes 491528 | tf_op jit(solution)/shard_map/ppermute | solution.py:447
  103.8 7.7 %collective-permute-start.15 = (bf16[320,256]{1,0:T(8,128)(2,1)}, bf16[320,256]{1,0:T(8,128)(2,1)S(1)}, u32[]{:S(2)}, u32[]{:S(2)}) collective-permute-start(bf16[320,256]{1,0:T(8,128)(2,1)} %get-tuple-element.29), channel_id=1, source_target_pairs={{0,3},{1,0},{2,1},{3,2},{4,7},{5,4},{6,5},{7,6},{8,11},{9,8},{10,9... | collective-permute-start | bytes 491528 | tf_op jit(solution)/shard_map/ppermute | solution.py:447
Sparse Core Ops, SparseCore 0:
  9.9 45.2 all-gather.2
  57.0 41.2 all-gather.4

commit v5 on v4

--- a/solution.py
+++ b/solution.py
@@ -235,8 +235,8 @@
     own, sums = pl.pallas_call(
         functools.partial(own_kernel, chunk=512),
         out_shape=[
-            jax.ShapeDtypeStruct((span, width), jnp.float32),
-            jax.ShapeDtypeStruct((8, span), jnp.float32),
+            pltpu.VMEM((span, width), jnp.float32),
+            pltpu.VMEM((8, span), jnp.float32),
         ],
         in_specs=[smem, smem, vmem, vmem, anywhere, anywhere],
         out_specs=[vmem, vmem],
@@ -252,7 +252,7 @@
         out_specs=[vmem] * 2,
         compiler_params=params,
         name="merge",
-    )(own, sums, arrived)
+    )(in_vmem(own), in_vmem(sums), arrived)
 
 
 def after_kernel(*refs):

time: 121 us -> 119 us (0.983)
  Pallas kernels: 33.1 us -> 31.2 us
  transfers between devices with their start and end apart: 20 -> 20, of which waited for: 9 -> 9; matrix products, arithmetic and copies ran while one was open for 22% -> 22% of each run, Pallas kernels for 28% -> 27%
where the time goes in v5:
time: 119 us; the launch traced here: 118 us
  Pallas kernels  31.2 us (26%)
  starting transfers between devices  26.1 us (22%)
  waiting for transfers between devices  15.7 us (13%)
  other arithmetic  14.4 us (12%)
  between operations  14.4 us (12%)
  local copies, waits for them, and re-layouts  8.18 us (7%)
  matrix products  7.77 us (7%)
    ppermute x6, starting transfers between devices, settle(): lax.ppermute(subtotals[k - 1], 'tensor', along(k)).astype(jnp.float32)  10 us
    pallas_call x1, Pallas kernels, attend(): pl.pallas_call(functools.partial(other_kernel, chunk=512), out_shape=jax....  8.26 us
    pallas_call x1, Pallas kernels, attend(): pl.pallas_call(functools.partial(own_kernel, chunk=512), out_shape=[pltpu...  7.78 us
    ppermute x6, starting transfers between devices, spread(): lax.ppermute(value, 'tensor', along_x(k))  7.75 us
    pallas_call x2, Pallas kernels, project(): pl.pallas_call(project_kernel, out_shape=[sent] * (SIDE - 1) + [jax.Shape...  7.29 us
    ppermute x6, waiting for transfers between devices, spread(): lax.ppermute(value, 'tensor', along_x(k))  4.86 us
    dot_general x1, matrix products, local(): jnp.dot(normed, w_query, preferred_element_type=jnp.float32)  4.4 us
    pallas_call x1, Pallas kernels, arrange(): pl.pallas_call(arrange_kernel, out_shape=[jax.ShapeDtypeStruct((n, column...  4.13 us
  transfers between devices with their start and end apart: 20, of which 9 were waited for; matrix products, arithmetic and copies ran while one was open for 22% of the time, Pallas kernels for 27%

profile of v5, /device:TPU:6, one launch (start us, length us, event | category | flops | bytes accessed | tf_op | source)
XLA Modules:
  0.0 117.8 jit_solution(11710938640633554154)
XLA Ops:
  7.3 1.8 %constant_dynamic-slice_fusion.refs_1_ = bf16[8,64,256]{2,1,0:T(8,128)(2,1)} fusion(bf16[8,128,256]{2,1,0:T(8,128)(2,1)} %pool_ref.1, s32[]{:T(128)S(6)} %select_n.31), kind=kLoop, calls=%fused_computation.32 | loop fusion | bytes 524292 | tf_op jit(solution)/shard_map/dynamic_slice | solution.py:476
  9.8 4.1 %arrange.1 = (bf16[4,320,256]{2,1,0:T(8,128)(2,1)}, bf16[6,320,256]{2,1,0:T(8,128)(2,1)}, bf16[6,320,256]{2,1,0:T(8,128)(2,1)}) custom-call(s32[2]{0:T(128)} %after.4.place_ref, bf16[256,5120]{1,0:T(8,128)(2,1)} %w_ref.1), custom_call_target="tpu_custom_call" | custom-call | tf_op jit(solution)/shard_map/arrange/pallas_call | solution.py:298
  13.9 2.3 %collective-permute-start = (bf16[6,320,256]{2,1,0:T(8,128)(2,1)}, bf16[6,320,256]{2,1,0:T(8,128)(2,1)}, u32[]{:S(2)}, u32[]{:S(2)}) collective-permute-start(bf16[6,320,256]{2,1,0:T(8,128)(2,1)} %get-tuple-element.17), channel_id=1, source_target_pairs={{0,4},{1,5},{2,6},{3,7},{4,8},{5,9},{6,10},{7,11},{8,12},{9,13},{1... | collective-permute-start | bytes 2949128 | tf_op jit(solution)/shard_map/ppermute | solution.py:481
  16.2 1.5 %dynamic_slice.14 = s32[1]{0:T(128)} dynamic-slice(s32[16]{0:T(128)} %param.21, s32[]{:T(128)S(6)} %select_n.27), dynamic_slice_sizes={1} | dynamic-slice | bytes 12 | tf_op jit(solution)/shard_map/dynamic_slice | solution.py:486
  18.5 3.6 %fusion = f32[512]{0:T(512)S(1)} fusion(bf16[512,5120]{1,0:T(8,128)(2,1)} %param.13), kind=kLoop, calls=%fused_computation.2 | loop fusion | flops 7863808 | bytes 5244928 | tf_op jit(solution)/shard_map/reduce_sum | solution.py:19
  22.1 3.4 %fusion.3 = f32[512,256]{1,0:T(8,128)S(1)} fusion(bf16[5120,256]{1,0:T(8,128)(2,1)} %param.16, bf16[512,5120]{1,0:T(8,128)(2,1)S(1)} %copy-done.1, f32[5120]{0:T(1024)S(1)} %copy-done.10, f32[512]{0:T(512)S(1)} %add_rsqrt_fusion.2), kind=kOutput, calls=%fused_computation.5 | convolution fusion | flops 1352663040 | bytes 8411136 | tf_op jit(solution)/shard_map/dot_general | solution.py:490
  25.8 1.2 %subtract_convert_fusion = (bf16[512,64]{1,0:T(8,128)(2,1)S(1)}, bf16[512,64]{1,0:T(8,128)(2,1)S(1)}, f32[512,64]{1,0:T(8,128)S(1)}, f32[512,64]{1,0:T(8,128)S(1)}) fusion(f32[512,128]{1,0:T(8,128)S(1)} %multiply_multiply_fusion.1, f32[512]{0:T(512)S(1)} %add_convert_fusion.4, f32[64]{0:T(128)S(1)} %multiply_power_fusion), kind=kLoop, calls=%fused_computation.18 | loop fusion | flops 294912 | bytes 657664 | tf_op jit(solution)/shard_map/convert.1
  27.3 4.4 %multiply_reduce_fusion = (f32[512,2]{0,1:T(2,128)S(1)}, f32[512,256]{0,1:T(8,128)S(1)}) fusion(bf16[5120,256]{1,0:T(8,128)(2,1)S(1)} %copy-done, bf16[512,5120]{1,0:T(8,128)(2,1)} %param.13, f32[5120]{0:T(1024)} %param.14, f32[512]{0:T(512)S(1)} %add_rsqrt_fusion.2), kind=kOutput, calls=%fused_computation.8 | convolution fusion | flops 1352924160 | bytes 8415232 | tf_op jit(solution)/shard_map/dot_general | solution.py:485
  33.2 1.3 %pad_add_fusion.refs_5_.info_ref = s32[2]{0:T(128)} fusion(s32[1]{0:T(128)} %bitcast.1, s32[1]{0:T(128)} %dynamic_slice.14), kind=kLoop, calls=%fused_computation.37 | loop fusion | flops 2 | bytes 16 | tf_op jit(solution)/shard_map/stack | solution.py:504
  34.7 3.2 %collective-permute-done.refs_1_.refs_5_ = bf16[6,320,256]{2,1,0:T(8,128)(2,1)} collective-permute-done((bf16[6,320,256]{2,1,0:T(8,128)(2,1)}, bf16[6,320,256]{2,1,0:T(8,128)(2,1)}, u32[]{:S(2)}, u32[]{:S(2)}) %collective-permute-start) | collective-permute-done | bytes 983072 | tf_op jit(solution)/shard_map/ppermute | solution.py:481
  37.8 1.3 %collective-permute-done.1.refs_2_.refs_6_ = bf16[6,320,256]{2,1,0:T(8,128)(2,1)} collective-permute-done((bf16[6,320,256]{2,1,0:T(8,128)(2,1)}, bf16[6,320,256]{2,1,0:T(8,128)(2,1)}, u32[]{:S(2)}, u32[]{:S(2)}) %collective-permute-start.1) | collective-permute-done | bytes 983072 | tf_op jit(solution)/shard_map/ppermute | solution.py:482
  39.1 1.7 %collective-permute-start.2 = (bf16[512,256]{1,0:T(8,128)(2,1)}, bf16[512,256]{1,0:T(8,128)(2,1)S(1)}, u32[]{:S(2)}, u32[]{:S(2)}) collective-permute-start(bf16[512,256]{1,0:T(8,128)(2,1)} %after.5.refs_2_.q_ref), channel_id=1, source_target_pairs={{0,1},{1,0},{2,3},{3,2},{4,5},{5,4},{6,7},{7,6},{8,9},{9,8},{10,11... | collective-permute-start | bytes 786440 | tf_op jit(solution)/shard_map/ppermute | solution.py:508
  43.2 2.0 %collective-permute-start.4 = (bf16[2,320,256]{2,1,0:T(8,128)(2,1)S(1)}, bf16[2,320,256]{2,1,0:T(8,128)(2,1)S(1)}, u32[]{:S(2)}, u32[]{:S(2)}) collective-permute-start(bf16[2,320,256]{2,1,0:T(8,128)(2,1)S(1)} %slice.40), channel_id=1, source_target_pairs={{0,12},{1,13},{2,14},{3,15},{4,0},{5,1},{6,2},{7,3},{8,4},{9,5},{1... | collective-permute-start | bytes 983048 | tf_op jit(solution)/shard_map/ppermute | solution.py:507
  45.2 1.3 %fusion.11.refs_4_.rows_ref = s32[48]{0:T(128)} fusion(s32[16,48]{1,0:T(8,128)} %param.23, s32[]{:T(128)S(6)} %select_n.27, s32[16,48]{1,0:T(8,128)} %param.22), kind=kLoop, calls=%fused_computation.40 | loop fusion | flops 96 | bytes 580 | tf_op jit(solution)/shard_map/add | solution.py:495
  50.3 2.4 %collective-permute-done.4.refs_9_.refs_8_ = bf16[2,320,256]{2,1,0:T(8,128)(2,1)S(1)} collective-permute-done((bf16[2,320,256]{2,1,0:T(8,128)(2,1)S(1)}, bf16[2,320,256]{2,1,0:T(8,128)(2,1)S(1)}, u32[]{:S(2)}, u32[]{:S(2)}) %collective-permute-start.4) | collective-permute-done | bytes 327712 | tf_op jit(solution)/shard_map/ppermute | solution.py:507
  52.7 2.2 %all-gather.3.cloned.1.call-done.refs_1_.pool_ref = bf16[128,64,256]{2,1,0:T(8,128)(2,1)} async-done(((bf16[8,64,256]{2,1,0:T(8,128)(2,1)}), bf16[128,64,256]{2,1,0:T(8,128)(2,1)}) %all-gather.3.cloned.1.call-update) | async-done | bytes 4194320 | tf_op jit(solution)/shard_map/all_gather | solution.py:477
  54.8 8.3 %other.1.later_ref = bf16[544,256]{1,0:T(8,128)(2,1)} custom-call(s32[48]{0:T(128)} %fusion.11.refs_4_.rows_ref, s32[2]{0:T(128)} %pad_add_fusion.refs_5_.info_ref, bf16[512,256]{1,0:T(8,128)(2,1)} %copy-done.5, bf16[128,64,256]{2,1,0:T(8,128)(2,1)} %all-gather.3.cloned.1.call-done.refs_1_.pool_ref), custom_call_target="tpu_custom_call" | custom-call | flops 1610612736 | bytes 1572864 | tf_op jit(solution)/shard_map/other/pallas_call | solution.py:224
  63.1 1.9 %collective-permute-start.5 = (bf16[544,256]{1,0:T(8,128)(2,1)}, bf16[544,256]{1,0:T(8,128)(2,1)S(1)}, u32[]{:S(2)}, u32[]{:S(2)}) collective-permute-start(bf16[544,256]{1,0:T(8,128)(2,1)} %other.1.later_ref), channel_id=1, source_target_pairs={{0,1},{1,0},{2,3},{3,2},{4,5},{5,4},{6,7},{7,6},{8,9},{9,8},{10,11... | collective-permute-start | bytes 835592 | tf_op jit(solution)/shard_map/ppermute | solution.py:234
  65.0 7.8 %own.1 = (f32[512,256]{1,0:T(8,128)S(1)}, f32[8,512]{1,0:T(8,128)S(1)}) custom-call(s32[48]{0:T(128)} %fusion.11.refs_4_.rows_ref, s32[2]{0:T(128)} %pad_add_fusion.refs_5_.info_ref, bf16[512,256]{1,0:T(8,128)(2,1)} %after.5.refs_2_.q_ref, bf16[512,256]{1,0:T(8,128)(2,1)} %after.6.fresh_ref, ...), custom_call_target="tpu_custom_call" | custom-call | flops 1879048192 | bytes 1835008 | tf_op jit(solution)/shard_map/own/pallas_call | solution.py:235
  72.8 1.2 %merge.1 = (bf16[256,256]{1,0:T(8,128)(2,1)}, bf16[256,256]{1,0:T(8,128)(2,1)}) custom-call(f32[512,256]{1,0:T(8,128)S(1)} %get-tuple-element.19.own_ref, f32[8,512]{1,0:T(8,128)S(1)} %get-tuple-element.20.sum_ref, bf16[544,256]{1,0:T(8,128)(2,1)S(1)} %collective-permute-done.5.other_ref), custom_call_target="tpu_custom_call" | custom-call | tf_op jit(solution)/shard_map/merge/pallas_call | solution.py:248
  74.1 2.7 %collective-permute-start.7 = (bf16[256,256]{1,0:T(8,128)(2,1)}, bf16[256,256]{1,0:T(8,128)(2,1)S(1)}, u32[]{:S(2)}, u32[]{:S(2)}) collective-permute-start(bf16[256,256]{1,0:T(8,128)(2,1)} %get-tuple-element.21.refs_0_), channel_id=1, source_target_pairs={{0,8},{1,9},{2,10},{3,11},{4,12},{5,13},{6,14},{7,15},{8,0},{9,1},... | collective-permute-start | bytes 393224 | tf_op jit(solution)/shard_map/ppermute | solution.py:436
  76.8 3.2 %collective-permute-start.12 = (bf16[256,256]{1,0:T(8,128)(2,1)}, bf16[256,256]{1,0:T(8,128)(2,1)S(1)}, u32[]{:S(2)}, u32[]{:S(2)}) collective-permute-start(bf16[256,256]{1,0:T(8,128)(2,1)} %get-tuple-element.27.refs_0_), channel_id=1, source_target_pairs={{0,4},{1,5},{2,6},{3,7},{4,8},{5,9},{6,10},{7,11},{8,12},{9,13},{1... | collective-permute-start | bytes 393224 | tf_op jit(solution)/shard_map/ppermute | solution.py:436
  80.6 1.6 %collective-permute-start.14 = (bf16[256,256]{1,0:T(8,128)(2,1)}, bf16[256,256]{1,0:T(8,128)(2,1)S(1)}, u32[]{:S(2)}, u32[]{:S(2)}) collective-permute-start(bf16[256,256]{1,0:T(8,128)(2,1)} %get-tuple-element.27.refs_0_), channel_id=1, source_target_pairs={{0,12},{1,13},{2,14},{3,15},{4,0},{5,1},{6,2},{7,3},{8,4},{9,5},{1... | collective-permute-start | bytes 393224 | tf_op jit(solution)/shard_map/ppermute | solution.py:436
  82.2 4.4 %collective-permute-done.8.refs_3_ = bf16[256,256]{1,0:T(8,128)(2,1)S(1)} collective-permute-done((bf16[256,256]{1,0:T(8,128)(2,1)}, bf16[256,256]{1,0:T(8,128)(2,1)S(1)}, u32[]{:S(2)}, u32[]{:S(2)}) %collective-permute-start.8) | collective-permute-done | bytes 131104 | tf_op jit(solution)/shard_map/ppermute | solution.py:436
  86.6 3.6 %project.2 = (bf16[320,256]{1,0:T(8,128)(2,1)}, bf16[320,256]{1,0:T(8,128)(2,1)}, bf16[320,256]{1,0:T(8,128)(2,1)}, f32[320,256]{1,0:T(8,128)}) custom-call(bf16[256,256]{1,0:T(8,128)(2,1)} %get-tuple-element.21.refs_0_, bf16[256,256]{1,0:T(8,128)(2,1)S(1)} %collective-permute-done.6.refs_1_, bf16[256,256]{1,0:T(8,128)(2,1)S(1)} %collective-permute-done.7.refs_2_, ...), custom_call_target="tpu_custom_call" | custom-call | flops 671088640 | bytes 2621440 | tf_op jit(solution)/shard_map/project/pallas_call | solution.py:365
  90.3 3.4 %collective-permute-start.11 = (bf16[320,256]{1,0:T(8,128)(2,1)}, bf16[320,256]{1,0:T(8,128)(2,1)S(1)}, u32[]{:S(2)}, u32[]{:S(2)}) collective-permute-start(bf16[320,256]{1,0:T(8,128)(2,1)} %get-tuple-element.26), channel_id=1, source_target_pairs={{0,2},{1,3},{2,0},{3,1},{4,6},{5,7},{6,4},{7,5},{8,10},{9,11},{10,... | collective-permute-start | bytes 491528 | tf_op jit(solution)/shard_map/ppermute | solution.py:447
  94.5 2.4 %collective-permute-start.9 = (bf16[320,256]{1,0:T(8,128)(2,1)}, bf16[320,256]{1,0:T(8,128)(2,1)S(1)}, u32[]{:S(2)}, u32[]{:S(2)}) collective-permute-start(bf16[320,256]{1,0:T(8,128)(2,1)} %get-tuple-element.24), channel_id=1, source_target_pairs={{0,3},{1,0},{2,1},{3,2},{4,7},{5,4},{6,5},{7,6},{8,11},{9,8},{10,9... | collective-permute-start | bytes 491528 | tf_op jit(solution)/shard_map/ppermute | solution.py:447
  96.9 3.6 %project.3 = (bf16[320,256]{1,0:T(8,128)(2,1)}, bf16[320,256]{1,0:T(8,128)(2,1)}, bf16[320,256]{1,0:T(8,128)(2,1)}, f32[320,256]{1,0:T(8,128)}) custom-call(bf16[256,256]{1,0:T(8,128)(2,1)} %get-tuple-element.27.refs_0_, bf16[256,256]{1,0:T(8,128)(2,1)S(1)} %collective-permute-done.12.refs_1_, bf16[256,256]{1,0:T(8,128)(2,1)S(1)} %collective-permute-done.13.refs_2_, ...), custom_call_target="tpu_custom_call" | custom-call | flops 671088640 | bytes 2621440 | tf_op jit(solution)/shard_map/project/pallas_call | solution.py:365
  101.5 2.4 %collective-permute-start.15 = (bf16[320,256]{1,0:T(8,128)(2,1)}, bf16[320,256]{1,0:T(8,128)(2,1)S(1)}, u32[]{:S(2)}, u32[]{:S(2)}) collective-permute-start(bf16[320,256]{1,0:T(8,128)(2,1)} %get-tuple-element.29), channel_id=1, source_target_pairs={{0,3},{1,0},{2,1},{3,2},{4,7},{5,4},{6,5},{7,6},{8,11},{9,8},{10,9... | collective-permute-start | bytes 491528 | tf_op jit(solution)/shard_map/ppermute | solution.py:447
  104.0 1.0 add_convert_fusion.1
  105.0 2.6 %store.1.refs_1_ = bf16[8,128,256]{2,1,0:T(8,128)(2,1)} custom-call(s32[8]{0:T(128)} %select_reduce_fusion.refs_6_.pick_ref, s32[8]{0:T(128)} %convert_element_type.55.refs_7_.have_ref, bf16[64,128,256]{2,1,0:T(8,128)(2,1)} %all-gather.5.cloned.1.call-done.fresh_ref, bf16[8,128,256]{2,1,0:T(8,128)(2,1)} %pool_ref.1), custom_call_target="tpu_custom_call" | custom-call | tf_op jit(solution)/shard_map/store/pallas_call | solution.py:412
  107.8 1.4 %collective-permute-done.16 = bf16[320,256]{1,0:T(8,128)(2,1)S(1)} collective-permute-done((bf16[320,256]{1,0:T(8,128)(2,1)}, bf16[320,256]{1,0:T(8,128)(2,1)S(1)}, u32[]{:S(2)}, u32[]{:S(2)}) %collective-permute-start.16) | collective-permute-done | bytes 163872 | tf_op jit(solution)/shard_map/ppermute | solution.py:447
  (80 shorter events, 14.3 us)
Async XLA Ops:
  7.2 20.1 %copy-start = (bf16[5120,256]{1,0:T(8,128)(2,1)S(1)}, bf16[5120,256]{1,0:T(8,128)(2,1)}, u32[]{:S(2)}) copy-start(bf16[5120,256]{1,0:T(8,128)(2,1)} %param.15) | copy-start | bytes 7864324
  7.2 14.9 %copy-start.10 = (f32[5120]{0:T(1024)S(1)}, f32[5120]{0:T(1024)}, u32[]{:S(2)}) copy-start(f32[5120]{0:T(1024)} %param.14) | copy-start | bytes 61444
  7.2 47.6 %all-gather.3.cloned.1.call-start = ((), (), s32[]{:S(2)}) async-start(), calls=%async_computation | async-start | bytes 4456448 | tf_op jit(solution)/shard_map/all_gather | solution.py:477
  9.1 95.9 %all-gather.5.cloned.1.call-start = ((), (), s32[]{:S(2)}) async-start(), calls=%async_computation.1 | async-start | bytes 4456448 | tf_op jit(solution)/shard_map/all_gather | solution.py:512
  13.9 23.9 %collective-permute-start = (bf16[6,320,256]{2,1,0:T(8,128)(2,1)}, bf16[6,320,256]{2,1,0:T(8,128)(2,1)}, u32[]{:S(2)}, u32[]{:S(2)}) collective-permute-start(bf16[6,320,256]{2,1,0:T(8,128)(2,1)} %get-tuple-element.17), channel_id=1, source_target_pairs={{0,4},{1,5},{2,6},{3,7},{4,8},{5,9},{6,10},{7,11},{8,12},{9,13},{1... | collective-permute-start | bytes 2949128 | tf_op jit(solution)/shard_map/ppermute | solution.py:481
  16.2 22.9 %collective-permute-start.1 = (bf16[6,320,256]{2,1,0:T(8,128)(2,1)}, bf16[6,320,256]{2,1,0:T(8,128)(2,1)}, u32[]{:S(2)}, u32[]{:S(2)}) collective-permute-start(bf16[6,320,256]{2,1,0:T(8,128)(2,1)} %get-tuple-element.18), channel_id=1, source_target_pairs={{0,12},{1,13},{2,14},{3,15},{4,0},{5,1},{6,2},{7,3},{8,4},{9,5},{1... | collective-permute-start | bytes 2949128 | tf_op jit(solution)/shard_map/ppermute | solution.py:482
  16.2 5.9 %copy-start.1 = (bf16[512,5120]{1,0:T(8,128)(2,1)S(1)}, bf16[512,5120]{1,0:T(8,128)(2,1)}, u32[]{:S(2)}) copy-start(bf16[512,5120]{1,0:T(8,128)(2,1)} %param.13) | copy-start | bytes 15728644
  22.1 3.6 %copy-start.8 = (f32[128]{0:T(128)S(1)}, f32[128]{0:T(128)}, u32[]{:S(2)}) copy-start(f32[128]{0:T(128)} %param.18) | copy-start | bytes 1540
  25.5 1.6 %copy-start.4 = (f32[512,256]{1,0:T(8,128)}, f32[512,256]{1,0:T(8,128)S(1)}, u32[]{:S(2)}) copy-start(f32[512,256]{1,0:T(8,128)S(1)} %fusion.3) | copy-start | bytes 1572868
  27.3 4.5 %copy-start.9 = (f32[128]{0:T(128)S(1)}, f32[128]{0:T(128)}, u32[]{:S(2)}) copy-start(f32[128]{0:T(128)} %param.17) | copy-start | bytes 1540
  27.3 5.5 %copy-start.6 = (s32[16,4]{0,1:T(4,128)S(1)}, s32[16,4]{0,1:T(4,128)}, u32[]{:S(2)}) copy-start(s32[16,4]{0,1:T(4,128)} %param.25) | copy-start | bytes 772
  27.3 5.7 %copy-start.7 = (s32[16,4]{0,1:T(4,128)S(1)}, s32[16,4]{0,1:T(4,128)}, u32[]{:S(2)}) copy-start(s32[16,4]{0,1:T(4,128)} %param.24) | copy-start | bytes 772
  39.1 10.5 %collective-permute-start.2 = (bf16[512,256]{1,0:T(8,128)(2,1)}, bf16[512,256]{1,0:T(8,128)(2,1)S(1)}, u32[]{:S(2)}, u32[]{:S(2)}) collective-permute-start(bf16[512,256]{1,0:T(8,128)(2,1)} %after.5.refs_2_.q_ref), channel_id=1, source_target_pairs={{0,1},{1,0},{2,3},{3,2},{4,5},{5,4},{6,7},{7,6},{8,9},{9,8},{10,11... | collective-permute-start | bytes 786440 | tf_op jit(solution)/shard_map/ppermute | solution.py:508
  41.8 8.1 %collective-permute-start.3 = (bf16[2,320,256]{2,1,0:T(8,128)(2,1)S(1)}, bf16[2,320,256]{2,1,0:T(8,128)(2,1)S(1)}, u32[]{:S(2)}, u32[]{:S(2)}) collective-permute-start(bf16[2,320,256]{2,1,0:T(8,128)(2,1)S(1)} %slice.39), channel_id=1, source_target_pairs={{0,4},{1,5},{2,6},{3,7},{4,8},{5,9},{6,10},{7,11},{8,12},{9,13},{1... | collective-permute-start | bytes 983048 | tf_op jit(solution)/shard_map/ppermute | solution.py:506
  43.2 9.5 %collective-permute-start.4 = (bf16[2,320,256]{2,1,0:T(8,128)(2,1)S(1)}, bf16[2,320,256]{2,1,0:T(8,128)(2,1)S(1)}, u32[]{:S(2)}, u32[]{:S(2)}) collective-permute-start(bf16[2,320,256]{2,1,0:T(8,128)(2,1)S(1)} %slice.40), channel_id=1, source_target_pairs={{0,12},{1,13},{2,14},{3,15},{4,0},{5,1},{6,2},{7,3},{8,4},{9,5},{1... | collective-permute-start | bytes 983048 | tf_op jit(solution)/shard_map/ppermute | solution.py:507
  49.6 0.7 copy-start.5
  50.3 4.5 %copy-start.2 = (bf16[2,320,256]{2,1,0:T(8,128)(2,1)}, bf16[2,320,256]{2,1,0:T(8,128)(2,1)S(1)}, u32[]{:S(2)}) copy-start(bf16[2,320,256]{2,1,0:T(8,128)(2,1)S(1)} %collective-permute-done.3.refs_8_.refs_7_) | copy-start | bytes 983044
  52.7 2.2 %copy-start.3 = (bf16[2,320,256]{2,1,0:T(8,128)(2,1)}, bf16[2,320,256]{2,1,0:T(8,128)(2,1)S(1)}, u32[]{:S(2)}) copy-start(bf16[2,320,256]{2,1,0:T(8,128)(2,1)S(1)} %collective-permute-done.4.refs_9_.refs_8_) | copy-start | bytes 983044
  63.1 9.7 %collective-permute-start.5 = (bf16[544,256]{1,0:T(8,128)(2,1)}, bf16[544,256]{1,0:T(8,128)(2,1)S(1)}, u32[]{:S(2)}, u32[]{:S(2)}) collective-permute-start(bf16[544,256]{1,0:T(8,128)(2,1)} %other.1.later_ref), channel_id=1, source_target_pairs={{0,1},{1,0},{2,3},{3,2},{4,5},{5,4},{6,7},{7,6},{8,9},{9,8},{10,11... | collective-permute-start | bytes 835592 | tf_op jit(solution)/shard_map/ppermute | solution.py:234
  74.0 6.6 %collective-permute-start.6 = (bf16[256,256]{1,0:T(8,128)(2,1)}, bf16[256,256]{1,0:T(8,128)(2,1)S(1)}, u32[]{:S(2)}, u32[]{:S(2)}) collective-permute-start(bf16[256,256]{1,0:T(8,128)(2,1)} %get-tuple-element.21.refs_0_), channel_id=1, source_target_pairs={{0,4},{1,5},{2,6},{3,7},{4,8},{5,9},{6,10},{7,11},{8,12},{9,13},{1... | collective-permute-start | bytes 393224 | tf_op jit(solution)/shard_map/ppermute | solution.py:436
  74.1 8.1 %collective-permute-start.7 = (bf16[256,256]{1,0:T(8,128)(2,1)}, bf16[256,256]{1,0:T(8,128)(2,1)S(1)}, u32[]{:S(2)}, u32[]{:S(2)}) collective-permute-start(bf16[256,256]{1,0:T(8,128)(2,1)} %get-tuple-element.21.refs_0_), channel_id=1, source_target_pairs={{0,8},{1,9},{2,10},{3,11},{4,12},{5,13},{6,14},{7,15},{8,0},{9,1},... | collective-permute-start | bytes 393224 | tf_op jit(solution)/shard_map/ppermute | solution.py:436
  76.8 9.8 %collective-permute-start.8 = (bf16[256,256]{1,0:T(8,128)(2,1)}, bf16[256,256]{1,0:T(8,128)(2,1)S(1)}, u32[]{:S(2)}, u32[]{:S(2)}) collective-permute-start(bf16[256,256]{1,0:T(8,128)(2,1)} %get-tuple-element.21.refs_0_), channel_id=1, source_target_pairs={{0,12},{1,13},{2,14},{3,15},{4,0},{5,1},{6,2},{7,3},{8,4},{9,5},{1... | collective-permute-start | bytes 393224 | tf_op jit(solution)/shard_map/ppermute | solution.py:436
  76.8 17.6 %collective-permute-start.12 = (bf16[256,256]{1,0:T(8,128)(2,1)}, bf16[256,256]{1,0:T(8,128)(2,1)S(1)}, u32[]{:S(2)}, u32[]{:S(2)}) collective-permute-start(bf16[256,256]{1,0:T(8,128)(2,1)} %get-tuple-element.27.refs_0_), channel_id=1, source_target_pairs={{0,4},{1,5},{2,6},{3,7},{4,8},{5,9},{6,10},{7,11},{8,12},{9,13},{1... | collective-permute-start | bytes 393224 | tf_op jit(solution)/shard_map/ppermute | solution.py:436
  80.1 16.8 %collective-permute-start.13 = (bf16[256,256]{1,0:T(8,128)(2,1)}, bf16[256,256]{1,0:T(8,128)(2,1)S(1)}, u32[]{:S(2)}, u32[]{:S(2)}) collective-permute-start(bf16[256,256]{1,0:T(8,128)(2,1)} %get-tuple-element.27.refs_0_), channel_id=1, source_target_pairs={{0,8},{1,9},{2,10},{3,11},{4,12},{5,13},{6,14},{7,15},{8,0},{9,1},... | collective-permute-start | bytes 393224 | tf_op jit(solution)/shard_map/ppermute | solution.py:436
  80.6 16.3 %collective-permute-start.14 = (bf16[256,256]{1,0:T(8,128)(2,1)}, bf16[256,256]{1,0:T(8,128)(2,1)S(1)}, u32[]{:S(2)}, u32[]{:S(2)}) collective-permute-start(bf16[256,256]{1,0:T(8,128)(2,1)} %get-tuple-element.27.refs_0_), channel_id=1, source_target_pairs={{0,12},{1,13},{2,14},{3,15},{4,0},{5,1},{6,2},{7,3},{8,4},{9,5},{1... | collective-permute-start | bytes 393224 | tf_op jit(solution)/shard_map/ppermute | solution.py:436
  90.3 11.2 %collective-permute-start.11 = (bf16[320,256]{1,0:T(8,128)(2,1)}, bf16[320,256]{1,0:T(8,128)(2,1)S(1)}, u32[]{:S(2)}, u32[]{:S(2)}) collective-permute-start(bf16[320,256]{1,0:T(8,128)(2,1)} %get-tuple-element.26), channel_id=1, source_target_pairs={{0,2},{1,3},{2,0},{3,1},{4,6},{5,7},{6,4},{7,5},{8,10},{9,11},{10,... | collective-permute-start | bytes 491528 | tf_op jit(solution)/shard_map/ppermute | solution.py:447
  93.6 10.3 %collective-permute-start.10 = (bf16[320,256]{1,0:T(8,128)(2,1)}, bf16[320,256]{1,0:T(8,128)(2,1)S(1)}, u32[]{:S(2)}, u32[]{:S(2)}) collective-permute-start(bf16[320,256]{1,0:T(8,128)(2,1)} %get-tuple-element.25), channel_id=1, source_target_pairs={{0,1},{1,2},{2,3},{3,0},{4,5},{5,6},{6,7},{7,4},{8,9},{9,10},{10,1... | collective-permute-start | bytes 491528 | tf_op jit(solution)/shard_map/ppermute | solution.py:447
  94.5 9.5 %collective-permute-start.9 = (bf16[320,256]{1,0:T(8,128)(2,1)}, bf16[320,256]{1,0:T(8,128)(2,1)S(1)}, u32[]{:S(2)}, u32[]{:S(2)}) collective-permute-start(bf16[320,256]{1,0:T(8,128)(2,1)} %get-tuple-element.24), channel_id=1, source_target_pairs={{0,3},{1,0},{2,1},{3,2},{4,7},{5,4},{6,5},{7,6},{8,11},{9,8},{10,9... | collective-permute-start | bytes 491528 | tf_op jit(solution)/shard_map/ppermute | solution.py:447
  100.5 7.2 %collective-permute-start.17 = (bf16[320,256]{1,0:T(8,128)(2,1)}, bf16[320,256]{1,0:T(8,128)(2,1)S(1)}, u32[]{:S(2)}, u32[]{:S(2)}) collective-permute-start(bf16[320,256]{1,0:T(8,128)(2,1)} %get-tuple-element.31), channel_id=1, source_target_pairs={{0,2},{1,3},{2,0},{3,1},{4,6},{5,7},{6,4},{7,5},{8,10},{9,11},{10,... | collective-permute-start | bytes 491528 | tf_op jit(solution)/shard_map/ppermute | solution.py:447
  100.6 8.6 %collective-permute-start.16 = (bf16[320,256]{1,0:T(8,128)(2,1)}, bf16[320,256]{1,0:T(8,128)(2,1)S(1)}, u32[]{:S(2)}, u32[]{:S(2)}) collective-permute-start(bf16[320,256]{1,0:T(8,128)(2,1)} %get-tuple-element.30), channel_id=1, source_target_pairs={{0,1},{1,2},{2,3},{3,0},{4,5},{5,6},{6,7},{7,4},{8,9},{9,10},{10,1... | collective-permute-start | bytes 491528 | tf_op jit(solution)/shard_map/ppermute | solution.py:447
  101.5 7.7 %collective-permute-start.15 = (bf16[320,256]{1,0:T(8,128)(2,1)}, bf16[320,256]{1,0:T(8,128)(2,1)S(1)}, u32[]{:S(2)}, u32[]{:S(2)}) collective-permute-start(bf16[320,256]{1,0:T(8,128)(2,1)} %get-tuple-element.29), channel_id=1, source_target_pairs={{0,3},{1,0},{2,1},{3,2},{4,7},{5,4},{6,5},{7,6},{8,11},{9,8},{10,9... | collective-permute-start | bytes 491528 | tf_op jit(solution)/shard_map/ppermute | solution.py:447
Sparse Core Ops, SparseCore 0:
  9.9 44.9 all-gather.2
  56.6 41.3 all-gather.4
